TPU v7x, 32 devices: a whole 2x2x4 slice. The times are simulated.
32 devices in a mesh: parts: 2 (over y), grp: 4 (over x, core), ep: 4 (over z).
Axes of the slice: x: 2, y: 2, z: 4, core: 2. Of those that a mesh axis runs over, the one named last changes fastest.
Arguments:
- tokens: bfloat16 [4096, 1024], P(('parts', 'grp', 'ep')), parts along dimension 0, may hold values from -6 to 6
- cotangent: bfloat16 [4096, 1024], P(('parts', 'grp', 'ep')), parts along dimension 0, may hold values from -6 to 6
- expert_ids: int32 [4096, 5], P(('parts', 'grp', 'ep')), parts along dimension 0, may hold values from 0 to 15, all different within a row; in each aligned block of 128 rows (0 to 127, 128 to 255, ...) at most 80 rows name the same one
- route_weights: float32 [4096, 5], P(('parts', 'grp', 'ep')), parts along dimension 0, may hold values from 0.1 to 1
- w_gate: bfloat16 [16, 1024, 512], P(('grp', 'ep')), may hold values from -0.1875 to 0.1875
- w_up: bfloat16 [16, 1024, 512], P(('grp', 'ep')), may hold values from -0.1875 to 0.1875
- w_down: bfloat16 [16, 512, 1024], P(('grp', 'ep')), may hold values from -0.25 to 0.25
Outputs:
- grad_tokens: bfloat16 [4096, 1024], P(('parts', 'grp', 'ep')), parts along dimension 0
- grad_weights: bfloat16 [4096, 5], P(('parts', 'grp', 'ep')), parts along dimension 0
There are 2 independent parts, one for each index of `parts`. A program takes and returns all parts, laid end to end along the dimension named above; an argument that names none is the same for every part. Nothing has to cross between parts.
Inputs may be any that keep to these rules, and one draw needn't show every extreme that they name: `expert_ids`: each row names 5 different experts. In each aligned block of 128 rows (the rows of one device) no expert is named by more than 80 rows, a bound that some block reaches.
All inputs are finite; a program needn't handle non-finite values.
Results may differ from a plain program's by a relative error of at most 0.0057.
Values may be sent and summed in bfloat16 or wider, within the bound.
No kernel may reach another device: no remote copies, remote signals or barrier semaphores. Data moves between devices by JAX's collectives and lax.ppermute only.
A program may use at most 64 MiB of HBM per device.

v0:
```python
import jax
import jax.numpy as jnp
from jax import lax
from jax.sharding import PartitionSpec as P


def expert_grads(rows_in, grads_in, w_gate, w_up, w_down):
    contract = (((1,), (1,)), ((), ()))
    gate_pre = jnp.dot(rows_in, w_gate, preferred_element_type=jnp.float32)
    up_pre = jnp.dot(rows_in, w_up, preferred_element_type=jnp.float32)
    hidden_grad = lax.dot_general(grads_in, w_down, contract, preferred_element_type=jnp.float32)
    sigmoid_gate = jax.nn.sigmoid(gate_pre)
    activation = gate_pre * sigmoid_gate
    hidden = activation * up_pre
    weight_grad = jnp.sum(hidden_grad * hidden, axis=-1).astype(jnp.bfloat16)
    grad_up = (hidden_grad * activation).astype(jnp.bfloat16)
    grad_gate = (
        hidden_grad * up_pre * sigmoid_gate * (1.0 + gate_pre * (1.0 - sigmoid_gate))
    ).astype(jnp.bfloat16)
    row_terms = (
        lax.dot_general(grad_gate, w_gate, contract, preferred_element_type=jnp.float32)
        + lax.dot_general(grad_up, w_up, contract, preferred_element_type=jnp.float32)
    ).astype(jnp.bfloat16)
    return (row_terms, weight_grad)


def slot_plan(routes, experts, capacity):
    tok_rows, top_count = routes.shape
    flat_ids = routes.reshape(-1)
    pad_pair = flat_ids.shape[0]
    pair_ids = jnp.arange(pad_pair, dtype=jnp.int32)
    sort_order = jnp.argsort(flat_ids, stable=True)
    sorted_ids = flat_ids[sort_order]
    onehot = (flat_ids[:, None] == jnp.arange(experts, dtype=jnp.int32)[None, :]).astype(jnp.int32)
    counts = jnp.sum(onehot, axis=0)
    starts = jnp.cumsum(counts) - counts
    sorted_rank = pair_ids - starts[sorted_ids]
    sorted_slot = sorted_ids * capacity + sorted_rank
    slot_of_pair = jnp.zeros((pad_pair,), jnp.int32).at[sort_order].set(sorted_slot)
    slot_pair = jnp.full((experts * capacity,), pad_pair, jnp.int32).at[sorted_slot].set(sort_order)
    slot_token = jnp.where(slot_pair < pad_pair, slot_pair // top_count, tok_rows)
    return (slot_of_pair, slot_token, slot_pair)


def place_rows(source_rows, slot_token):
    padded = jnp.concatenate(
        [source_rows, jnp.zeros((1, source_rows.shape[1]), source_rows.dtype)], 0
    )
    return padded[slot_token]


def on_device(tokens, cotangent, expert_ids, route_weights, w_gate, w_up, w_down):
    group_count = lax.axis_size("grp")
    lane_count = lax.axis_size("ep")
    experts = group_count * lane_count
    tok_rows, top_count = expert_ids.shape
    model_width = tokens.shape[1]
    capacity = 2 * tok_rows * top_count // experts
    slot_of_pair, slot_token, unused_pairs = slot_plan(expert_ids, experts, capacity)
    send_rows = place_rows(tokens, slot_token).reshape(
        group_count, lane_count, capacity, model_width
    )
    send_grads = place_rows(cotangent, slot_token).reshape(
        group_count, lane_count, capacity, model_width
    )
    send_rows, send_grads = (
        lax.all_to_all(send_rows, "grp", split_axis=0, concat_axis=0, tiled=True),
        lax.all_to_all(send_grads, "grp", split_axis=0, concat_axis=0, tiled=True),
    )
    rows_in = lax.all_to_all(send_rows, "ep", split_axis=1, concat_axis=1, tiled=True)
    grads_in = lax.all_to_all(send_grads, "ep", split_axis=1, concat_axis=1, tiled=True)
    leading = rows_in.shape[:3]
    row_terms, weight_grad = expert_grads(
        rows_in.reshape(-1, model_width),
        grads_in.reshape(-1, model_width),
        w_gate[0],
        w_up[0],
        w_down[0],
    )
    row_terms = row_terms.reshape(leading + (model_width,))
    weight_grad = weight_grad.reshape(leading)
    row_terms, weight_grad = (
        lax.all_to_all(row_terms, "ep", split_axis=1, concat_axis=1, tiled=True),
        lax.all_to_all(weight_grad, "ep", split_axis=1, concat_axis=1, tiled=True),
    )
    row_terms, weight_grad = (
        lax.all_to_all(row_terms, "grp", split_axis=0, concat_axis=0, tiled=True),
        lax.all_to_all(weight_grad, "grp", split_axis=0, concat_axis=0, tiled=True),
    )
    row_terms = row_terms.reshape(experts * capacity, model_width)
    weight_grad = weight_grad.reshape(experts * capacity)
    picked = row_terms[slot_of_pair].reshape(tok_rows, top_count, model_width)
    grad_tokens = jnp.sum(route_weights[:, :, None] * picked.astype(jnp.float32), axis=1)
    grad_weights = weight_grad[slot_of_pair].reshape(tok_rows, top_count)
    return (grad_tokens.astype(jnp.bfloat16), grad_weights)


def solution(mesh):
    in_specs = (
        P(("parts", "grp", "ep"), None),
        P(("parts", "grp", "ep"), None),
        P(("parts", "grp", "ep"), None),
        P(("parts", "grp", "ep"), None),
        P(("grp", "ep"), None, None),
        P(("grp", "ep"), None, None),
        P(("grp", "ep"), None, None),
    )
    out_specs = (P(("parts", "grp", "ep"), None), P(("parts", "grp", "ep"), None))
    return jax.shard_map(
        on_device, mesh=mesh, in_specs=in_specs, out_specs=out_specs, check_vma=False
    )
```

profile of v0, /device:TPU:0, one launch (start us, length us, event | category | flops | bytes accessed | tf_op | source)
XLA Modules:
  0.0 371.9 jit_solution(18165416981116099275)
XLA Ops:
  2.9 4.4 %sort.17 = (s32[640]{0:T(1024)}, s32[640]{0:T(1024)S(1)}) sort(s32[640]{0:T(1024)S(1)} %reshape.108, s32[640]{0:T(1024)S(1)} %iota.14), dimensions={0}, to_apply=%region_0.0 | sort | flops 6400 | bytes 10240 | tf_op jit(solution)/shard_map/jit(argsort)/sort | solution.py:32
  10.0 4.5 %fusion.15 = (s32[640]{0:T(1024)S(1)}, s32[640,1]{0,1:T(1,128)S(1)}) fusion(s32[]{:T(128)} %bitcast.10, s32[]{:T(128)} %bitcast.11, s32[]{:T(128)} %bitcast.12, s32[]{:T(128)} %bitcast.13, s32[]{:T(128)} %bitcast.14, s32[]{:T(128)} %bitcast.16, s32[]{:T(128)} %bitcast.15, s32[640]{0:T(1024)S(1)} %gather_fusion), kind=kLoop, calls=%fused_computation.57 | loop fusion | flops 9600 | bytes 7708 | tf_op jit(solution)/shard_map/gather | solution.py:37
  14.6 5.5 %subtract_add_fusion = (s32[640]{0:T(1024)S(1)}, s32[640]{0:T(1024)S(1)}) fusion(s32[640]{0:T(1024)S(1)} %gather_fusion, pred[640]{0:T(1024)(128)(4,1)S(1)} %get-tuple-element.22, pred[640]{0:T(1024)(128)(4,1)S(1)} %get-tuple-element.21, pred[640]{0:T(1024)(128)(4,1)S(1)} %get-tuple-element.20, pred[640]{0:T(1024)(128)(4,1)S(1)} %get-tuple-element.19, ...), kind=kLoop, calls=%fused_computation.54 | loop fusion | flops 7680 | bytes 16036 | tf_op jit(solution)/shard_map/add | solution.py:38
  20.1 4.1 %scatter_custom_fusion = s32[1280]{0:T(1024)S(1)} fusion(s32[640]{0:T(1024)S(1)} %fusion.16, s32[640]{0:T(1024)S(1)} %get-tuple-element.3, s32[]{:T(128)} %constant.14.clone.1), kind=kCustom, calls=%fused_computation.55 | custom fusion | bytes 5124 | tf_op jit(solution)/shard_map/scatter | solution.py:40
  24.3 5.1 %gather_fusion.2 = bf16[1280,1024]{1,0:T(8,128)(2,1)} fusion(bf16[129,1024]{1,0:T(8,128)(2,1)S(1)} %concatenate.7, s32[2048]{0:T(1024)S(1)} %pad_clamp_fusion), kind=kCustom, calls=%fused_computation.2 | custom fusion | bytes 5248000 | tf_op jit(solution)/shard_map/gather | solution.py:49
  29.4 4.7 %all-to-all-start.2 = ((bf16[4,4,80,1024]{3,2,1,0:T(8,128)(2,1)}), bf16[4,4,80,1024]{3,2,1,0:T(8,128)(2,1)}, u32[]{:S(2)}, u32[]{:S(2)}) async-start(bf16[4,4,80,1024]{3,2,1,0:T(8,128)(2,1)} %bitcast.42), calls=%async_computation.2 | async-start | bytes 5242880 | tf_op jit(solution)/shard_map/all_to_all | solution.py:67
  34.1 5.1 %gather_fusion.1 = bf16[1280,1024]{1,0:T(8,128)(2,1)} fusion(bf16[129,1024]{1,0:T(8,128)(2,1)S(1)} %concatenate.6, s32[2048]{0:T(1024)S(1)} %pad_clamp_fusion), kind=kCustom, calls=%fused_computation.1 | custom fusion | bytes 5248000 | tf_op jit(solution)/shard_map/gather | solution.py:49
  39.3 26.8 %all-to-all-done.2 = bf16[4,4,80,1024]{3,2,1,0:T(8,128)(2,1)} async-done(((bf16[4,4,80,1024]{3,2,1,0:T(8,128)(2,1)}), bf16[4,4,80,1024]{3,2,1,0:T(8,128)(2,1)}, u32[]{:S(2)}, u32[]{:S(2)}) %all-to-all-start.2) | async-done | bytes 2621472 | tf_op jit(solution)/shard_map/all_to_all | solution.py:67
  66.1 4.5 %all-to-all-start = ((bf16[4,4,80,1024]{3,2,1,0:T(8,128)(2,1)}), bf16[4,4,80,1024]{3,2,1,0:T(8,128)(2,1)}, u32[]{:S(2)}, u32[]{:S(2)}) async-start(bf16[4,4,80,1024]{3,2,1,0:T(8,128)(2,1)} %bitcast.41), calls=%async_computation | async-start | bytes 5242880 | tf_op jit(solution)/shard_map/all_to_all | solution.py:68
  74.2 27.8 %all-to-all-done = bf16[4,4,80,1024]{3,2,1,0:T(8,128)(2,1)} async-done(((bf16[4,4,80,1024]{3,2,1,0:T(8,128)(2,1)}), bf16[4,4,80,1024]{3,2,1,0:T(8,128)(2,1)}, u32[]{:S(2)}, u32[]{:S(2)}) %all-to-all-start) | async-done | bytes 2621472 | tf_op jit(solution)/shard_map/all_to_all | solution.py:68
  102.0 5.7 %all-to-all-start.3 = ((bf16[4,4,80,1024]{3,2,0,1:T(8,128)(2,1)}), bf16[4,4,80,1024]{3,2,0,1:T(8,128)(2,1)}, u32[]{:S(2)}, u32[]{:S(2)}) async-start(bf16[4,4,80,1024]{3,2,0,1:T(8,128)(2,1)} %copy.52), calls=%async_computation.3 | async-start | bytes 5242880 | tf_op jit(solution)/shard_map/all_to_all | solution.py:70
  111.3 55.7 %all-to-all-done.3 = bf16[4,4,80,1024]{3,2,0,1:T(8,128)(2,1)} async-done(((bf16[4,4,80,1024]{3,2,0,1:T(8,128)(2,1)}), bf16[4,4,80,1024]{3,2,0,1:T(8,128)(2,1)}, u32[]{:S(2)}, u32[]{:S(2)}) %all-to-all-start.3) | async-done | bytes 2621472 | tf_op jit(solution)/shard_map/all_to_all | solution.py:70
  167.0 4.7 %all-to-all-start.1 = ((bf16[4,4,80,1024]{3,2,0,1:T(8,128)(2,1)}), bf16[4,4,80,1024]{3,2,0,1:T(8,128)(2,1)}, u32[]{:S(2)}, u32[]{:S(2)}) async-start(bf16[4,4,80,1024]{3,2,0,1:T(8,128)(2,1)} %copy.50), calls=%async_computation.1 | async-start | bytes 5242880 | tf_op jit(solution)/shard_map/all_to_all | solution.py:71
  180.2 50.4 %all-to-all-done.1 = bf16[4,4,80,1024]{3,2,0,1:T(8,128)(2,1)} async-done(((bf16[4,4,80,1024]{3,2,0,1:T(8,128)(2,1)}), bf16[4,4,80,1024]{3,2,0,1:T(8,128)(2,1)}, u32[]{:S(2)}, u32[]{:S(2)}) %all-to-all-start.1) | async-done | bytes 2621472 | tf_op jit(solution)/shard_map/all_to_all | solution.py:71
  236.9 4.6 %fusion.1 = f32[1280,1024]{1,0:T(8,128)} fusion(f32[1280,512]{0,1:T(8,128)S(1)} %copy-done.7, f32[1280,512]{0,1:T(8,128)S(1)} %get-tuple-element.44, f32[1280,512]{0,1:T(8,128)S(1)} %copy-done.9, bf16[1,1024,512]{2,1,0:T(8,128)(2,1)S(1)} %copy-done), kind=kOutput, calls=%fused_computation.14 | convolution fusion | flops 1348730880 | bytes 14155776 | tf_op jit(solution)/shard_map/dot_general | solution.py:21
  245.5 5.8 %add_convert_fusion = bf16[1280,1024]{1,0:T(8,128)(2,1)S(1)} fusion(f32[1280,1024]{1,0:T(8,128)} %fusion.1, f32[1280,512]{0,1:T(8,128)} %copy-done.8, bf16[1,1024,512]{2,1,0:T(8,128)(2,1)S(1)} %copy-done.6, f32[1280,512]{0,1:T(8,128)} %fusion.3), kind=kOutput, calls=%fused_computation.7 | convolution fusion | flops 1348730880 | bytes 14155776 | tf_op jit(solution)/shard_map/dot_general | solution.py:22
  253.0 5.0 %all-to-all-start.4 = ((bf16[4,4,80,1024]{3,2,0,1:T(8,128)(2,1)}), bf16[4,4,80,1024]{3,2,0,1:T(8,128)(2,1)}, u32[]{:S(2)}, u32[]{:S(2)}) async-start(bf16[4,4,80,1024]{3,2,0,1:T(8,128)(2,1)} %copy.54), calls=%async_computation.4 | async-start | bytes 5242880 | tf_op jit(solution)/shard_map/all_to_all | solution.py:83
  258.7 57.9 %all-to-all-done.4 = bf16[4,4,80,1024]{3,2,0,1:T(8,128)(2,1)} async-done(((bf16[4,4,80,1024]{3,2,0,1:T(8,128)(2,1)}), bf16[4,4,80,1024]{3,2,0,1:T(8,128)(2,1)}, u32[]{:S(2)}, u32[]{:S(2)}) %all-to-all-start.4) | async-done | bytes 2621472 | tf_op jit(solution)/shard_map/all_to_all | solution.py:83
  323.6 4.5 %all-to-all-start.5 = ((bf16[4,4,80,1024]{3,2,1,0:T(8,128)(2,1)}), bf16[4,4,80,1024]{3,2,1,0:T(8,128)(2,1)}, u32[]{:S(2)}, u32[]{:S(2)}) async-start(bf16[4,4,80,1024]{3,2,1,0:T(8,128)(2,1)} %copy.55), calls=%async_computation.5 | async-start | bytes 5242880 | tf_op jit(solution)/shard_map/all_to_all | solution.py:87
  328.1 4.3 %scatter_custom_fusion.1 = s32[640]{0:T(1024)S(1)} fusion(s32[640]{0:T(1024)S(1)} %compare_select_fusion.4, s32[640]{0:T(1024)S(1)} %get-tuple-element.23, s32[]{:T(128)} %constant.6.clone.1), kind=kCustom, calls=%fused_computation.59 | custom fusion | bytes 2564 | tf_op jit(solution)/shard_map/scatter | solution.py:39
  332.7 4.3 %gather_fusion.4 = bf16[640]{0:T(1024)(128)(2,1)S(1)} fusion(bf16[1280]{0:T(1024)(128)(2,1)S(1)} %reshape.117, s32[1024]{0:T(1024)S(1)} %pad_clamp_fusion.1), kind=kCustom, calls=%fused_computation.4 | custom fusion | bytes 5120 | tf_op jit(solution)/shard_map/gather | solution.py:94
  337.9 21.6 %all-to-all-done.5 = bf16[4,4,80,1024]{3,2,1,0:T(8,128)(2,1)} async-done(((bf16[4,4,80,1024]{3,2,1,0:T(8,128)(2,1)}), bf16[4,4,80,1024]{3,2,1,0:T(8,128)(2,1)}, u32[]{:S(2)}, u32[]{:S(2)}) %all-to-all-start.5) | async-done | bytes 2621472 | tf_op jit(solution)/shard_map/all_to_all | solution.py:87
  359.5 6.0 %gather_fusion.3 = bf16[640,1024]{1,0:T(8,128)(2,1)S(1)} fusion(bf16[1280,1024]{1,0:T(8,128)(2,1)} %bitcast.25, s32[1024]{0:T(1024)S(1)} %pad_clamp_fusion.1), kind=kCustom, calls=%fused_computation.3 | custom fusion | bytes 2624000 | tf_op jit(solution)/shard_map/gather | solution.py:92
  367.6 4.3 %multiply_reduce_fusion = bf16[128,1024]{1,0:T(8,128)(2,1)} fusion(f32[128,5,1024]{2,1,0:T(8,128)} %reshape.119, f32[128,5]{1,0:T(8,128)S(1)} %copy.47), kind=kLoop, calls=%fused_computation.8 | loop fusion | flops 1179648 | bytes 2886144 | tf_op jit(solution)/shard_map/reduce_sum | solution.py:93
  (61 shorter events, 43.5 us)
Async XLA Ops:
  0.6 173.2 %copy-start = (bf16[1,1024,512]{2,1,0:T(8,128)(2,1)S(1)}, bf16[1,1024,512]{2,1,0:T(8,128)(2,1)}, u32[]{:S(2)}) copy-start(bf16[1,1024,512]{2,1,0:T(8,128)(2,1)} %param.11) | copy-start | bytes 3145732
  0.6 23.6 %copy-start.1 = (bf16[128,1024]{1,0:T(8,128)(2,1)S(1)}, bf16[128,1024]{1,0:T(8,128)(2,1)}, u32[]{:S(2)}) copy-start(bf16[128,1024]{1,0:T(8,128)(2,1)} %param.7) | copy-start | bytes 786436
  29.4 4.7 %copy-start.2 = (bf16[128,1024]{1,0:T(8,128)(2,1)S(1)}, bf16[128,1024]{1,0:T(8,128)(2,1)}, u32[]{:S(2)}) copy-start(bf16[128,1024]{1,0:T(8,128)(2,1)} %param.8) | copy-start | bytes 786436
  29.4 36.7 %all-to-all-start.2 = ((bf16[4,4,80,1024]{3,2,1,0:T(8,128)(2,1)}), bf16[4,4,80,1024]{3,2,1,0:T(8,128)(2,1)}, u32[]{:S(2)}, u32[]{:S(2)}) async-start(bf16[4,4,80,1024]{3,2,1,0:T(8,128)(2,1)} %bitcast.42), calls=%async_computation.2 | async-start | bytes 5242880 | tf_op jit(solution)/shard_map/all_to_all | solution.py:67
  66.1 35.9 %all-to-all-start = ((bf16[4,4,80,1024]{3,2,1,0:T(8,128)(2,1)}), bf16[4,4,80,1024]{3,2,1,0:T(8,128)(2,1)}, u32[]{:S(2)}, u32[]{:S(2)}) async-start(bf16[4,4,80,1024]{3,2,1,0:T(8,128)(2,1)} %bitcast.41), calls=%async_computation | async-start | bytes 5242880 | tf_op jit(solution)/shard_map/all_to_all | solution.py:68
  102.0 65.0 %all-to-all-start.3 = ((bf16[4,4,80,1024]{3,2,0,1:T(8,128)(2,1)}), bf16[4,4,80,1024]{3,2,0,1:T(8,128)(2,1)}, u32[]{:S(2)}, u32[]{:S(2)}) async-start(bf16[4,4,80,1024]{3,2,0,1:T(8,128)(2,1)} %copy.52), calls=%async_computation.3 | async-start | bytes 5242880 | tf_op jit(solution)/shard_map/all_to_all | solution.py:70
  167.0 63.6 %all-to-all-start.1 = ((bf16[4,4,80,1024]{3,2,0,1:T(8,128)(2,1)}), bf16[4,4,80,1024]{3,2,0,1:T(8,128)(2,1)}, u32[]{:S(2)}, u32[]{:S(2)}) async-start(bf16[4,4,80,1024]{3,2,0,1:T(8,128)(2,1)} %copy.50), calls=%async_computation.1 | async-start | bytes 5242880 | tf_op jit(solution)/shard_map/all_to_all | solution.py:71
  173.8 3.2 copy-start.5
  180.2 52.6 %copy-start.4 = (bf16[1,512,1024]{2,1,0:T(8,128)(2,1)S(1)}, bf16[1,512,1024]{2,1,0:T(8,128)(2,1)}, u32[]{:S(2)}) copy-start(bf16[1,512,1024]{2,1,0:T(8,128)(2,1)} %param.13) | copy-start | bytes 3145732
  230.6 2.5 copy-start.7
  233.1 3.8 %copy-start.9 = (f32[1280,512]{0,1:T(8,128)S(1)}, f32[1280,512]{0,1:T(8,128)}, u32[]{:S(2)}) copy-start(f32[1280,512]{0,1:T(8,128)} %fusion.6) | copy-start | bytes 7864324
  236.9 4.7 %copy-start.8 = (f32[1280,512]{0,1:T(8,128)}, f32[1280,512]{0,1:T(8,128)S(1)}, u32[]{:S(2)}) copy-start(f32[1280,512]{0,1:T(8,128)S(1)} %get-tuple-element.44) | copy-start | bytes 7864324
  236.9 8.6 %copy-start.6 = (bf16[1,1024,512]{2,1,0:T(8,128)(2,1)S(1)}, bf16[1,1024,512]{2,1,0:T(8,128)(2,1)}, u32[]{:S(2)}) copy-start(bf16[1,1024,512]{2,1,0:T(8,128)(2,1)} %param.12) | copy-start | bytes 3145732
  242.2 10.8 %all-to-all-start.6 = ((bf16[4,4,80]{2,0,1:T(4,128)(2,1)}), bf16[4,4,80]{2,0,1:T(4,128)(2,1)S(1)}, u32[]{:S(2)}, u32[]{:S(2)}) async-start(bf16[4,4,80]{2,0,1:T(4,128)(2,1)} %copy.56), calls=%async_computation.6 | async-start | bytes 8192 | tf_op jit(solution)/shard_map/all_to_all | solution.py:84
  253.0 63.5 %all-to-all-start.4 = ((bf16[4,4,80,1024]{3,2,0,1:T(8,128)(2,1)}), bf16[4,4,80,1024]{3,2,0,1:T(8,128)(2,1)}, u32[]{:S(2)}, u32[]{:S(2)}) async-start(bf16[4,4,80,1024]{3,2,0,1:T(8,128)(2,1)} %copy.54), calls=%async_computation.4 | async-start | bytes 5242880 | tf_op jit(solution)/shard_map/all_to_all | solution.py:83
  316.6 7.0 %all-to-all-start.7 = ((bf16[4,4,80]{2,1,0:T(4,128)(2,1)}), bf16[4,4,80]{2,1,0:T(4,128)(2,1)S(1)}, u32[]{:S(2)}, u32[]{:S(2)}) async-start(bf16[4,4,80]{2,1,0:T(4,128)(2,1)} %copy.57), calls=%async_computation.7 | async-start | bytes 8192 | tf_op jit(solution)/shard_map/all_to_all | solution.py:88
  323.4 9.0 %copy-start.3 = (f32[128,5]{0,1:T(8,128)S(1)}, f32[128,5]{0,1:T(8,128)}, u32[]{:S(2)}) copy-start(f32[128,5]{0,1:T(8,128)} %param.10) | copy-start | bytes 7684
  323.6 35.9 %all-to-all-start.5 = ((bf16[4,4,80,1024]{3,2,1,0:T(8,128)(2,1)}), bf16[4,4,80,1024]{3,2,1,0:T(8,128)(2,1)}, u32[]{:S(2)}, u32[]{:S(2)}) async-start(bf16[4,4,80,1024]{3,2,1,0:T(8,128)(2,1)} %copy.55), calls=%async_computation.5 | async-start | bytes 5242880 | tf_op jit(solution)/shard_map/all_to_all | solution.py:87
where the time goes:
time: 373 us; the launch traced here: 372 us
  waiting for transfers between devices  240 us (64%)
  local copies, waits for them, and re-layouts  55.2 us (15%)
  starting transfers between devices  35.7 us (10%)
  matrix products  20.5 us (5%)
  other arithmetic  19.1 us (5%)
    all_to_all x1, waiting for transfers between devices, on_device(): lax.all_to_all(row_terms, 'ep', split_axis=1, concat_axis=1, tiled=True)  57.9 us
    all_to_all x1, waiting for transfers between devices, on_device(): lax.all_to_all(send_rows, 'ep', split_axis=1, concat_axis=1, tiled=True)  55.7 us
    all_to_all x1, waiting for transfers between devices, on_device(): lax.all_to_all(send_grads, 'ep', split_axis=1, concat_axis=1, tiled=True)  50.4 us
    all_to_all x1, waiting for transfers between devices, on_device(): lax.all_to_all(send_grads, 'grp', split_axis=0, concat_axis=0, tiled=True)  27.8 us
    all_to_all x1, waiting for transfers between devices, on_device(): lax.all_to_all(send_rows, 'grp', split_axis=0, concat_axis=0, tiled=True)  26.8 us
    all_to_all x1, waiting for transfers between devices, on_device(): lax.all_to_all(row_terms, 'grp', split_axis=0, concat_axis=0, tiled=True)  21.6 us
    gather x2, local copies, waits for them, and re-layouts, place_rows(): return padded[slot_token]  10.2 us
  transfers between devices with their start and end apart: 8, of which 7 were waited for; matrix products, arithmetic and copies ran while one was open for 11% of the time, Pallas kernels for 0%

commit v1 on v0

v1 whole, which is shorter than its diff:
```python
import jax
import jax.numpy as jnp
import numpy as np
from jax import lax
from jax.experimental import pallas as pl
from jax.experimental.pallas import tpu as pltpu
from jax.sharding import PartitionSpec as P

BOTH = ("grp", "ep")
CONTRACT_LAST = (((1,), (1,)), ((), ()))


def expert_grads(rows_in, grads_in, w_gate, w_up, w_down):
    gate_pre = jnp.dot(rows_in, w_gate, preferred_element_type=jnp.float32)
    up_pre = jnp.dot(rows_in, w_up, preferred_element_type=jnp.float32)
    hidden_grad = lax.dot_general(grads_in, w_down, CONTRACT_LAST, preferred_element_type=jnp.float32)
    sigmoid_gate = 1.0 / (1.0 + jnp.exp(-gate_pre))
    activation = gate_pre * sigmoid_gate
    hidden = activation * up_pre
    weight_grad = jnp.sum(hidden_grad * hidden, axis=-1, keepdims=True)
    grad_up = (hidden_grad * activation).astype(jnp.bfloat16)
    grad_gate = (
        hidden_grad * up_pre * sigmoid_gate * (1.0 + gate_pre * (1.0 - sigmoid_gate))
    ).astype(jnp.bfloat16)
    row_terms = (
        lax.dot_general(grad_gate, w_gate, CONTRACT_LAST, preferred_element_type=jnp.float32)
        + lax.dot_general(grad_up, w_up, CONTRACT_LAST, preferred_element_type=jnp.float32)
    ).astype(jnp.bfloat16)
    return (row_terms, weight_grad)


def slot_plan(routes, experts, capacity):
    tok_rows, top_count = routes.shape
    flat_ids = routes.reshape(-1)
    pad_pair = flat_ids.shape[0]
    pair_ids = jnp.arange(pad_pair, dtype=jnp.int32)
    sort_order = jnp.argsort(flat_ids, stable=True)
    sorted_ids = flat_ids[sort_order]
    onehot = (flat_ids[:, None] == jnp.arange(experts, dtype=jnp.int32)[None, :]).astype(jnp.int32)
    counts = jnp.sum(onehot, axis=0)
    starts = jnp.cumsum(counts) - counts
    sorted_rank = pair_ids - starts[sorted_ids]
    sorted_slot = sorted_ids * capacity + sorted_rank
    slot_of_pair = jnp.zeros((pad_pair,), jnp.int32).at[sort_order].set(sorted_slot)
    slot_pair = jnp.full((experts * capacity,), pad_pair, jnp.int32).at[sorted_slot].set(sort_order)
    slot_token = jnp.where(slot_pair < pad_pair, slot_pair // top_count, tok_rows)
    return (slot_of_pair, slot_token)


def place_rows(source_rows, slot_token):
    padded = jnp.concatenate(
        [source_rows, jnp.zeros((1, source_rows.shape[1]), source_rows.dtype)], 0
    )
    return padded[slot_token]


def routed_plan(tokens, cotangent, expert_ids, route_weights, w_gate, w_up, w_down):
    group_count = lax.axis_size("grp")
    lane_count = lax.axis_size("ep")
    experts = group_count * lane_count
    tok_rows, top_count = expert_ids.shape
    model_width = tokens.shape[1]
    capacity = 2 * tok_rows * top_count // experts
    slot_of_pair, slot_token = slot_plan(expert_ids, experts, capacity)
    shape = (group_count, lane_count, capacity)

    def there_and(array, axes):
        for axis in axes:
            at = BOTH.index(axis)
            array = lax.all_to_all(array, axis, split_axis=at, concat_axis=at, tiled=True)
        return array

    rows_in = there_and(place_rows(tokens, slot_token).reshape(shape + (model_width,)), BOTH)
    grads_in = there_and(place_rows(cotangent, slot_token).reshape(shape + (model_width,)), BOTH)
    row_terms, weight_grad = expert_grads(
        rows_in.reshape(-1, model_width),
        grads_in.reshape(-1, model_width),
        w_gate[0],
        w_up[0],
        w_down[0],
    )
    row_terms = there_and(row_terms.reshape(shape + (model_width,)), BOTH[::-1])
    weight_grad = there_and(weight_grad.astype(jnp.bfloat16).reshape(shape), BOTH[::-1])
    row_terms = row_terms.reshape(experts * capacity, model_width)
    weight_grad = weight_grad.reshape(experts * capacity)
    picked = row_terms[slot_of_pair].reshape(tok_rows, top_count, model_width)
    grad_tokens = jnp.sum(route_weights[:, :, None] * picked.astype(jnp.float32), axis=1)
    grad_weights = weight_grad[slot_of_pair].reshape(tok_rows, top_count)
    return (grad_tokens.astype(jnp.bfloat16), grad_weights)


def grads_kernel(blocks, rows, *refs):
    token_refs, refs = refs[:blocks], refs[blocks:]
    grad_refs, refs = refs[:blocks], refs[blocks:]
    share_ref, gate_a, up_a, down_a, gate_b, up_b, down_b, sum_ref, weight_ref = refs
    rows_in = jnp.concatenate([ref[...] for ref in token_refs], 0)
    grads_in = jnp.concatenate([ref[...] for ref in grad_refs], 0)
    total = None
    for at, (gate, up, down) in enumerate(((gate_a, up_a, down_a), (gate_b, up_b, down_b))):
        row_terms, weight_grad = expert_grads(rows_in, grads_in, gate[...], up[...], down[...])
        scaled = share_ref[:, at : at + 1] * row_terms.astype(jnp.float32)
        total = scaled if total is None else total + scaled
        weight_ref[:, at : at + 1] = weight_grad
    sum_ref[...] = total


def block_grads(tokens, grads, shares, weights):
    blocks = len(tokens)
    rows, width = tokens[0].shape
    hidden = weights[0].shape[1]
    return pl.pallas_call(
        lambda *refs: grads_kernel(blocks, rows, *refs),
        out_shape=(
            jax.ShapeDtypeStruct((blocks * rows, width), jnp.float32),
            jax.ShapeDtypeStruct((blocks * rows, 2), jnp.float32),
        ),
        compiler_params=pltpu.CompilerParams(vmem_limit_bytes=32 << 20),
        cost_estimate=pl.CostEstimate(
            flops=2 * 10 * blocks * rows * width * hidden,
            bytes_accessed=12 * width * hidden + 8 * blocks * rows * width,
            transcendentals=2 * blocks * rows * hidden,
        ),
    )(*tokens, *grads, shares, *weights)


def ring_order(chips_x, lanes):
    order = []
    for x in range(chips_x):
        column = [(x, z) for z in range(lanes)]
        order += column if x % 2 == 0 else column[::-1]
    return order


def ring_plan(tokens, cotangent, expert_ids, route_weights, w_gate, w_up, w_down):
    group_count = lax.axis_size("grp")
    lanes = lax.axis_size("ep")
    devices = group_count * lanes
    chips_x = group_count // 2
    rows, top_count = expert_ids.shape
    width = tokens.shape[1]
    order = ring_order(chips_x, lanes)
    chips = len(order)
    far = chips // 2

    def device(place, core):
        x, z = order[place % chips]
        return (2 * x + core) * lanes + z

    place_of = np.zeros((devices,), np.int32)
    core_of = np.zeros((devices,), np.int32)
    for place in range(chips):
        for core in range(2):
            place_of[device(place, core)] = place
            core_of[device(place, core)] = core
    source_table = np.array(
        [[device(int(place_of[d]) - o, int(core_of[d])) for o in range(chips)] for d in range(devices)], np.int32
    )
    offset_table = np.array(
        [
            [(int(place_of[d]) - int(place_of[t])) % chips if core_of[d] == core_of[t] else chips for t in range(devices)]
            for d in range(devices)
        ],
        np.int32,
    )
    ahead = [(device(p, c), device(p + 1, c)) for p in range(chips) for c in range(2)]
    behind = [(device(p, c), device(p - 1, c)) for p in range(chips) for c in range(2)]
    across = [(device(p, c), device(p, 1 - c)) for p in range(chips) for c in range(2)]

    def send(array, pairs):
        return lax.ppermute(array, BOTH, pairs)

    me = lax.axis_index("grp") * lanes + lax.axis_index("ep")
    core = lax.rem(lax.axis_index("grp"), 2)

    got = {0: (tokens, cotangent)}
    token_up = token_down = tokens
    grad_up = grad_down = cotangent
    mine = (w_gate[0], w_up[0], w_down[0])
    for step in range(1, far + 1):
        token_up = send(token_up, ahead)
        grad_down = send(grad_down, behind)
        if step < far:
            grad_up = send(grad_up, ahead)
            token_down = send(token_down, behind)
            got[step] = (token_up, grad_up)
            got[chips - step] = (token_down, grad_down)
        else:
            got[far] = (token_up, grad_down)
        if step == 1:
            other = tuple(send(w, across) for w in mine)

    expert_list = jnp.arange(devices, dtype=jnp.int32)
    chosen = expert_ids[None, :, :] == expert_list[:, None, None]
    dense = jnp.sum(jnp.where(chosen, route_weights[None], 0.0), axis=-1)
    dense = dense.reshape(chips_x, 1, 2, lanes, rows).transpose(0, 1, 3, 2, 4)
    dense = jnp.broadcast_to(dense, (chips_x, 2, lanes, 2, rows)).reshape(devices, 2, rows)
    dense = lax.all_to_all(dense, BOTH, split_axis=0, concat_axis=0, tiled=True)
    shares = jnp.take(dense, jnp.asarray(source_table)[me], axis=0)
    shares = jnp.where(core == 0, shares, shares[:, ::-1]).transpose(0, 2, 1)

    sums, weight_grads = {}, {}
    for step in range(far + 1):
        offsets = (step,) if step in (0, far) else (step, chips - step)
        total, weight_grad = block_grads(
            [got[o][0] for o in offsets],
            [got[o][1] for o in offsets],
            jnp.concatenate([shares[o] for o in offsets], 0),
            mine + other,
        )
        for at, o in enumerate(offsets):
            sums[o] = total[at * rows : (at + 1) * rows]
            weight_grads[o] = weight_grad[at * rows : (at + 1) * rows]

    half = width // 2
    halves = (slice(0, half), slice(half, width))

    def chain(columns, pairs, offsets):
        moving = sums[offsets[0]][:, columns].astype(jnp.bfloat16)
        for o in offsets[1:]:
            moving = send(moving, pairs)
            moving = (moving.astype(jnp.float32) + sums[o][:, columns]).astype(jnp.bfloat16)
        return send(moving, pairs).astype(jnp.float32)

    up_way = [(chips - s) for s in range(far, 0, -1)]
    down_way = list(range(far, 0, -1))
    back = [
        sums[0][:, halves[0]] + chain(halves[0], ahead, up_way) + chain(halves[0], behind, down_way[1:]),
        sums[0][:, halves[1]] + chain(halves[1], ahead, up_way[1:]) + chain(halves[1], behind, down_way),
    ]
    grad_tokens = jnp.concatenate(back, 1).astype(jnp.bfloat16)

    by_offset = jnp.stack([weight_grads[o] for o in range(chips)] + [jnp.zeros((rows, 2), jnp.float32)])
    by_offset = by_offset.transpose(0, 2, 1).astype(jnp.bfloat16)
    by_offset = jnp.where(core == 0, by_offset, by_offset[:, ::-1])
    outgoing = jnp.take(by_offset, jnp.asarray(offset_table)[me], axis=0)
    incoming = lax.all_to_all(outgoing, BOTH, split_axis=0, concat_axis=0, tiled=True)
    incoming = incoming.reshape(chips_x, 2, lanes, 2, rows).sum(axis=1)
    incoming = incoming.transpose(0, 2, 1, 3).reshape(devices, rows)
    grad_weights = jnp.sum(jnp.where(chosen, incoming[:, :, None], 0), axis=0)
    return (grad_tokens, grad_weights.astype(jnp.bfloat16))


def on_device(tokens, cotangent, expert_ids, route_weights, w_gate, w_up, w_down):
    group_count = lax.axis_size("grp")
    experts = group_count * lax.axis_size("ep")
    rows, top_count = expert_ids.shape
    capacity = 2 * rows * top_count // experts
    dense = 2 * capacity >= rows and group_count % 2 == 0
    plan = ring_plan if dense else routed_plan
    return plan(tokens, cotangent, expert_ids, route_weights, w_gate, w_up, w_down)


def solution(mesh):
    in_specs = (
        P(("parts", "grp", "ep"), None),
        P(("parts", "grp", "ep"), None),
        P(("parts", "grp", "ep"), None),
        P(("parts", "grp", "ep"), None),
        P(("grp", "ep"), None, None),
        P(("grp", "ep"), None, None),
        P(("grp", "ep"), None, None),
    )
    out_specs = (P(("parts", "grp", "ep"), None), P(("parts", "grp", "ep"), None))
    return jax.shard_map(
        on_device, mesh=mesh, in_specs=in_specs, out_specs=out_specs, check_vma=False
    )
```

time: 373 us -> 129 us (0.35)
  waiting for transfers between devices: 240 us -> 25.3 us
  local copies, waits for them, and re-layouts: 55.2 us -> 20.2 us
  Pallas kernels: 0 us -> 24.9 us
  matrix products: 20.5 us -> 0 us
  blocking collectives: 0 us -> 10.3 us
  other arithmetic: 19.1 us -> 9.09 us
    all_to_all x8 -> x1, waiting for transfers between devices: 240 us -> 0.01 us  [ring_plan(): dense = lax.all_to_all(dense, BOTH, split_axis=0, concat_axis=0, tiled=True)]
    ppermute x0 -> x31, starting transfers between devices: none -> 31.1 us  [send(): return lax.ppermute(array, BOTH, pairs)]
    all_to_all x8 -> x1, starting transfers between devices: 35.7 us -> 6.36 us  [ring_plan(): dense = lax.all_to_all(dense, BOTH, split_axis=0, concat_axis=0, tiled=True)]
    ppermute x0 -> x31, waiting for transfers between devices: none -> 25.3 us  [send(): return lax.ppermute(array, BOTH, pairs)]
    pallas_call x0 -> x5, Pallas kernels: none -> 24.9 us  [block_grads(): pl.pallas_call(lambda *refs: grads_kernel(blocks, rows, *refs), out_shape...]
    gather x6 -> x2, local copies, waits for them, and re-layouts: 24 us -> 1.16 us  [the longest x1 0.59 us: ring_plan(): outgoing = jnp.take(by_offset, jnp.asarray(offset_table)[me], axis=0)]
    dot_general x5 -> x0, matrix products: 20.5 us -> none  [the longest x1 5.75 us: expert_grads(): lax.dot_general(grad_up, w_up, contract, preferred_element_type=jnp.float32)]
    all_to_all x6 -> x0, local copies, waits for them, and re-layouts: 15.5 us -> none  [the longest x1 3.6 us: on_device(): lax.all_to_all(row_terms, 'ep', split_axis=1, concat_axis=1, tiled=True)]
  transfers between devices with their start and end apart: 8 -> 32, of which waited for: 7 -> 12; matrix products, arithmetic and copies ran while one was open for 11% -> 11% of each run, Pallas kernels for 0% -> 19%
where the time goes in v1:
time: 129 us; the launch traced here: 128 us
  starting transfers between devices  37.4 us (29%)
  waiting for transfers between devices  25.3 us (20%)
  Pallas kernels  24.9 us (19%)
  local copies, waits for them, and re-layouts  20.2 us (16%)
  blocking collectives  10.3 us (8%)
  other arithmetic  9.09 us (7%)
    ppermute x31, starting transfers between devices, send(): return lax.ppermute(array, BOTH, pairs)  31.1 us
    ppermute x31, waiting for transfers between devices, send(): return lax.ppermute(array, BOTH, pairs)  25.3 us
    pallas_call x5, Pallas kernels, block_grads(): pl.pallas_call(lambda *refs: grads_kernel(blocks, rows, *refs), out_shape...  24.9 us
    unnamed x71, local copies, waits for them, and re-layouts  13 us
    all_to_all x1, blocking collectives, ring_plan(): lax.all_to_all(outgoing, BOTH, split_axis=0, concat_axis=0, tiled=True)  10.3 us
    all_to_all x1, starting transfers between devices, ring_plan(): dense = lax.all_to_all(dense, BOTH, split_axis=0, concat_axis=0, tiled=True)  6.36 us
    another operation x12, local copies, waits for them, and re-layouts, ring_plan(): jnp.stack([weight_grads[o] for o in range(chips)] + [jnp.zeros((rows, 2),...  2.77 us
  transfers between devices with their start and end apart: 32, of which 12 were waited for; matrix products, arithmetic and copies ran while one was open for 11% of the time, Pallas kernels for 19%

profile of v1, /device:TPU:0, one launch (start us, length us, event | category | flops | bytes accessed | tf_op | source)
XLA Modules:
  0.0 128.3 jit_solution(13330149065931214295)
XLA Ops:
  0.6 3.1 %collective-permute-start.3 = (bf16[128,1024]{1,0:T(8,128)(2,1)}, bf16[128,1024]{1,0:T(8,128)(2,1)S(1)}, u32[]{:S(2)}, u32[]{:S(2)}) collective-permute-start(bf16[128,1024]{1,0:T(8,128)(2,1)} %refs_0_.1), channel_id=1, source_target_pairs={{0,1},{4,5},{1,2},{5,6},{2,3},{6,7},{3,11},{7,15},{11,10},{15,14},... | collective-permute-start | bytes 786440 | tf_op jit(solution)/shard_map/ppermute | solution.py:170
  3.7 2.0 %collective-permute-start.15 = (bf16[128,1024]{1,0:T(8,128)(2,1)}, bf16[128,1024]{1,0:T(8,128)(2,1)S(1)}, u32[]{:S(2)}, u32[]{:S(2)}) collective-permute-start(bf16[128,1024]{1,0:T(8,128)(2,1)} %refs_1_.1), channel_id=1, source_target_pairs={{0,1},{4,5},{1,2},{5,6},{2,3},{6,7},{3,11},{7,15},{11,10},{15,14},... | collective-permute-start | bytes 786440 | tf_op jit(solution)/shard_map/ppermute | solution.py:170
  7.1 6.4 %all-to-all-start = ((f32[16,2,128]{2,1,0:T(2,128)}), f32[16,2,128]{2,1,0:T(2,128)S(1)}, u32[]{:S(2)}, u32[]{:S(2)}) async-start(f32[16,2,128]{2,1,0:T(2,128)} %bitcast.4), calls=%async_computation | async-start | bytes 32768 | tf_op jit(solution)/shard_map/all_to_all | solution.py:197
  15.3 1.7 %collective-permute-start.4 = (bf16[128,1024]{1,0:T(8,128)(2,1)S(1)}, bf16[128,1024]{1,0:T(8,128)(2,1)S(1)}, u32[]{:S(2)}, u32[]{:S(2)}) collective-permute-start(bf16[128,1024]{1,0:T(8,128)(2,1)S(1)} %collective-permute-done.3.refs_0_), channel_id=1, source_target_pairs={{0,1},{4,5},{1,2},{5,6},{2,3},{6,7},{3,11},{7,15},{11,10},{15,14},... | collective-permute-start | bytes 786440 | tf_op jit(solution)/shard_map/ppermute | solution.py:170
  18.1 1.7 %collective-permute-start.16 = (bf16[128,1024]{1,0:T(8,128)(2,1)S(1)}, bf16[128,1024]{1,0:T(8,128)(2,1)S(1)}, u32[]{:S(2)}, u32[]{:S(2)}) collective-permute-start(bf16[128,1024]{1,0:T(8,128)(2,1)S(1)} %collective-permute-done.15.refs_2_), channel_id=1, source_target_pairs={{0,1},{4,5},{1,2},{5,6},{2,3},{6,7},{3,11},{7,15},{11,10},{15,14},... | collective-permute-start | bytes 786440 | tf_op jit(solution)/shard_map/ppermute | solution.py:170
  24.5 1.6 %collective-permute-done.13.refs_1_ = bf16[128,1024]{1,0:T(8,128)(2,1)S(1)} collective-permute-done((bf16[128,1024]{1,0:T(8,128)(2,1)S(1)}, bf16[128,1024]{1,0:T(8,128)(2,1)S(1)}, u32[]{:S(2)}, u32[]{:S(2)}) %collective-permute-start.13) | collective-permute-done | bytes 262176 | tf_op jit(solution)/shard_map/ppermute | solution.py:170
  27.2 2.3 %collective-permute-done.16.refs_2_ = bf16[128,1024]{1,0:T(8,128)(2,1)S(1)} collective-permute-done((bf16[128,1024]{1,0:T(8,128)(2,1)S(1)}, bf16[128,1024]{1,0:T(8,128)(2,1)S(1)}, u32[]{:S(2)}, u32[]{:S(2)}) %collective-permute-start.16) | collective-permute-done | bytes 262176 | tf_op jit(solution)/shard_map/ppermute | solution.py:170
  29.5 1.6 %collective-permute-start.5 = (bf16[128,1024]{1,0:T(8,128)(2,1)S(1)}, bf16[128,1024]{1,0:T(8,128)(2,1)S(1)}, u32[]{:S(2)}, u32[]{:S(2)}) collective-permute-start(bf16[128,1024]{1,0:T(8,128)(2,1)S(1)} %collective-permute-done.4.refs_0_), channel_id=1, source_target_pairs={{0,1},{4,5},{1,2},{5,6},{2,3},{6,7},{3,11},{7,15},{11,10},{15,14},... | collective-permute-start | bytes 786440 | tf_op jit(solution)/shard_map/ppermute | solution.py:170
  32.0 5.4 %collective-permute-done.5.refs_0_ = bf16[128,1024]{1,0:T(8,128)(2,1)S(1)} collective-permute-done((bf16[128,1024]{1,0:T(8,128)(2,1)S(1)}, bf16[128,1024]{1,0:T(8,128)(2,1)S(1)}, u32[]{:S(2)}, u32[]{:S(2)}) %collective-permute-start.5) | collective-permute-done | bytes 262176 | tf_op jit(solution)/shard_map/ppermute | solution.py:170
  37.4 1.7 %collective-permute-start.6 = (bf16[128,1024]{1,0:T(8,128)(2,1)S(1)}, bf16[128,1024]{1,0:T(8,128)(2,1)S(1)}, u32[]{:S(2)}, u32[]{:S(2)}) collective-permute-start(bf16[128,1024]{1,0:T(8,128)(2,1)S(1)} %collective-permute-done.5.refs_0_), channel_id=1, source_target_pairs={{0,1},{4,5},{1,2},{5,6},{2,3},{6,7},{3,11},{7,15},{11,10},{15,14},... | collective-permute-start | bytes 786440 | tf_op jit(solution)/shard_map/ppermute | solution.py:170
  43.0 2.3 %collective-permute-done.6.refs_0_ = bf16[128,1024]{1,0:T(8,128)(2,1)S(1)} collective-permute-done((bf16[128,1024]{1,0:T(8,128)(2,1)S(1)}, bf16[128,1024]{1,0:T(8,128)(2,1)S(1)}, u32[]{:S(2)}, u32[]{:S(2)}) %collective-permute-start.6) | collective-permute-done | bytes 262176 | tf_op jit(solution)/shard_map/ppermute | solution.py:170
  45.4 2.9 %collective-permute-done.10.refs_1_ = bf16[128,1024]{1,0:T(8,128)(2,1)S(1)} collective-permute-done((bf16[128,1024]{1,0:T(8,128)(2,1)S(1)}, bf16[128,1024]{1,0:T(8,128)(2,1)S(1)}, u32[]{:S(2)}, u32[]{:S(2)}) %collective-permute-start.10) | collective-permute-done | bytes 262176 | tf_op jit(solution)/shard_map/ppermute | solution.py:170
  48.3 4.8 %shard_map.105 = (f32[128,1024]{1,0:T(8,128)S(1)}, f32[128,2]{1,0:T(8,128)S(1)}) custom-call(bf16[128,1024]{1,0:T(8,128)(2,1)S(1)} %collective-permute-done.6.refs_0_, bf16[128,1024]{1,0:T(8,128)(2,1)S(1)} %collective-permute-done.10.refs_1_, f32[128,2]{1,0:T(8,128)S(1)} %get-tuple-element.43.refs_2_, bf16[1024,512]{1,0:T(8,128)(2,1)S(1)} %bitcast.61, ...), custom_call_target="tpu_custom_call" | custom-call | flops 1342177280 | bytes 7340032 | tf_op jit(solution)/shard_map/pallas_call | solution.py:111
  54.5 1.5 %collective-permute-start.11 = (bf16[128,512]{1,0:T(8,128)(2,1)}, bf16[128,512]{1,0:T(8,128)(2,1)}, u32[]{:S(2)}, u32[]{:S(2)}) collective-permute-start(bf16[128,512]{1,0:T(8,128)(2,1)} %get-tuple-element.44), channel_id=1, source_target_pairs={{0,1},{4,5},{1,2},{5,6},{2,3},{6,7},{3,11},{7,15},{11,10},{15,14},... | collective-permute-start | bytes 393224 | tf_op jit(solution)/shard_map/ppermute | solution.py:170
  56.5 5.1 %shard_map.106 = (f32[256,1024]{1,0:T(8,128)S(1)}, f32[256,2]{1,0:T(8,128)S(1)}) custom-call(bf16[128,1024]{1,0:T(8,128)(2,1)S(1)} %collective-permute-done.5.refs_0_, bf16[128,1024]{1,0:T(8,128)(2,1)S(1)} %collective-permute-done.14.refs_1_, bf16[128,1024]{1,0:T(8,128)(2,1)S(1)} %collective-permute-done.17.refs_2_, ...), custom_call_target="tpu_custom_call" | custom-call | flops 2684354560 | bytes 8388608 | tf_op jit(solution)/shard_map/pallas_call | solution.py:111
  64.7 4.8 %shard_map.104 = (f32[128,1024]{1,0:T(8,128)S(1)}, f32[128,2]{1,0:T(8,128)S(1)}) custom-call(bf16[128,1024]{1,0:T(8,128)(2,1)S(1)} %copy-done.10, bf16[128,1024]{1,0:T(8,128)(2,1)S(1)} %copy-done.11, f32[128,2]{1,0:T(8,128)S(1)} %get-tuple-element.36.refs_2_, bf16[1024,512]{1,0:T(8,128)(2,1)S(1)} %bitcast.63, bf16[1024,512]{1,0:T(8,128)(2,1)S(1)} %bitcast.69, ...), custom_call_target="tpu_custom_call" | custom-call | flops 1342177280 | bytes 7340032 | tf_op jit(solution)/shard_map/pallas_call | solution.py:111
  75.5 5.1 %shard_map.108 = (f32[256,1024]{1,0:T(8,128)S(1)}, f32[256,2]{1,0:T(8,128)S(1)}) custom-call(bf16[128,1024]{1,0:T(8,128)(2,1)S(1)} %copy-done.15, bf16[128,1024]{1,0:T(8,128)(2,1)S(1)} %copy-done.17, bf16[128,1024]{1,0:T(8,128)(2,1)S(1)} %copy-done.19, bf16[128,1024]{1,0:T(8,128)(2,1)S(1)} %copy-done.21, f32[256,2]{1,0:T(8,128)S(1)} %pad_maximum_fusion.3.refs_4_, ...), custom_call_target="tpu_custom_call" | custom-call | flops 2684354560 | bytes 8388608 | tf_op jit(solution)/shard_map/pallas_call | solution.py:111
  85.2 5.2 %shard_map.107 = (f32[256,1024]{1,0:T(8,128)S(1)}, f32[256,2]{1,0:T(8,128)S(1)}) custom-call(bf16[128,1024]{1,0:T(8,128)(2,1)S(1)} %copy-done.23, bf16[128,1024]{1,0:T(8,128)(2,1)S(1)} %copy-done.26, bf16[128,1024]{1,0:T(8,128)(2,1)S(1)} %copy-done.28, bf16[128,1024]{1,0:T(8,128)(2,1)} %collective-permute-done.8.refs_3_, ...), custom_call_target="tpu_custom_call" | custom-call | flops 2684354560 | bytes 8388608 | tf_op jit(solution)/shard_map/pallas_call | solution.py:111
  94.1 1.5 %collective-permute-start.18 = (bf16[128,512]{1,0:T(8,128)(2,1)S(1)}, bf16[128,512]{1,0:T(8,128)(2,1)S(1)}, u32[]{:S(2)}, u32[]{:S(2)}) collective-permute-start(bf16[128,512]{1,0:T(8,128)(2,1)S(1)} %get-tuple-element.30), channel_id=1, source_target_pairs={{0,1},{4,5},{1,2},{5,6},{2,3},{6,7},{3,11},{7,15},{11,10},{15,14},... | collective-permute-start | bytes 393224 | tf_op jit(solution)/shard_map/ppermute | solution.py:170
  96.2 4.2 %collective-permute-done.18 = bf16[128,512]{1,0:T(8,128)(2,1)S(1)} collective-permute-done((bf16[128,512]{1,0:T(8,128)(2,1)S(1)}, bf16[128,512]{1,0:T(8,128)(2,1)S(1)}, u32[]{:S(2)}, u32[]{:S(2)}) %collective-permute-start.18) | collective-permute-done | bytes 131104 | tf_op jit(solution)/shard_map/ppermute | solution.py:170
  100.5 1.5 %collective-permute-done.28 = bf16[128,512]{1,0:T(8,128)(2,1)S(1)} collective-permute-done((bf16[128,512]{1,0:T(8,128)(2,1)S(1)}, bf16[128,512]{1,0:T(8,128)(2,1)S(1)}, u32[]{:S(2)}, u32[]{:S(2)}) %collective-permute-start.28) | collective-permute-done | bytes 131104 | tf_op jit(solution)/shard_map/ppermute | solution.py:170
  103.2 1.5 %collective-permute-start.19 = (bf16[128,512]{1,0:T(8,128)(2,1)S(1)}, bf16[128,512]{1,0:T(8,128)(2,1)S(1)}, u32[]{:S(2)}, u32[]{:S(2)}) collective-permute-start(bf16[128,512]{1,0:T(8,128)(2,1)S(1)} %get-tuple-element.26), channel_id=1, source_target_pairs={{0,1},{4,5},{1,2},{5,6},{2,3},{6,7},{3,11},{7,15},{11,10},{15,14},... | collective-permute-start | bytes 393224 | tf_op jit(solution)/shard_map/ppermute | solution.py:170
  107.9 1.6 %collective-permute-done.19 = bf16[128,512]{1,0:T(8,128)(2,1)S(1)} collective-permute-done((bf16[128,512]{1,0:T(8,128)(2,1)S(1)}, bf16[128,512]{1,0:T(8,128)(2,1)S(1)}, u32[]{:S(2)}, u32[]{:S(2)}) %collective-permute-start.19) | collective-permute-done | bytes 131104 | tf_op jit(solution)/shard_map/ppermute | solution.py:170
  116.1 10.3 %all_to_all.10 = bf16[16,2,128]{2,1,0:T(2,128)(2,1)S(1)} all-to-all(bf16[16,2,128]{2,1,0:T(2,128)(2,1)S(1)} %broadcast_select_fusion), channel_id=1, replica_groups=mesh['parts'=2,'grp'=4,'ep'=4] {'grp','ep'}, dimensions={0} | all-to-all | bytes 16384 | tf_op jit(solution)/shard_map/all_to_all | solution.py:236
  (168 shorter events, 47.4 us)
Async XLA Ops:
  0.6 14.6 %collective-permute-start.3 = (bf16[128,1024]{1,0:T(8,128)(2,1)}, bf16[128,1024]{1,0:T(8,128)(2,1)S(1)}, u32[]{:S(2)}, u32[]{:S(2)}) collective-permute-start(bf16[128,1024]{1,0:T(8,128)(2,1)} %refs_0_.1), channel_id=1, source_target_pairs={{0,1},{4,5},{1,2},{5,6},{2,3},{6,7},{3,11},{7,15},{11,10},{15,14},... | collective-permute-start | bytes 786440 | tf_op jit(solution)/shard_map/ppermute | solution.py:170
  3.7 13.3 %collective-permute-start.12 = (bf16[128,1024]{1,0:T(8,128)(2,1)}, bf16[128,1024]{1,0:T(8,128)(2,1)S(1)}, u32[]{:S(2)}, u32[]{:S(2)}) collective-permute-start(bf16[128,1024]{1,0:T(8,128)(2,1)} %refs_0_.1), channel_id=1, source_target_pairs={{0,8},{4,12},{1,0},{5,4},{2,1},{6,5},{3,2},{7,6},{11,3},{15,7},{10... | collective-permute-start | bytes 786440 | tf_op jit(solution)/shard_map/ppermute | solution.py:170
  3.7 14.3 %collective-permute-start.15 = (bf16[128,1024]{1,0:T(8,128)(2,1)}, bf16[128,1024]{1,0:T(8,128)(2,1)S(1)}, u32[]{:S(2)}, u32[]{:S(2)}) collective-permute-start(bf16[128,1024]{1,0:T(8,128)(2,1)} %refs_1_.1), channel_id=1, source_target_pairs={{0,1},{4,5},{1,2},{5,6},{2,3},{6,7},{3,11},{7,15},{11,10},{15,14},... | collective-permute-start | bytes 786440 | tf_op jit(solution)/shard_map/ppermute | solution.py:170
  5.7 14.8 %collective-permute-start.7 = (bf16[128,1024]{1,0:T(8,128)(2,1)}, bf16[128,1024]{1,0:T(8,128)(2,1)S(1)}, u32[]{:S(2)}, u32[]{:S(2)}) collective-permute-start(bf16[128,1024]{1,0:T(8,128)(2,1)} %refs_1_.1), channel_id=1, source_target_pairs={{0,8},{4,12},{1,0},{5,4},{2,1},{6,5},{3,2},{7,6},{11,3},{15,7},{10... | collective-permute-start | bytes 786440 | tf_op jit(solution)/shard_map/ppermute | solution.py:170
  7.1 15.7 %all-to-all-start = ((f32[16,2,128]{2,1,0:T(2,128)}), f32[16,2,128]{2,1,0:T(2,128)S(1)}, u32[]{:S(2)}, u32[]{:S(2)}) async-start(f32[16,2,128]{2,1,0:T(2,128)} %bitcast.4), calls=%async_computation | async-start | bytes 32768 | tf_op jit(solution)/shard_map/all_to_all | solution.py:197
  13.4 26.7 %collective-permute-start = (bf16[1024,512]{1,0:T(8,128)(2,1)}, bf16[1024,512]{1,0:T(8,128)(2,1)}, u32[]{:S(2)}, u32[]{:S(2)}) collective-permute-start(bf16[1024,512]{1,0:T(8,128)(2,1)} %bitcast.60), channel_id=1, source_target_pairs={{0,4},{4,0},{1,5},{5,1},{2,6},{6,2},{3,7},{7,3},{11,15},{15,11},{1... | collective-permute-start | bytes 3145736 | tf_op jit(solution)/shard_map/ppermute | solution.py:170
  15.3 9.2 %collective-permute-start.4 = (bf16[128,1024]{1,0:T(8,128)(2,1)S(1)}, bf16[128,1024]{1,0:T(8,128)(2,1)S(1)}, u32[]{:S(2)}, u32[]{:S(2)}) collective-permute-start(bf16[128,1024]{1,0:T(8,128)(2,1)S(1)} %collective-permute-done.3.refs_0_), channel_id=1, source_target_pairs={{0,1},{4,5},{1,2},{5,6},{2,3},{6,7},{3,11},{7,15},{11,10},{15,14},... | collective-permute-start | bytes 786440 | tf_op jit(solution)/shard_map/ppermute | solution.py:170
  17.0 9.2 %collective-permute-start.13 = (bf16[128,1024]{1,0:T(8,128)(2,1)S(1)}, bf16[128,1024]{1,0:T(8,128)(2,1)S(1)}, u32[]{:S(2)}, u32[]{:S(2)}) collective-permute-start(bf16[128,1024]{1,0:T(8,128)(2,1)S(1)} %collective-permute-done.12.refs_1_), channel_id=1, source_target_pairs={{0,8},{4,12},{1,0},{5,4},{2,1},{6,5},{3,2},{7,6},{11,3},{15,7},{10... | collective-permute-start | bytes 786440 | tf_op jit(solution)/shard_map/ppermute | solution.py:170
  18.1 11.5 %collective-permute-start.16 = (bf16[128,1024]{1,0:T(8,128)(2,1)S(1)}, bf16[128,1024]{1,0:T(8,128)(2,1)S(1)}, u32[]{:S(2)}, u32[]{:S(2)}) collective-permute-start(bf16[128,1024]{1,0:T(8,128)(2,1)S(1)} %collective-permute-done.15.refs_2_), channel_id=1, source_target_pairs={{0,1},{4,5},{1,2},{5,6},{2,3},{6,7},{3,11},{7,15},{11,10},{15,14},... | collective-permute-start | bytes 786440 | tf_op jit(solution)/shard_map/ppermute | solution.py:170
  20.5 10.7 %collective-permute-start.8 = (bf16[128,1024]{1,0:T(8,128)(2,1)S(1)}, bf16[128,1024]{1,0:T(8,128)(2,1)}, u32[]{:S(2)}, u32[]{:S(2)}) collective-permute-start(bf16[128,1024]{1,0:T(8,128)(2,1)S(1)} %collective-permute-done.7.refs_3_), channel_id=1, source_target_pairs={{0,8},{4,12},{1,0},{5,4},{2,1},{6,5},{3,2},{7,6},{11,3},{15,7},{10... | collective-permute-start | bytes 786440 | tf_op jit(solution)/shard_map/ppermute | solution.py:170
  24.5 17.9 %collective-permute-start.1 = (bf16[1024,512]{1,0:T(8,128)(2,1)}, bf16[1024,512]{1,0:T(8,128)(2,1)}, u32[]{:S(2)}, u32[]{:S(2)}) collective-permute-start(bf16[1024,512]{1,0:T(8,128)(2,1)} %bitcast.66), channel_id=1, source_target_pairs={{0,4},{4,0},{1,5},{5,1},{2,6},{6,2},{3,7},{7,3},{11,15},{15,11},{1... | collective-permute-start | bytes 3145736 | tf_op jit(solution)/shard_map/ppermute | solution.py:170
  26.2 16.9 %collective-permute-start.2 = (bf16[512,1024]{1,0:T(8,128)(2,1)}, bf16[512,1024]{1,0:T(8,128)(2,1)}, u32[]{:S(2)}, u32[]{:S(2)}) collective-permute-start(bf16[512,1024]{1,0:T(8,128)(2,1)} %bitcast.72), channel_id=1, source_target_pairs={{0,4},{4,0},{1,5},{5,1},{2,6},{6,2},{3,7},{7,3},{11,15},{15,11},{1... | collective-permute-start | bytes 3145736 | tf_op jit(solution)/shard_map/ppermute | solution.py:170
  37.4 8.0 %collective-permute-start.6 = (bf16[128,1024]{1,0:T(8,128)(2,1)S(1)}, bf16[128,1024]{1,0:T(8,128)(2,1)S(1)}, u32[]{:S(2)}, u32[]{:S(2)}) collective-permute-start(bf16[128,1024]{1,0:T(8,128)(2,1)S(1)} %collective-permute-done.5.refs_0_), channel_id=1, source_target_pairs={{0,1},{4,5},{1,2},{5,6},{2,3},{6,7},{3,11},{7,15},{11,10},{15,14},... | collective-permute-start | bytes 786440 | tf_op jit(solution)/shard_map/ppermute | solution.py:170
  39.0 9.2 %collective-permute-start.10 = (bf16[128,1024]{1,0:T(8,128)(2,1)S(1)}, bf16[128,1024]{1,0:T(8,128)(2,1)S(1)}, u32[]{:S(2)}, u32[]{:S(2)}) collective-permute-start(bf16[128,1024]{1,0:T(8,128)(2,1)S(1)} %collective-permute-done.9.refs_3_), channel_id=1, source_target_pairs={{0,8},{4,12},{1,0},{5,4},{2,1},{6,5},{3,2},{7,6},{11,3},{15,7},{10... | collective-permute-start | bytes 786440 | tf_op jit(solution)/shard_map/ppermute | solution.py:170
  41.0 15.5 %collective-permute-start.14 = (bf16[128,1024]{1,0:T(8,128)(2,1)S(1)}, bf16[128,1024]{1,0:T(8,128)(2,1)S(1)}, u32[]{:S(2)}, u32[]{:S(2)}) collective-permute-start(bf16[128,1024]{1,0:T(8,128)(2,1)S(1)} %copy-done.25), channel_id=1, source_target_pairs={{0,8},{4,12},{1,0},{5,4},{2,1},{6,5},{3,2},{7,6},{11,3},{15,7},{10... | collective-permute-start | bytes 786440 | tf_op jit(solution)/shard_map/ppermute | solution.py:170
  42.4 14.1 %collective-permute-start.17 = (bf16[128,1024]{1,0:T(8,128)(2,1)}, bf16[128,1024]{1,0:T(8,128)(2,1)S(1)}, u32[]{:S(2)}, u32[]{:S(2)}) collective-permute-start(bf16[128,1024]{1,0:T(8,128)(2,1)} %copy-done.27), channel_id=1, source_target_pairs={{0,1},{4,5},{1,2},{5,6},{2,3},{6,7},{3,11},{7,15},{11,10},{15,14},... | collective-permute-start | bytes 786440 | tf_op jit(solution)/shard_map/ppermute | solution.py:170
  54.5 38.4 %collective-permute-start.11 = (bf16[128,512]{1,0:T(8,128)(2,1)}, bf16[128,512]{1,0:T(8,128)(2,1)}, u32[]{:S(2)}, u32[]{:S(2)}) collective-permute-start(bf16[128,512]{1,0:T(8,128)(2,1)} %get-tuple-element.44), channel_id=1, source_target_pairs={{0,1},{4,5},{1,2},{5,6},{2,3},{6,7},{3,11},{7,15},{11,10},{15,14},... | collective-permute-start | bytes 393224 | tf_op jit(solution)/shard_map/ppermute | solution.py:170
  55.9 37.0 %collective-permute-start.27 = (bf16[128,512]{1,0:T(8,128)(2,1)}, bf16[128,512]{1,0:T(8,128)(2,1)}, u32[]{:S(2)}, u32[]{:S(2)}) collective-permute-start(bf16[128,512]{1,0:T(8,128)(2,1)} %get-tuple-element.45), channel_id=1, source_target_pairs={{0,8},{4,12},{1,0},{5,4},{2,1},{6,5},{3,2},{7,6},{11,3},{15,7},{10... | collective-permute-start | bytes 393224 | tf_op jit(solution)/shard_map/ppermute | solution.py:170
  62.7 33.6 %collective-permute-start.24 = (bf16[128,512]{1,0:T(8,128)(2,1)}, bf16[128,512]{1,0:T(8,128)(2,1)}, u32[]{:S(2)}, u32[]{:S(2)}) collective-permute-start(bf16[128,512]{1,0:T(8,128)(2,1)} %get-tuple-element.35), channel_id=1, source_target_pairs={{0,1},{4,5},{1,2},{5,6},{2,3},{6,7},{3,11},{7,15},{11,10},{15,14},... | collective-permute-start | bytes 393224 | tf_op jit(solution)/shard_map/ppermute | solution.py:170
  64.1 32.1 %collective-permute-start.21 = (bf16[128,512]{1,0:T(8,128)(2,1)}, bf16[128,512]{1,0:T(8,128)(2,1)}, u32[]{:S(2)}, u32[]{:S(2)}) collective-permute-start(bf16[128,512]{1,0:T(8,128)(2,1)} %get-tuple-element.34), channel_id=1, source_target_pairs={{0,8},{4,12},{1,0},{5,4},{2,1},{6,5},{3,2},{7,6},{11,3},{15,7},{10... | collective-permute-start | bytes 393224 | tf_op jit(solution)/shard_map/ppermute | solution.py:170
  111.9 15.5 %collective-permute-start.23 = (bf16[128,512]{1,0:T(8,128)(2,1)S(1)}, bf16[128,512]{1,0:T(8,128)(2,1)S(1)}, u32[]{:S(2)}, u32[]{:S(2)}) collective-permute-start(bf16[128,512]{1,0:T(8,128)(2,1)S(1)} %get-tuple-element.25), channel_id=1, source_target_pairs={{0,8},{4,12},{1,0},{5,4},{2,1},{6,5},{3,2},{7,6},{11,3},{15,7},{10... | collective-permute-start | bytes 393224 | tf_op jit(solution)/shard_map/ppermute | solution.py:170
  112.5 14.9 %collective-permute-start.20 = (bf16[128,512]{1,0:T(8,128)(2,1)S(1)}, bf16[128,512]{1,0:T(8,128)(2,1)S(1)}, u32[]{:S(2)}, u32[]{:S(2)}) collective-permute-start(bf16[128,512]{1,0:T(8,128)(2,1)S(1)} %get-tuple-element.22), channel_id=1, source_target_pairs={{0,1},{4,5},{1,2},{5,6},{2,3},{6,7},{3,11},{7,15},{11,10},{15,14},... | collective-permute-start | bytes 393224 | tf_op jit(solution)/shard_map/ppermute | solution.py:170
  114.0 13.4 %collective-permute-start.30 = (bf16[128,512]{1,0:T(8,128)(2,1)S(1)}, bf16[128,512]{1,0:T(8,128)(2,1)S(1)}, u32[]{:S(2)}, u32[]{:S(2)}) collective-permute-start(bf16[128,512]{1,0:T(8,128)(2,1)S(1)} %get-tuple-element.23), channel_id=1, source_target_pairs={{0,8},{4,12},{1,0},{5,4},{2,1},{6,5},{3,2},{7,6},{11,3},{15,7},{10... | collective-permute-start | bytes 393224 | tf_op jit(solution)/shard_map/ppermute | solution.py:170
  114.6 12.9 %collective-permute-start.26 = (bf16[128,512]{1,0:T(8,128)(2,1)S(1)}, bf16[128,512]{1,0:T(8,128)(2,1)S(1)}, u32[]{:S(2)}, u32[]{:S(2)}) collective-permute-start(bf16[128,512]{1,0:T(8,128)(2,1)S(1)} %get-tuple-element.24), channel_id=1, source_target_pairs={{0,1},{4,5},{1,2},{5,6},{2,3},{6,7},{3,11},{7,15},{11,10},{15,14},... | collective-permute-start | bytes 393224 | tf_op jit(solution)/shard_map/ppermute | solution.py:170
  (39 other events, 209.0 us)

commit v2 on v1

v2 whole, which is shorter than its diff:
```python
import jax
import jax.numpy as jnp
import numpy as np
from jax import lax
from jax.experimental import pallas as pl
from jax.experimental.pallas import tpu as pltpu
from jax.sharding import PartitionSpec as P

BOTH = ("grp", "ep")
CONTRACT_LAST = (((1,), (1,)), ((), ()))


def expert_grads(rows_in, grads_in, w_gate, w_up, w_down):
    gate_pre = jnp.dot(rows_in, w_gate, preferred_element_type=jnp.float32)
    up_pre = jnp.dot(rows_in, w_up, preferred_element_type=jnp.float32)
    hidden_grad = lax.dot_general(grads_in, w_down, CONTRACT_LAST, preferred_element_type=jnp.float32)
    sigmoid_gate = 1.0 / (1.0 + jnp.exp(-gate_pre))
    activation = gate_pre * sigmoid_gate
    hidden = activation * up_pre
    weight_grad = jnp.sum(hidden_grad * hidden, axis=-1, keepdims=True)
    grad_up = (hidden_grad * activation).astype(jnp.bfloat16)
    grad_gate = (
        hidden_grad * up_pre * sigmoid_gate * (1.0 + gate_pre * (1.0 - sigmoid_gate))
    ).astype(jnp.bfloat16)
    row_terms = (
        lax.dot_general(grad_gate, w_gate, CONTRACT_LAST, preferred_element_type=jnp.float32)
        + lax.dot_general(grad_up, w_up, CONTRACT_LAST, preferred_element_type=jnp.float32)
    ).astype(jnp.bfloat16)
    return (row_terms, weight_grad)


def slot_plan(routes, experts, capacity):
    tok_rows, top_count = routes.shape
    flat_ids = routes.reshape(-1)
    pad_pair = flat_ids.shape[0]
    pair_ids = jnp.arange(pad_pair, dtype=jnp.int32)
    sort_order = jnp.argsort(flat_ids, stable=True)
    sorted_ids = flat_ids[sort_order]
    onehot = (flat_ids[:, None] == jnp.arange(experts, dtype=jnp.int32)[None, :]).astype(jnp.int32)
    counts = jnp.sum(onehot, axis=0)
    starts = jnp.cumsum(counts) - counts
    sorted_rank = pair_ids - starts[sorted_ids]
    sorted_slot = sorted_ids * capacity + sorted_rank
    slot_of_pair = jnp.zeros((pad_pair,), jnp.int32).at[sort_order].set(sorted_slot)
    slot_pair = jnp.full((experts * capacity,), pad_pair, jnp.int32).at[sorted_slot].set(sort_order)
    slot_token = jnp.where(slot_pair < pad_pair, slot_pair // top_count, tok_rows)
    return (slot_of_pair, slot_token)


def place_rows(source_rows, slot_token):
    padded = jnp.concatenate(
        [source_rows, jnp.zeros((1, source_rows.shape[1]), source_rows.dtype)], 0
    )
    return padded[slot_token]


def routed_plan(tokens, cotangent, expert_ids, route_weights, w_gate, w_up, w_down):
    group_count = lax.axis_size("grp")
    lane_count = lax.axis_size("ep")
    experts = group_count * lane_count
    tok_rows, top_count = expert_ids.shape
    model_width = tokens.shape[1]
    capacity = 2 * tok_rows * top_count // experts
    slot_of_pair, slot_token = slot_plan(expert_ids, experts, capacity)
    shape = (group_count, lane_count, capacity)

    def there_and(array, axes):
        for axis in axes:
            at = BOTH.index(axis)
            array = lax.all_to_all(array, axis, split_axis=at, concat_axis=at, tiled=True)
        return array

    rows_in = there_and(place_rows(tokens, slot_token).reshape(shape + (model_width,)), BOTH)
    grads_in = there_and(place_rows(cotangent, slot_token).reshape(shape + (model_width,)), BOTH)
    row_terms, weight_grad = expert_grads(
        rows_in.reshape(-1, model_width),
        grads_in.reshape(-1, model_width),
        w_gate[0],
        w_up[0],
        w_down[0],
    )
    row_terms = there_and(row_terms.reshape(shape + (model_width,)), BOTH[::-1])
    weight_grad = there_and(weight_grad.astype(jnp.bfloat16).reshape(shape), BOTH[::-1])
    row_terms = row_terms.reshape(experts * capacity, model_width)
    weight_grad = weight_grad.reshape(experts * capacity)
    picked = row_terms[slot_of_pair].reshape(tok_rows, top_count, model_width)
    grad_tokens = jnp.sum(route_weights[:, :, None] * picked.astype(jnp.float32), axis=1)
    grad_weights = weight_grad[slot_of_pair].reshape(tok_rows, top_count)
    return (grad_tokens.astype(jnp.bfloat16), grad_weights)


def after(array, *others):
    return lax.optimization_barrier((array,) + others)[0]


def spread_experts(column, row_of, extra):
    rows = column.shape[0]
    across = lax.broadcasted_iota(jnp.int32, (rows, rows), 1)
    down = lax.broadcasted_iota(jnp.int32, (rows, rows), 0)
    line = jnp.sum(jnp.where(across == down, column, 0.0), axis=0, keepdims=True)
    return jnp.where(lax.broadcasted_iota(jnp.int32, (extra, rows), 0) == row_of, line, 0.0)


def grads_kernel(blocks, rows, extra, *refs):
    place_ref, refs = refs[0], refs[1:]
    token_refs, refs = refs[:blocks], refs[blocks:]
    grad_refs, refs = refs[:blocks], refs[blocks:]
    share_refs, refs = refs[:blocks], refs[blocks:]
    weights, outs = (refs[:3], refs[3:6]), refs[6:]
    rows_in = jnp.concatenate([ref[...] for ref in token_refs], 0)
    grads_in = jnp.concatenate([ref[...] for ref in grad_refs], 0)
    shares = jnp.concatenate([ref[...] for ref in share_refs], 0)
    total, spread = None, [None] * blocks
    for at, (gate, up, down) in enumerate(weights):
        row_terms, weight_grad = expert_grads(rows_in, grads_in, gate[...], up[...], down[...])
        scaled = shares[:, at : at + 1] * row_terms.astype(jnp.float32)
        total = scaled if total is None else total + scaled
        for i in range(blocks):
            lines = spread_experts(weight_grad[i * rows : (i + 1) * rows], place_ref[at], extra)
            spread[i] = lines if at == 0 else spread[i] + lines
    half = total.shape[1] // 2
    for i in range(blocks):
        left, right = outs[2 * i], outs[2 * i + 1]
        block = total[i * rows : (i + 1) * rows]
        left[:rows, :] = block[:, :half].astype(left.dtype)
        left[rows:, :] = jnp.zeros((extra, half), left.dtype)
        left[rows:, :rows] = spread[i].astype(jnp.bfloat16).astype(left.dtype)
        right[...] = block[:, half:].astype(right.dtype)


def block_grads(places, blocks_in, weights, extra, kinds):
    tokens, grads, shares = zip(*blocks_in)
    blocks = len(tokens)
    rows, width = tokens[0].shape
    hidden = weights[0].shape[1]
    outs = []
    for left, right in kinds:
        outs.append(jax.ShapeDtypeStruct((rows + extra, width // 2), left))
        outs.append(jax.ShapeDtypeStruct((rows, width // 2), right))
    vmem = pl.BlockSpec(memory_space=pltpu.VMEM)
    out = pl.pallas_call(
        lambda *refs: grads_kernel(blocks, rows, extra, *refs),
        in_specs=[pl.BlockSpec(memory_space=pltpu.SMEM)] + [vmem] * (3 * blocks + 6),
        out_shape=outs,
        compiler_params=pltpu.CompilerParams(vmem_limit_bytes=24 << 20),
        cost_estimate=pl.CostEstimate(
            flops=2 * 10 * blocks * rows * width * hidden,
            bytes_accessed=12 * width * hidden + 8 * blocks * rows * width,
            transcendentals=2 * blocks * rows * hidden,
        ),
    )(places, *tokens, *grads, *shares, *weights)
    return [(out[2 * i], out[2 * i + 1]) for i in range(blocks)]


def add_kernel(*refs):
    count = len(refs) // 3
    for i in range(count):
        came, own, out = refs[2 * i], refs[2 * i + 1], refs[2 * count + i]
        out[...] = (came[...].astype(jnp.float32) + own[...]).astype(out.dtype)


def add_pairs(*pairs):
    operands = [array for pair in pairs for array in pair]
    return pl.pallas_call(
        add_kernel,
        out_shape=[jax.ShapeDtypeStruct(came.shape, came.dtype) for came, own in pairs],
        compiler_params=pltpu.CompilerParams(vmem_limit_bytes=8 << 20),
    )(*operands)


def finish_kernel(left_own, right_own, left_a, left_b, right_a, right_b, ids, tokens_out, weights_out):
    rows, half = right_own.shape
    extra = left_own.shape[0] - rows
    as_f32 = lambda ref: ref[...].astype(jnp.float32)
    left = left_own[...] + as_f32(left_a) + as_f32(left_b)
    tokens_out[:, :half] = left[:rows].astype(tokens_out.dtype)
    tokens_out[:, half:] = (right_own[...] + as_f32(right_a) + as_f32(right_b)).astype(tokens_out.dtype)
    grads = left[rows:, :rows]
    by_token = jnp.concatenate([grads, jnp.zeros((rows - extra, rows), jnp.float32)], 0).T
    lanes = lax.broadcasted_iota(jnp.int32, (rows, rows), 1)
    for k in range(ids.shape[1]):
        picked = jnp.where(lanes == ids[:, k : k + 1], by_token, 0.0)
        weights_out[:, k : k + 1] = jnp.sum(picked, axis=1, keepdims=True).astype(weights_out.dtype)


def ring_order(chips_x, lanes):
    order = []
    for x in range(chips_x):
        column = [(x, z) for z in range(lanes)]
        order += column if x % 2 == 0 else column[::-1]
    return order


def ring_plan(tokens, cotangent, expert_ids, route_weights, w_gate, w_up, w_down):
    group_count = lax.axis_size("grp")
    lanes = lax.axis_size("ep")
    devices = group_count * lanes
    rows, top_count = expert_ids.shape
    order = ring_order(group_count // 2, lanes)
    chips = len(order)
    far = chips // 2
    extra = -(-devices // 16) * 16

    def device(place, core):
        x, z = order[place % chips]
        return (2 * x + core) * lanes + z

    source_table = np.zeros((devices, chips), np.int32)
    other_table = np.zeros((devices,), np.int32)
    for place in range(chips):
        for core in range(2):
            source_table[device(place, core)] = [device(place - o, core) for o in range(chips)]
            other_table[device(place, core)] = device(place, 1 - core)
    ahead = [(device(p, c), device(p + 1, c)) for p in range(chips) for c in range(2)]
    behind = [(device(p, c), device(p - 1, c)) for p in range(chips) for c in range(2)]
    across = [(device(p, c), device(p, 1 - c)) for p in range(chips) for c in range(2)]

    def send(array, pairs):
        return lax.ppermute(array, BOTH, pairs)

    me = lax.axis_index("grp") * lanes + lax.axis_index("ep")
    places = jnp.stack([me, jnp.asarray(other_table)[me]])

    token_up, token_down = send(tokens, ahead), send(tokens, behind)
    expert_list = jnp.arange(devices, dtype=jnp.int32)
    chosen = expert_ids[None, :, :] == expert_list[:, None, None]
    dense = jnp.sum(jnp.where(chosen, route_weights[None], 0.0), axis=-1)
    later = after(cotangent, dense)
    grad_up, grad_down = send(later, ahead), send(later, behind)
    mine = (w_gate[0], w_up[0], w_down[0])
    weights = mine + tuple(send(w, across) for w in mine)

    shares = lax.all_gather(dense, BOTH)[jnp.asarray(source_table)[me]]
    shares = jnp.take(shares, places, axis=1).transpose(0, 2, 1)

    sums = {}

    def compute(blocks):
        kinds = []
        for o, *unused in blocks:
            left = jnp.bfloat16 if o in (far, far - 1) else jnp.float32
            right = jnp.bfloat16 if o in (far, chips - far + 1) else jnp.float32
            kinds.append((left, right))
        out = block_grads(places, [(t, g, shares[o]) for o, t, g in blocks], weights, extra, kinds)
        for (o, *unused), pair in zip(blocks, out):
            sums[o] = pair

    compute([(0, tokens, cotangent)])
    got = [(1, token_up, grad_up), (chips - 1, token_down, grad_down)]
    for step in range(2, far):
        if step > 2:
            token_up = after(token_up, sums[step - 2][0])
            token_down = after(token_down, sums[step - 2][0])
        token_up, token_down = send(token_up, ahead), send(token_down, behind)
        grad_up, grad_down = send(grad_up, ahead), send(grad_down, behind)
        compute(got)
        got = [(step, token_up, grad_up), (chips - step, token_down, grad_down)]
    token_up = after(token_up, sums[far - 2][0])
    grad_down = after(grad_down, sums[far - 2][0])
    token_up, grad_down = send(token_up, ahead), send(grad_down, behind)
    compute(got)

    right_up, left_down = sums[chips - far + 1][1], sums[far - 1][0]
    right_up, left_down = send(right_up, ahead), send(left_down, behind)
    compute([(far, token_up, grad_down)])
    left_up, right_down = sums[far]
    for step in range(far, 0, -1):
        left_up, right_down = send(left_up, ahead), send(right_down, behind)
        if step > 2:
            right_up, left_down = add_pairs((right_up, sums[chips - step + 2][1]), (left_down, sums[step - 2][0]))
            right_up, left_down = send(right_up, ahead), send(left_down, behind)
        if step > 1:
            left_up, right_down = add_pairs((left_up, sums[chips - step + 1][0]), (right_down, sums[step - 1][1]))

    return pl.pallas_call(
        finish_kernel,
        out_shape=[
            jax.ShapeDtypeStruct(tokens.shape, tokens.dtype),
            jax.ShapeDtypeStruct(expert_ids.shape, jnp.bfloat16),
        ],
        compiler_params=pltpu.CompilerParams(vmem_limit_bytes=8 << 20),
    )(*sums[0], left_up, left_down, right_up, right_down, expert_ids)


def on_device(tokens, cotangent, expert_ids, route_weights, w_gate, w_up, w_down):
    group_count = lax.axis_size("grp")
    experts = group_count * lax.axis_size("ep")
    rows, top_count = expert_ids.shape
    capacity = 2 * rows * top_count // experts
    fits = rows % 128 == 0 and experts <= rows <= tokens.shape[1] // 2 and group_count % 2 == 0 and experts >= 8
    plan = ring_plan if fits and 2 * capacity >= rows else routed_plan
    return plan(tokens, cotangent, expert_ids, route_weights, w_gate, w_up, w_down)


def solution(mesh):
    in_specs = (
        P(("parts", "grp", "ep"), None),
        P(("parts", "grp", "ep"), None),
        P(("parts", "grp", "ep"), None),
        P(("parts", "grp", "ep"), None),
        P(("grp", "ep"), None, None),
        P(("grp", "ep"), None, None),
        P(("grp", "ep"), None, None),
    )
    out_specs = (P(("parts", "grp", "ep"), None), P(("parts", "grp", "ep"), None))
    return jax.shard_map(
        on_device, mesh=mesh, in_specs=in_specs, out_specs=out_specs, check_vma=False
    )
```

time: 129 us -> 133 us (1.031)
  blocking collectives: 10.3 us -> 34.7 us
  local copies, waits for them, and re-layouts: 20.2 us -> 11.4 us
  starting transfers between devices: 37.4 us -> 30.3 us
  other arithmetic: 9.09 us -> 3.03 us
  Pallas kernels: 24.9 us -> 26.7 us
    all_gather x0 -> x1, blocking collectives: none -> 34.7 us  [ring_plan(): shares = lax.all_gather(dense, BOTH)[jnp.asarray(source_table)[me]]]
    all_to_all x1 -> x0, blocking collectives: 10.3 us -> none  [ring_plan(): lax.all_to_all(outgoing, BOTH, split_axis=0, concat_axis=0, tiled=True)]
    unnamed x71 -> x27, local copies, waits for them, and re-layouts: 13 us -> 5.99 us
    all_to_all x1 -> x0, starting transfers between devices: 6.36 us -> none  [ring_plan(): dense = lax.all_to_all(dense, BOTH, split_axis=0, concat_axis=0, tiled=True)]
    another operation x12 -> x0, local copies, waits for them, and re-layouts: 2.77 us -> none  [ring_plan(): jnp.stack([weight_grads[o] for o in range(chips)] + [jnp.zeros((rows, 2),...]
    convert_element_type x3 -> x0, other arithmetic: 2.55 us -> none  [chain(): (moving.astype(jnp.float32) + sums[o][:, columns]).astype(jnp.bfloat16)]
    pallas_call x5 -> x11, Pallas kernels: 24.9 us -> 26.7 us  [the longest x5 22.6 us: block_grads(): pl.pallas_call(lambda *refs: grads_kernel(blocks, rows, extra, *refs), in...]
    slice x2 -> x0, local copies, waits for them, and re-layouts: 1.49 us -> none  [chain(): moving = sums[offsets[0]][:, columns].astype(jnp.bfloat16)]
  transfers between devices with their start and end apart: 32 -> 31, of which waited for: 12 -> 7; matrix products, arithmetic and copies ran while one was open for 11% -> 5% of each run, Pallas kernels for 19% -> 18%
where the time goes in v2:
time: 133 us; the launch traced here: 132 us
  blocking collectives  34.7 us (26%)
  starting transfers between devices  30.3 us (23%)
  Pallas kernels  26.7 us (20%)
  waiting for transfers between devices  25.1 us (19%)
  local copies, waits for them, and re-layouts  11.4 us (9%)
  other arithmetic  3.03 us (2%)
    all_gather x1, blocking collectives, ring_plan(): shares = lax.all_gather(dense, BOTH)[jnp.asarray(source_table)[me]]  34.7 us
    ppermute x31, starting transfers between devices, send(): return lax.ppermute(array, BOTH, pairs)  30.3 us
    ppermute x31, waiting for transfers between devices, send(): return lax.ppermute(array, BOTH, pairs)  25.1 us
    pallas_call x5, Pallas kernels, block_grads(): pl.pallas_call(lambda *refs: grads_kernel(blocks, rows, extra, *refs), in...  22.6 us
    unnamed x27, local copies, waits for them, and re-layouts  5.99 us
  transfers between devices with their start and end apart: 31, of which 7 were waited for; matrix products, arithmetic and copies ran while one was open for 5% of the time, Pallas kernels for 18%

profile of v2, /device:TPU:0, one launch (start us, length us, event | category | flops | bytes accessed | tf_op | source)
XLA Modules:
  0.0 132.1 jit_solution(1419411668555700921)
XLA Ops:
  1.5 3.1 %collective-permute-start.6 = (bf16[128,1024]{1,0:T(8,128)(2,1)}, bf16[128,1024]{1,0:T(8,128)(2,1)S(1)}, u32[]{:S(2)}, u32[]{:S(2)}) collective-permute-start(bf16[128,1024]{1,0:T(8,128)(2,1)} %refs_2_.1), channel_id=1, source_target_pairs={{0,1},{4,5},{1,2},{5,6},{2,3},{6,7},{3,11},{7,15},{11,10},{15,14},... | collective-permute-start | bytes 786440 | tf_op jit(solution)/shard_map/ppermute | solution.py:219
  7.1 3.9 %collective-permute-done.6.refs_3_ = bf16[128,1024]{1,0:T(8,128)(2,1)S(1)} collective-permute-done((bf16[128,1024]{1,0:T(8,128)(2,1)}, bf16[128,1024]{1,0:T(8,128)(2,1)S(1)}, u32[]{:S(2)}, u32[]{:S(2)}) %collective-permute-start.6) | collective-permute-done | bytes 262176 | tf_op jit(solution)/shard_map/ppermute | solution.py:219
  11.0 1.8 %collective-permute-start.3 = (bf16[128,1024]{1,0:T(8,128)(2,1)}, bf16[128,1024]{1,0:T(8,128)(2,1)}, u32[]{:S(2)}, u32[]{:S(2)}) collective-permute-start(bf16[128,1024]{1,0:T(8,128)(2,1)} %refs_1_.1), channel_id=1, source_target_pairs={{0,1},{4,5},{1,2},{5,6},{2,3},{6,7},{3,11},{7,15},{11,10},{15,14},... | collective-permute-start | bytes 786440 | tf_op jit(solution)/shard_map/ppermute | solution.py:219
  13.8 34.7 %all-gather = f32[256,128]{1,0:T(8,128)} all-gather(f32[16,128]{1,0:T(8,128)S(1)} %select_reduce_fusion), channel_id=2, replica_groups=mesh['parts'=2,'grp'=4,'ep'=4] {'grp','ep'}, dimensions={0}, use_global_device_ids=true | all-gather | bytes 139264 | tf_op jit(solution)/shard_map/all_gather | solution.py:233
  50.5 2.0 %collective-permute-start.11 = (bf16[128,1024]{1,0:T(8,128)(2,1)}, bf16[128,1024]{1,0:T(8,128)(2,1)}, u32[]{:S(2)}, u32[]{:S(2)}) collective-permute-start(bf16[128,1024]{1,0:T(8,128)(2,1)} %collective-permute-done.7.refs_4_), channel_id=1, source_target_pairs={{0,8},{4,12},{1,0},{5,4},{2,1},{6,5},{3,2},{7,6},{11,3},{15,7},{10... | collective-permute-start | bytes 786440 | tf_op jit(solution)/shard_map/ppermute | solution.py:219
  54.8 3.2 %collective-permute-done.11.refs_4_ = bf16[128,1024]{1,0:T(8,128)(2,1)} collective-permute-done((bf16[128,1024]{1,0:T(8,128)(2,1)}, bf16[128,1024]{1,0:T(8,128)(2,1)}, u32[]{:S(2)}, u32[]{:S(2)}) %collective-permute-start.11) | collective-permute-done | bytes 262176 | tf_op jit(solution)/shard_map/ppermute | solution.py:219
  58.0 1.9 %collective-permute-start.9 = (bf16[128,1024]{1,0:T(8,128)(2,1)}, bf16[128,1024]{1,0:T(8,128)(2,1)S(1)}, u32[]{:S(2)}, u32[]{:S(2)}) collective-permute-start(bf16[128,1024]{1,0:T(8,128)(2,1)} %collective-permute-done.5.refs_2_), channel_id=1, source_target_pairs={{0,8},{4,12},{1,0},{5,4},{2,1},{6,5},{3,2},{7,6},{11,3},{15,7},{10... | collective-permute-start | bytes 786440 | tf_op jit(solution)/shard_map/ppermute | solution.py:219
  60.0 1.9 %collective-permute-start.13 = (bf16[128,1024]{1,0:T(8,128)(2,1)}, bf16[128,1024]{1,0:T(8,128)(2,1)S(1)}, u32[]{:S(2)}, u32[]{:S(2)}) collective-permute-start(bf16[128,1024]{1,0:T(8,128)(2,1)} %collective-permute-done.11.refs_4_), channel_id=1, source_target_pairs={{0,8},{4,12},{1,0},{5,4},{2,1},{6,5},{3,2},{7,6},{11,3},{15,7},{10... | collective-permute-start | bytes 786440 | tf_op jit(solution)/shard_map/ppermute | solution.py:219
  64.4 4.9 %shard_map.105 = (f32[144,512]{1,0:T(8,128)S(1)}, f32[128,512]{1,0:T(8,128)S(1)}, f32[144,512]{1,0:T(8,128)S(1)}, f32[128,512]{1,0:T(8,128)S(1)}) custom-call(s32[2]{0:T(128)S(1)} %get-tuple-element.75.refs_0_, bf16[128,1024]{1,0:T(8,128)(2,1)} %collective-permute-done.3.refs_1_, bf16[128,1024]{1,0:T(8,128)(2,1)} %collective-permute-done.5.refs_2_, ...), custom_call_target="tpu_custom_call" | custom-call | flops 2684354560 | bytes 8388608 | tf_op jit(solution)/shard_map/pallas_call | solution.py:141
  69.5 4.7 %shard_map.106 = (f32[144,512]{1,0:T(8,128)S(1)}, f32[128,512]{1,0:T(8,128)S(1)}, f32[144,512]{1,0:T(8,128)S(1)}, f32[128,512]{1,0:T(8,128)S(1)}) custom-call(s32[2]{0:T(128)S(1)} %get-tuple-element.75.refs_0_, bf16[128,1024]{1,0:T(8,128)(2,1)S(1)} %collective-permute-done.4.refs_1_, bf16[128,1024]{1,0:T(8,128)(2,1)S(1)} %collective-permute-done.9.refs_2_, ...), custom_call_target="tpu_custom_call" | custom-call | flops 2684354560 | bytes 8388608 | tf_op jit(solution)/shard_map/pallas_call | solution.py:141
  74.2 1.9 %collective-permute-start.14 = (bf16[128,1024]{1,0:T(8,128)(2,1)S(1)}, bf16[128,1024]{1,0:T(8,128)(2,1)S(1)}, u32[]{:S(2)}, u32[]{:S(2)}) collective-permute-start(bf16[128,1024]{1,0:T(8,128)(2,1)S(1)} %collective-permute-done.13.refs_4_), channel_id=1, source_target_pairs={{0,8},{4,12},{1,0},{5,4},{2,1},{6,5},{3,2},{7,6},{11,3},{15,7},{10... | collective-permute-start | bytes 786440 | tf_op jit(solution)/shard_map/ppermute | solution.py:219
  76.1 2.2 %collective-permute-done.8.refs_1_ = bf16[128,1024]{1,0:T(8,128)(2,1)S(1)} collective-permute-done((bf16[128,1024]{1,0:T(8,128)(2,1)S(1)}, bf16[128,1024]{1,0:T(8,128)(2,1)S(1)}, u32[]{:S(2)}, u32[]{:S(2)}) %collective-permute-start.8) | collective-permute-done | bytes 262176 | tf_op jit(solution)/shard_map/ppermute | solution.py:219
  78.3 2.1 %collective-permute-start.16 = (bf16[128,1024]{1,0:T(8,128)(2,1)S(1)}, bf16[128,1024]{1,0:T(8,128)(2,1)S(1)}, u32[]{:S(2)}, u32[]{:S(2)}) collective-permute-start(bf16[128,1024]{1,0:T(8,128)(2,1)S(1)} %collective-permute-done.9.refs_2_), channel_id=1, source_target_pairs={{0,8},{4,12},{1,0},{5,4},{2,1},{6,5},{3,2},{7,6},{11,3},{15,7},{10... | collective-permute-start | bytes 786440 | tf_op jit(solution)/shard_map/ppermute | solution.py:219
  80.4 1.6 %collective-permute-done.14.refs_2_ = bf16[128,1024]{1,0:T(8,128)(2,1)S(1)} collective-permute-done((bf16[128,1024]{1,0:T(8,128)(2,1)S(1)}, bf16[128,1024]{1,0:T(8,128)(2,1)S(1)}, u32[]{:S(2)}, u32[]{:S(2)}) %collective-permute-start.14) | collective-permute-done | bytes 262176 | tf_op jit(solution)/shard_map/ppermute | solution.py:219
  82.0 2.7 %collective-permute-done.12.refs_1_ = bf16[128,1024]{1,0:T(8,128)(2,1)S(1)} collective-permute-done((bf16[128,1024]{1,0:T(8,128)(2,1)S(1)}, bf16[128,1024]{1,0:T(8,128)(2,1)S(1)}, u32[]{:S(2)}, u32[]{:S(2)}) %collective-permute-start.12) | collective-permute-done | bytes 262176 | tf_op jit(solution)/shard_map/ppermute | solution.py:219
  84.7 4.2 %shard_map.107 = (bf16[144,512]{1,0:T(8,128)(2,1)S(1)}, bf16[128,512]{1,0:T(8,128)(2,1)S(1)}) custom-call(s32[2]{0:T(128)S(1)} %get-tuple-element.75.refs_0_, bf16[128,1024]{1,0:T(8,128)(2,1)S(1)} %collective-permute-done.12.refs_1_, bf16[128,1024]{1,0:T(8,128)(2,1)S(1)} %collective-permute-done.14.refs_2_, f32[128,2]{1,0:T(8,128)S(1)} %get-tuple-element.78.refs_3_, ...), custom_call_target="tpu_custom_call" | custom-call | flops 1342177280 | bytes 7340032 | tf_op jit(solution)/shard_map/pallas_call | solution.py:141
  89.0 2.0 %collective-permute-start.18 = (bf16[128,512]{1,0:T(8,128)(2,1)S(1)}, bf16[128,512]{1,0:T(8,128)(2,1)S(1)}, u32[]{:S(2)}, u32[]{:S(2)}) collective-permute-start(bf16[128,512]{1,0:T(8,128)(2,1)S(1)} %get-tuple-element.44), channel_id=1, source_target_pairs={{0,8},{4,12},{1,0},{5,4},{2,1},{6,5},{3,2},{7,6},{11,3},{15,7},{10... | collective-permute-start | bytes 393224 | tf_op jit(solution)/shard_map/ppermute | solution.py:219
  91.0 4.6 %shard_map.108 = (bf16[144,512]{1,0:T(8,128)(2,1)S(1)}, f32[128,512]{1,0:T(8,128)S(1)}, f32[144,512]{1,0:T(8,128)S(1)}, bf16[128,512]{1,0:T(8,128)(2,1)S(1)}) custom-call(s32[2]{0:T(128)S(1)} %get-tuple-element.75.refs_0_, bf16[128,1024]{1,0:T(8,128)(2,1)S(1)} %collective-permute-done.8.refs_1_, bf16[128,1024]{1,0:T(8,128)(2,1)S(1)} %collective-permute-done.16.refs_2_, ...), custom_call_target="tpu_custom_call" | custom-call | flops 2684354560 | bytes 8388608 | tf_op jit(solution)/shard_map/pallas_call | solution.py:141
  95.8 2.0 %collective-permute-start.19 = (bf16[144,512]{1,0:T(8,128)(2,1)S(1)}, bf16[144,512]{1,0:T(8,128)(2,1)S(1)}, u32[]{:S(2)}, u32[]{:S(2)}) collective-permute-start(bf16[144,512]{1,0:T(8,128)(2,1)S(1)} %get-tuple-element.46), channel_id=1, source_target_pairs={{0,1},{4,5},{1,2},{5,6},{2,3},{6,7},{3,11},{7,15},{11,10},{15,14},... | collective-permute-start | bytes 442376 | tf_op jit(solution)/shard_map/ppermute | solution.py:219
  98.1 1.8 %collective-permute-start.20 = (bf16[128,512]{1,0:T(8,128)(2,1)S(1)}, bf16[128,512]{1,0:T(8,128)(2,1)S(1)}, u32[]{:S(2)}, u32[]{:S(2)}) collective-permute-start(bf16[128,512]{1,0:T(8,128)(2,1)S(1)} %get-tuple-element.48), channel_id=1, source_target_pairs={{0,8},{4,12},{1,0},{5,4},{2,1},{6,5},{3,2},{7,6},{11,3},{15,7},{10... | collective-permute-start | bytes 393224 | tf_op jit(solution)/shard_map/ppermute | solution.py:219
  99.9 5.4 %collective-permute-done.24.refs_0_ = bf16[128,512]{1,0:T(8,128)(2,1)S(1)} collective-permute-done((bf16[128,512]{1,0:T(8,128)(2,1)S(1)}, bf16[128,512]{1,0:T(8,128)(2,1)S(1)}, u32[]{:S(2)}, u32[]{:S(2)}) %collective-permute-start.24) | collective-permute-done | bytes 131104 | tf_op jit(solution)/shard_map/ppermute | solution.py:219
  109.5 6.1 %collective-permute-done.26.refs_0_ = bf16[128,512]{1,0:T(8,128)(2,1)S(1)} collective-permute-done((bf16[128,512]{1,0:T(8,128)(2,1)S(1)}, bf16[128,512]{1,0:T(8,128)(2,1)S(1)}, u32[]{:S(2)}, u32[]{:S(2)}) %collective-permute-start.26) | collective-permute-done | bytes 131104 | tf_op jit(solution)/shard_map/ppermute | solution.py:219
  124.7 4.2 %shard_map.104 = (f32[144,512]{1,0:T(8,128)S(1)}, f32[128,512]{1,0:T(8,128)S(1)}) custom-call(s32[2]{0:T(128)S(1)} %get-tuple-element.75.refs_0_, bf16[128,1024]{1,0:T(8,128)(2,1)S(1)} %copy-done.9, bf16[128,1024]{1,0:T(8,128)(2,1)S(1)} %copy-done.10, f32[128,2]{1,0:T(8,128)S(1)} %get-tuple-element.83.refs_3_, bf16[1024,512]{1,0:T(8,128)(2,1)S(1)} %bitcast.35, ...), custom_call_target="tpu_custom_call" | custom-call | flops 1342177280 | bytes 7340032 | tf_op jit(solution)/shard_map/pallas_call | solution.py:141
  128.9 2.5 %shard_map.114 = (bf16[128,1024]{1,0:T(8,128)(2,1)}, bf16[128,5]{1,0:T(8,128)(2,1)S(1)}) custom-call(f32[144,512]{1,0:T(8,128)S(1)} %get-tuple-element.33.left_own, f32[128,512]{1,0:T(8,128)S(1)} %get-tuple-element.34.right_own, bf16[144,512]{1,0:T(8,128)(2,1)} %collective-permute-done.23.left_a, bf16[144,512]{1,0:T(8,128)(2,1)} %collective-permute-done.28.left_b, ...), custom_call_target="tpu_custom_call" | custom-call | tf_op jit(solution)/shard_map/pallas_call | solution.py:275
  (91 shorter events, 25.8 us)
Async XLA Ops:
  1.5 9.5 %collective-permute-start.6 = (bf16[128,1024]{1,0:T(8,128)(2,1)}, bf16[128,1024]{1,0:T(8,128)(2,1)S(1)}, u32[]{:S(2)}, u32[]{:S(2)}) collective-permute-start(bf16[128,1024]{1,0:T(8,128)(2,1)} %refs_2_.1), channel_id=1, source_target_pairs={{0,1},{4,5},{1,2},{5,6},{2,3},{6,7},{3,11},{7,15},{11,10},{15,14},... | collective-permute-start | bytes 786440 | tf_op jit(solution)/shard_map/ppermute | solution.py:219
  4.5 9.0 %collective-permute-start.7 = (bf16[128,1024]{1,0:T(8,128)(2,1)}, bf16[128,1024]{1,0:T(8,128)(2,1)}, u32[]{:S(2)}, u32[]{:S(2)}) collective-permute-start(bf16[128,1024]{1,0:T(8,128)(2,1)} %refs_2_.1), channel_id=1, source_target_pairs={{0,8},{4,12},{1,0},{5,4},{2,1},{6,5},{3,2},{7,6},{11,3},{15,7},{10... | collective-permute-start | bytes 786440 | tf_op jit(solution)/shard_map/ppermute | solution.py:219
  4.5 55.3 %collective-permute-start = (bf16[1024,512]{1,0:T(8,128)(2,1)}, bf16[1024,512]{1,0:T(8,128)(2,1)S(1)}, u32[]{:S(2)}, u32[]{:S(2)}) collective-permute-start(bf16[1024,512]{1,0:T(8,128)(2,1)} %bitcast.30), channel_id=1, source_target_pairs={{0,4},{4,0},{1,5},{5,1},{2,6},{6,2},{3,7},{7,3},{11,15},{15,11},{1... | collective-permute-start | bytes 3145736 | tf_op jit(solution)/shard_map/ppermute | solution.py:219
  4.5 55.5 %collective-permute-start.1 = (bf16[1024,512]{1,0:T(8,128)(2,1)}, bf16[1024,512]{1,0:T(8,128)(2,1)S(1)}, u32[]{:S(2)}, u32[]{:S(2)}) collective-permute-start(bf16[1024,512]{1,0:T(8,128)(2,1)} %bitcast.36), channel_id=1, source_target_pairs={{0,4},{4,0},{1,5},{5,1},{2,6},{6,2},{3,7},{7,3},{11,15},{15,11},{1... | collective-permute-start | bytes 3145736 | tf_op jit(solution)/shard_map/ppermute | solution.py:219
  5.0 56.9 %collective-permute-start.2 = (bf16[512,1024]{1,0:T(8,128)(2,1)}, bf16[512,1024]{1,0:T(8,128)(2,1)}, u32[]{:S(2)}, u32[]{:S(2)}) collective-permute-start(bf16[512,1024]{1,0:T(8,128)(2,1)} %bitcast.42), channel_id=1, source_target_pairs={{0,4},{4,0},{1,5},{5,1},{2,6},{6,2},{3,7},{7,3},{11,15},{15,11},{1... | collective-permute-start | bytes 3145736 | tf_op jit(solution)/shard_map/ppermute | solution.py:219
  11.0 39.5 %collective-permute-start.3 = (bf16[128,1024]{1,0:T(8,128)(2,1)}, bf16[128,1024]{1,0:T(8,128)(2,1)}, u32[]{:S(2)}, u32[]{:S(2)}) collective-permute-start(bf16[128,1024]{1,0:T(8,128)(2,1)} %refs_1_.1), channel_id=1, source_target_pairs={{0,1},{4,5},{1,2},{5,6},{2,3},{6,7},{3,11},{7,15},{11,10},{15,14},... | collective-permute-start | bytes 786440 | tf_op jit(solution)/shard_map/ppermute | solution.py:219
  13.5 40.2 %collective-permute-start.5 = (bf16[128,1024]{1,0:T(8,128)(2,1)}, bf16[128,1024]{1,0:T(8,128)(2,1)}, u32[]{:S(2)}, u32[]{:S(2)}) collective-permute-start(bf16[128,1024]{1,0:T(8,128)(2,1)} %refs_1_.1), channel_id=1, source_target_pairs={{0,8},{4,12},{1,0},{5,4},{2,1},{6,5},{3,2},{7,6},{11,3},{15,7},{10... | collective-permute-start | bytes 786440 | tf_op jit(solution)/shard_map/ppermute | solution.py:219
  53.7 15.6 %collective-permute-start.4 = (bf16[128,1024]{1,0:T(8,128)(2,1)}, bf16[128,1024]{1,0:T(8,128)(2,1)S(1)}, u32[]{:S(2)}, u32[]{:S(2)}) collective-permute-start(bf16[128,1024]{1,0:T(8,128)(2,1)} %collective-permute-done.3.refs_1_), channel_id=1, source_target_pairs={{0,1},{4,5},{1,2},{5,6},{2,3},{6,7},{3,11},{7,15},{11,10},{15,14},... | collective-permute-start | bytes 786440 | tf_op jit(solution)/shard_map/ppermute | solution.py:219
  58.0 11.5 %collective-permute-start.9 = (bf16[128,1024]{1,0:T(8,128)(2,1)}, bf16[128,1024]{1,0:T(8,128)(2,1)S(1)}, u32[]{:S(2)}, u32[]{:S(2)}) collective-permute-start(bf16[128,1024]{1,0:T(8,128)(2,1)} %collective-permute-done.5.refs_2_), channel_id=1, source_target_pairs={{0,8},{4,12},{1,0},{5,4},{2,1},{6,5},{3,2},{7,6},{11,3},{15,7},{10... | collective-permute-start | bytes 786440 | tf_op jit(solution)/shard_map/ppermute | solution.py:219
  59.9 9.6 %collective-permute-start.10 = (bf16[128,1024]{1,0:T(8,128)(2,1)S(1)}, bf16[128,1024]{1,0:T(8,128)(2,1)S(1)}, u32[]{:S(2)}, u32[]{:S(2)}) collective-permute-start(bf16[128,1024]{1,0:T(8,128)(2,1)S(1)} %collective-permute-done.6.refs_3_), channel_id=1, source_target_pairs={{0,1},{4,5},{1,2},{5,6},{2,3},{6,7},{3,11},{7,15},{11,10},{15,14},... | collective-permute-start | bytes 786440 | tf_op jit(solution)/shard_map/ppermute | solution.py:219
  60.0 14.2 %collective-permute-start.13 = (bf16[128,1024]{1,0:T(8,128)(2,1)}, bf16[128,1024]{1,0:T(8,128)(2,1)S(1)}, u32[]{:S(2)}, u32[]{:S(2)}) collective-permute-start(bf16[128,1024]{1,0:T(8,128)(2,1)} %collective-permute-done.11.refs_4_), channel_id=1, source_target_pairs={{0,8},{4,12},{1,0},{5,4},{2,1},{6,5},{3,2},{7,6},{11,3},{15,7},{10... | collective-permute-start | bytes 786440 | tf_op jit(solution)/shard_map/ppermute | solution.py:219
  69.3 9.1 %collective-permute-start.8 = (bf16[128,1024]{1,0:T(8,128)(2,1)S(1)}, bf16[128,1024]{1,0:T(8,128)(2,1)S(1)}, u32[]{:S(2)}, u32[]{:S(2)}) collective-permute-start(bf16[128,1024]{1,0:T(8,128)(2,1)S(1)} %collective-permute-done.4.refs_1_), channel_id=1, source_target_pairs={{0,1},{4,5},{1,2},{5,6},{2,3},{6,7},{3,11},{7,15},{11,10},{15,14},... | collective-permute-start | bytes 786440 | tf_op jit(solution)/shard_map/ppermute | solution.py:219
  78.3 12.7 %collective-permute-start.17 = (bf16[128,1024]{1,0:T(8,128)(2,1)S(1)}, bf16[128,1024]{1,0:T(8,128)(2,1)S(1)}, u32[]{:S(2)}, u32[]{:S(2)}) collective-permute-start(bf16[128,1024]{1,0:T(8,128)(2,1)S(1)} %collective-permute-done.10.refs_3_), channel_id=1, source_target_pairs={{0,1},{4,5},{1,2},{5,6},{2,3},{6,7},{3,11},{7,15},{11,10},{15,14},... | collective-permute-start | bytes 786440 | tf_op jit(solution)/shard_map/ppermute | solution.py:219
  78.3 12.7 %collective-permute-start.16 = (bf16[128,1024]{1,0:T(8,128)(2,1)S(1)}, bf16[128,1024]{1,0:T(8,128)(2,1)S(1)}, u32[]{:S(2)}, u32[]{:S(2)}) collective-permute-start(bf16[128,1024]{1,0:T(8,128)(2,1)S(1)} %collective-permute-done.9.refs_2_), channel_id=1, source_target_pairs={{0,8},{4,12},{1,0},{5,4},{2,1},{6,5},{3,2},{7,6},{11,3},{15,7},{10... | collective-permute-start | bytes 786440 | tf_op jit(solution)/shard_map/ppermute | solution.py:219
  95.6 9.6 %collective-permute-start.25 = (bf16[144,512]{1,0:T(8,128)(2,1)S(1)}, bf16[144,512]{1,0:T(8,128)(2,1)S(1)}, u32[]{:S(2)}, u32[]{:S(2)}) collective-permute-start(bf16[144,512]{1,0:T(8,128)(2,1)S(1)} %get-tuple-element.57), channel_id=1, source_target_pairs={{0,8},{4,12},{1,0},{5,4},{2,1},{6,5},{3,2},{7,6},{11,3},{15,7},{10... | collective-permute-start | bytes 442376 | tf_op jit(solution)/shard_map/ppermute | solution.py:219
  95.8 10.2 %collective-permute-start.19 = (bf16[144,512]{1,0:T(8,128)(2,1)S(1)}, bf16[144,512]{1,0:T(8,128)(2,1)S(1)}, u32[]{:S(2)}, u32[]{:S(2)}) collective-permute-start(bf16[144,512]{1,0:T(8,128)(2,1)S(1)} %get-tuple-element.46), channel_id=1, source_target_pairs={{0,1},{4,5},{1,2},{5,6},{2,3},{6,7},{3,11},{7,15},{11,10},{15,14},... | collective-permute-start | bytes 442376 | tf_op jit(solution)/shard_map/ppermute | solution.py:219
  105.3 10.3 %collective-permute-start.27 = (bf16[144,512]{1,0:T(8,128)(2,1)S(1)}, bf16[144,512]{1,0:T(8,128)(2,1)S(1)}, u32[]{:S(2)}, u32[]{:S(2)}) collective-permute-start(bf16[144,512]{1,0:T(8,128)(2,1)S(1)} %get-tuple-element.60), channel_id=1, source_target_pairs={{0,8},{4,12},{1,0},{5,4},{2,1},{6,5},{3,2},{7,6},{11,3},{15,7},{10... | collective-permute-start | bytes 442376 | tf_op jit(solution)/shard_map/ppermute | solution.py:219
  106.0 11.4 %collective-permute-start.21 = (bf16[144,512]{1,0:T(8,128)(2,1)S(1)}, bf16[144,512]{1,0:T(8,128)(2,1)S(1)}, u32[]{:S(2)}, u32[]{:S(2)}) collective-permute-start(bf16[144,512]{1,0:T(8,128)(2,1)S(1)} %get-tuple-element.50), channel_id=1, source_target_pairs={{0,1},{4,5},{1,2},{5,6},{2,3},{6,7},{3,11},{7,15},{11,10},{15,14},... | collective-permute-start | bytes 442376 | tf_op jit(solution)/shard_map/ppermute | solution.py:219
  107.5 8.1 %collective-permute-start.26 = (bf16[128,512]{1,0:T(8,128)(2,1)S(1)}, bf16[128,512]{1,0:T(8,128)(2,1)S(1)}, u32[]{:S(2)}, u32[]{:S(2)}) collective-permute-start(bf16[128,512]{1,0:T(8,128)(2,1)S(1)} %get-tuple-element.58), channel_id=1, source_target_pairs={{0,1},{4,5},{1,2},{5,6},{2,3},{6,7},{3,11},{7,15},{11,10},{15,14},... | collective-permute-start | bytes 393224 | tf_op jit(solution)/shard_map/ppermute | solution.py:219
  109.0 8.4 %collective-permute-start.22 = (bf16[128,512]{1,0:T(8,128)(2,1)S(1)}, bf16[128,512]{1,0:T(8,128)(2,1)S(1)}, u32[]{:S(2)}, u32[]{:S(2)}) collective-permute-start(bf16[128,512]{1,0:T(8,128)(2,1)S(1)} %get-tuple-element.52), channel_id=1, source_target_pairs={{0,8},{4,12},{1,0},{5,4},{2,1},{6,5},{3,2},{7,6},{11,3},{15,7},{10... | collective-permute-start | bytes 393224 | tf_op jit(solution)/shard_map/ppermute | solution.py:219
  116.3 12.6 %collective-permute-start.28 = (bf16[144,512]{1,0:T(8,128)(2,1)}, bf16[144,512]{1,0:T(8,128)(2,1)}, u32[]{:S(2)}, u32[]{:S(2)}) collective-permute-start(bf16[144,512]{1,0:T(8,128)(2,1)} %get-tuple-element.61), channel_id=1, source_target_pairs={{0,8},{4,12},{1,0},{5,4},{2,1},{6,5},{3,2},{7,6},{11,3},{15,7},{10... | collective-permute-start | bytes 442376 | tf_op jit(solution)/shard_map/ppermute | solution.py:219
  118.2 10.7 %collective-permute-start.23 = (bf16[144,512]{1,0:T(8,128)(2,1)}, bf16[144,512]{1,0:T(8,128)(2,1)}, u32[]{:S(2)}, u32[]{:S(2)}) collective-permute-start(bf16[144,512]{1,0:T(8,128)(2,1)} %get-tuple-element.54), channel_id=1, source_target_pairs={{0,1},{4,5},{1,2},{5,6},{2,3},{6,7},{3,11},{7,15},{11,10},{15,14},... | collective-permute-start | bytes 442376 | tf_op jit(solution)/shard_map/ppermute | solution.py:219
  119.1 9.8 %collective-permute-start.29 = (bf16[128,512]{1,0:T(8,128)(2,1)}, bf16[128,512]{1,0:T(8,128)(2,1)}, u32[]{:S(2)}, u32[]{:S(2)}) collective-permute-start(bf16[128,512]{1,0:T(8,128)(2,1)} %get-tuple-element.62), channel_id=1, source_target_pairs={{0,1},{4,5},{1,2},{5,6},{2,3},{6,7},{3,11},{7,15},{11,10},{15,14},... | collective-permute-start | bytes 393224 | tf_op jit(solution)/shard_map/ppermute | solution.py:219
  120.2 8.7 %collective-permute-start.30 = (bf16[128,512]{1,0:T(8,128)(2,1)}, bf16[128,512]{1,0:T(8,128)(2,1)}, u32[]{:S(2)}, u32[]{:S(2)}) collective-permute-start(bf16[128,512]{1,0:T(8,128)(2,1)} %get-tuple-element.63), channel_id=1, source_target_pairs={{0,8},{4,12},{1,0},{5,4},{2,1},{6,5},{3,2},{7,6},{11,3},{15,7},{10... | collective-permute-start | bytes 393224 | tf_op jit(solution)/shard_map/ppermute | solution.py:219
  (20 other events, 221.4 us)

commit v3 on v2

--- a/solution.py
+++ b/solution.py
@@ -1,12 +1,12 @@
 import jax
 import jax.numpy as jnp
-import numpy as np
 from jax import lax
 from jax.experimental import pallas as pl
 from jax.experimental.pallas import tpu as pltpu
 from jax.sharding import PartitionSpec as P
 
 BOTH = ("grp", "ep")
+LIGHT = pl.CostEstimate(flops=0, transcendentals=0, bytes_accessed=0)
 CONTRACT_LAST = (((1,), (1,)), ((), ()))
 
 
@@ -14,6 +14,17 @@
     gate_pre = jnp.dot(rows_in, w_gate, preferred_element_type=jnp.float32)
     up_pre = jnp.dot(rows_in, w_up, preferred_element_type=jnp.float32)
     hidden_grad = lax.dot_general(grads_in, w_down, CONTRACT_LAST, preferred_element_type=jnp.float32)
+    grad_gate, grad_up, weight_grad = hidden_grads(gate_pre, up_pre, hidden_grad)
+    return (both_terms(grad_gate, grad_up, w_gate, w_up), weight_grad)
+
+
+def both_terms(grad_gate, grad_up, w_gate, w_up):
+    row_terms = lax.dot_general(grad_gate, w_gate, CONTRACT_LAST, preferred_element_type=jnp.float32)
+    row_terms += lax.dot_general(grad_up, w_up, CONTRACT_LAST, preferred_element_type=jnp.float32)
+    return row_terms.astype(jnp.bfloat16)
+
+
+def hidden_grads(gate_pre, up_pre, hidden_grad):
     sigmoid_gate = 1.0 / (1.0 + jnp.exp(-gate_pre))
     activation = gate_pre * sigmoid_gate
     hidden = activation * up_pre
@@ -22,11 +33,7 @@
     grad_gate = (
         hidden_grad * up_pre * sigmoid_gate * (1.0 + gate_pre * (1.0 - sigmoid_gate))
     ).astype(jnp.bfloat16)
-    row_terms = (
-        lax.dot_general(grad_gate, w_gate, CONTRACT_LAST, preferred_element_type=jnp.float32)
-        + lax.dot_general(grad_up, w_up, CONTRACT_LAST, preferred_element_type=jnp.float32)
-    ).astype(jnp.bfloat16)
-    return (row_terms, weight_grad)
+    return (grad_gate, grad_up, weight_grad)
 
 
 def slot_plan(routes, experts, capacity):
@@ -89,8 +96,8 @@
     return (grad_tokens.astype(jnp.bfloat16), grad_weights)
 
 
-def after(array, *others):
-    return lax.optimization_barrier((array,) + others)[0]
+def after_all(*arrays):
+    return lax.optimization_barrier(arrays)
 
 
 def spread_experts(column, row_of, extra):
@@ -101,22 +108,92 @@
     return jnp.where(lax.broadcasted_iota(jnp.int32, (extra, rows), 0) == row_of, line, 0.0)
 
 
-def grads_kernel(blocks, rows, extra, *refs):
+def bf16_pieces(values):
+    pieces = []
+    for unused in range(3):
+        piece = values.astype(jnp.bfloat16)
+        values = values - piece.astype(jnp.float32)
+        pieces.append(piece)
+    return pieces
+
+
+def read_share(lines, expert, experts, rows):
+    pieces = lines.astype(jnp.float32)
+    groups = pieces.shape[1] // rows
+    slot = lax.broadcasted_iota(jnp.int32, pieces.shape, 0) * groups
+    slot = slot + lax.broadcasted_iota(jnp.int32, pieces.shape, 1) // rows
+    wanted = (slot == expert) | (slot == expert + experts) | (slot == expert + 2 * experts)
+    kept = jnp.where(wanted, pieces, 0.0)
+    line = sum(kept[:, g * rows : (g + 1) * rows] for g in range(groups))
+    line = jnp.sum(line, axis=0, keepdims=True)
+    across = lax.broadcasted_iota(jnp.int32, (rows, rows), 1)
+    down = lax.broadcasted_iota(jnp.int32, (rows, rows), 0)
+    return jnp.sum(jnp.where(across == down, line, 0.0), axis=1, keepdims=True)
+
+
+def merge_kernel(gate, up, down, out):
+    hidden = gate.shape[1]
+    out[:, :hidden] = gate[...]
+    out[:, hidden : 2 * hidden] = up[...]
+    out[:, 2 * hidden :] = down[...].T
+
+
+def merge_weights(w_gate, w_up, w_down):
+    return pl.pallas_call(
+        merge_kernel,
+        out_shape=pltpu.HBM((w_gate.shape[0], 3 * w_gate.shape[1]), w_gate.dtype),
+        compiler_params=pltpu.CompilerParams(vmem_limit_bytes=24 << 20),
+        cost_estimate=LIGHT,
+    )(w_gate, w_up, w_down)
+
+
+def hold_kernel(count, pieces, *refs):
+    sources, held, sems = refs[:count], refs[count : 2 * count], refs[-1]
+    copies = []
+    for at in range(count):
+        rows = sources[at].shape[0] // pieces
+        for i in range(pieces):
+            part = pl.ds(i * rows, rows)
+            copies.append(pltpu.make_async_copy(sources[at].at[part], held[at].at[part], sems.at[at, i]))
+    for copy in copies:
+        copy.start()
+    for copy in copies:
+        copy.wait()
+
+
+def hold(*arrays, pieces=4):
+    return pl.pallas_call(
+        lambda *refs: hold_kernel(len(arrays), pieces, *refs),
+        in_specs=[pl.BlockSpec(memory_space=pl.ANY)] * len(arrays),
+        out_shape=[pltpu.VMEM(array.shape, array.dtype) for array in arrays],
+        scratch_shapes=[pltpu.SemaphoreType.DMA((len(arrays), pieces))],
+        compiler_params=pltpu.CompilerParams(vmem_limit_bytes=24 << 20),
+        cost_estimate=LIGHT,
+    )(*arrays)
+
+
+def grads_kernel(blocks, rows, experts, extra, *refs):
     place_ref, refs = refs[0], refs[1:]
-    token_refs, refs = refs[:blocks], refs[blocks:]
-    grad_refs, refs = refs[:blocks], refs[blocks:]
-    share_refs, refs = refs[:blocks], refs[blocks:]
-    weights, outs = (refs[:3], refs[3:6]), refs[6:]
+    token_refs, grad_refs, refs = refs[:blocks], refs[blocks : 2 * blocks], refs[2 * blocks :]
+    weights, outs = refs[:2], refs[2:]
+    places = [jnp.max(place_ref[:, at : at + 1]) for at in range(2)]
     rows_in = jnp.concatenate([ref[...] for ref in token_refs], 0)
-    grads_in = jnp.concatenate([ref[...] for ref in grad_refs], 0)
-    shares = jnp.concatenate([ref[...] for ref in share_refs], 0)
+    with_lines = [ref[...] for ref in grad_refs]
+    grads_in = jnp.concatenate([block[:rows] for block in with_lines], 0)
     total, spread = None, [None] * blocks
-    for at, (gate, up, down) in enumerate(weights):
-        row_terms, weight_grad = expert_grads(rows_in, grads_in, gate[...], up[...], down[...])
-        scaled = shares[:, at : at + 1] * row_terms.astype(jnp.float32)
+    for at, merged in enumerate(weights):
+        hidden = merged.shape[1] // 3
+        w_gate, w_up, w_down = (merged[:, i * hidden : (i + 1) * hidden] for i in range(3))
+        gate_pre = jnp.dot(rows_in, w_gate, preferred_element_type=jnp.float32)
+        up_pre = jnp.dot(rows_in, w_up, preferred_element_type=jnp.float32)
+        hidden_grad = jnp.dot(grads_in, w_down, preferred_element_type=jnp.float32)
+        grad_gate, grad_up, weight_grad = hidden_grads(gate_pre, up_pre, hidden_grad)
+        row_terms = both_terms(grad_gate, grad_up, w_gate, w_up)
+        shares = [read_share(block[rows:], places[at], experts, rows) for block in with_lines]
+        scaled = jnp.concatenate(shares, 0) * row_terms.astype(jnp.float32)
         total = scaled if total is None else total + scaled
         for i in range(blocks):
-            lines = spread_experts(weight_grad[i * rows : (i + 1) * rows], place_ref[at], extra)
+            lines = spread_experts(weight_grad[i * rows : (i + 1) * rows], places[at], extra)
             spread[i] = lines if at == 0 else spread[i] + lines
     half = total.shape[1] // 2
     for i in range(blocks):
@@ -128,27 +205,21 @@
         right[...] = block[:, half:].astype(right.dtype)
 
 
-def block_grads(places, blocks_in, weights, extra, kinds):
-    tokens, grads, shares = zip(*blocks_in)
+def block_grads(places, blocks_in, weights, experts, extra, kinds):
+    tokens, grads = zip(*blocks_in)
     blocks = len(tokens)
     rows, width = tokens[0].shape
-    hidden = weights[0].shape[1]
     outs = []
     for left, right in kinds:
         outs.append(jax.ShapeDtypeStruct((rows + extra, width // 2), left))
         outs.append(jax.ShapeDtypeStruct((rows, width // 2), right))
-    vmem = pl.BlockSpec(memory_space=pltpu.VMEM)
+    weights = [pltpu.with_memory_space_constraint(w, pltpu.VMEM) for w in weights]
     out = pl.pallas_call(
-        lambda *refs: grads_kernel(blocks, rows, extra, *refs),
-        in_specs=[pl.BlockSpec(memory_space=pltpu.SMEM)] + [vmem] * (3 * blocks + 6),
+        lambda *refs: grads_kernel(blocks, rows, experts, extra, *refs),
         out_shape=outs,
         compiler_params=pltpu.CompilerParams(vmem_limit_bytes=24 << 20),
-        cost_estimate=pl.CostEstimate(
-            flops=2 * 10 * blocks * rows * width * hidden,
-            bytes_accessed=12 * width * hidden + 8 * blocks * rows * width,
-            transcendentals=2 * blocks * rows * hidden,
-        ),
-    )(places, *tokens, *grads, *shares, *weights)
+        cost_estimate=LIGHT,
+    )(places, *tokens, *grads, *weights)
     return [(out[2 * i], out[2 * i + 1]) for i in range(blocks)]
 
 
@@ -165,6 +236,7 @@
         add_kernel,
         out_shape=[jax.ShapeDtypeStruct(came.shape, came.dtype) for came, own in pairs],
         compiler_params=pltpu.CompilerParams(vmem_limit_bytes=8 << 20),
+        cost_estimate=LIGHT,
     )(*operands)
 
 
@@ -195,7 +267,7 @@
     group_count = lax.axis_size("grp")
     lanes = lax.axis_size("ep")
     devices = group_count * lanes
-    rows, top_count = expert_ids.shape
+    rows, width = tokens.shape
     order = ring_order(group_count // 2, lanes)
     chips = len(order)
     far = chips // 2
@@ -205,12 +277,6 @@
         x, z = order[place % chips]
         return (2 * x + core) * lanes + z
 
-    source_table = np.zeros((devices, chips), np.int32)
-    other_table = np.zeros((devices,), np.int32)
-    for place in range(chips):
-        for core in range(2):
-            source_table[device(place, core)] = [device(place - o, core) for o in range(chips)]
-            other_table[device(place, core)] = device(place, 1 - core)
     ahead = [(device(p, c), device(p + 1, c)) for p in range(chips) for c in range(2)]
     behind = [(device(p, c), device(p - 1, c)) for p in range(chips) for c in range(2)]
     across = [(device(p, c), device(p, 1 - c)) for p in range(chips) for c in range(2)]
@@ -219,19 +285,21 @@
         return lax.ppermute(array, BOTH, pairs)
 
     me = lax.axis_index("grp") * lanes + lax.axis_index("ep")
-    places = jnp.stack([me, jnp.asarray(other_table)[me]])
+    other = jnp.where(lax.rem(lax.axis_index("grp"), 2) == 0, me + lanes, me - lanes)
+    places = jnp.stack([me, other]).reshape(1, 2)
 
     token_up, token_down = send(tokens, ahead), send(tokens, behind)
     expert_list = jnp.arange(devices, dtype=jnp.int32)
     chosen = expert_ids[None, :, :] == expert_list[:, None, None]
     dense = jnp.sum(jnp.where(chosen, route_weights[None], 0.0), axis=-1)
-    later = after(cotangent, dense)
-    grad_up, grad_down = send(later, ahead), send(later, behind)
-    mine = (w_gate[0], w_up[0], w_down[0])
-    weights = mine + tuple(send(w, across) for w in mine)
-
-    shares = lax.all_gather(dense, BOTH)[jnp.asarray(source_table)[me]]
-    shares = jnp.take(shares, places, axis=1).transpose(0, 2, 1)
+    lines = jnp.concatenate(bf16_pieces(dense), 0)
+    line_rows = -(-3 * devices * rows // (8 * width)) * 8
+    lines = jnp.pad(lines, ((0, line_rows * width // rows - 3 * devices), (0, 0))).reshape(line_rows, width)
+    cotangent = jnp.concatenate([cotangent, lines], 0)
+    grad_up, grad_down = send(cotangent, ahead), send(cotangent, behind)
+    mine = merge_weights(w_gate[0], w_up[0], w_down[0])
+    mine = after_all(mine, token_up, token_down, grad_up, grad_down)[0]
+    weights = hold(mine, send(mine, across))
 
     sums = {}
 
@@ -241,36 +309,39 @@
             left = jnp.bfloat16 if o in (far, far - 1) else jnp.float32
             right = jnp.bfloat16 if o in (far, chips - far + 1) else jnp.float32
             kinds.append((left, right))
-        out = block_grads(places, [(t, g, shares[o]) for o, t, g in blocks], weights, extra, kinds)
+        out = block_grads(places, [(t, g) for o, t, g in blocks], weights, devices, extra, kinds)
         for (o, *unused), pair in zip(blocks, out):
             sums[o] = pair
-
-    compute([(0, tokens, cotangent)])
-    got = [(1, token_up, grad_up), (chips - 1, token_down, grad_down)]
+        return out[0][0]
+
+    arrived = [[(0, tokens, cotangent)], [(1, token_up, grad_up), (chips - 1, token_down, grad_down)]]
     for step in range(2, far):
-        if step > 2:
-            token_up = after(token_up, sums[step - 2][0])
-            token_down = after(token_down, sums[step - 2][0])
+        if step == far - 1:
+            token_up, token_down = after_all(token_up, token_down, weights[0])[:2]
+            grad_up, grad_down = after_all(grad_up, grad_down, compute(arrived[0]))[:2]
         token_up, token_down = send(token_up, ahead), send(token_down, behind)
         grad_up, grad_down = send(grad_up, ahead), send(grad_down, behind)
-        compute(got)
-        got = [(step, token_up, grad_up), (chips - step, token_down, grad_down)]
-    token_up = after(token_up, sums[far - 2][0])
-    grad_down = after(grad_down, sums[far - 2][0])
+        arrived.append([(step, token_up, grad_up), (chips - step, token_down, grad_down)])
+    token_up = after_all(token_up, compute(arrived[far - 2]))[0]
     token_up, grad_down = send(token_up, ahead), send(grad_down, behind)
-    compute(got)
-
-    right_up, left_down = sums[chips - far + 1][1], sums[far - 1][0]
-    right_up, left_down = send(right_up, ahead), send(left_down, behind)
+    last = compute(arrived[far - 1])
+
+    right_up, left_down = send(sums[chips - far + 1][1], ahead), send(sums[far - 1][0], behind)
+    token_up = after_all(token_up, last)[0]
     compute([(far, token_up, grad_down)])
-    left_up, right_down = sums[far]
+    for o in range(far - 3, 0, -1):
+        compute(arrived[o])
+    left_up, right_down = after_all(*sums[far], right_up, left_down)[:2]
     for step in range(far, 0, -1):
         left_up, right_down = send(left_up, ahead), send(right_down, behind)
         if step > 2:
             right_up, left_down = add_pairs((right_up, sums[chips - step + 2][1]), (left_down, sums[step - 2][0]))
+            turn = right_up
             right_up, left_down = send(right_up, ahead), send(left_down, behind)
         if step > 1:
+            left_up, right_down = after_all(left_up, right_down, turn)[:2]
             left_up, right_down = add_pairs((left_up, sums[chips - step + 1][0]), (right_down, sums[step - 1][1]))
+            right_up, left_down = after_all(right_up, left_down, left_up)[:2]
 
     return pl.pallas_call(
         finish_kernel,
@@ -287,7 +358,7 @@
     experts = group_count * lax.axis_size("ep")
     rows, top_count = expert_ids.shape
     capacity = 2 * rows * top_count // experts
-    fits = rows % 128 == 0 and experts <= rows <= tokens.shape[1] // 2 and group_count % 2 == 0 and experts >= 8
+    fits = rows % 128 == 0 and experts <= rows <= tokens.shape[1] // 2 and group_count % 2 == 0 and experts >= 8 and tokens.shape[1] % rows == 0
     plan = ring_plan if fits and 2 * capacity >= rows else routed_plan
     return plan(tokens, cotangent, expert_ids, route_weights, w_gate, w_up, w_down)
 

time: 133 us -> 92.8 us (0.70)
  blocking collectives: 34.7 us -> 0 us
  waiting for transfers between devices: 25.1 us -> 32 us
  Pallas kernels: 26.7 us -> 22 us
  local copies, waits for them, and re-layouts: 11.4 us -> 7.77 us
  other arithmetic: 3.03 us -> 0.8 us
    all_gather x1 -> x0, blocking collectives: 34.7 us -> none  [ring_plan(): shares = lax.all_gather(dense, BOTH)[jnp.asarray(source_table)[me]]]
    ppermute x31 -> x29, waiting for transfers between devices: 25.1 us -> 32 us  [send(): return lax.ppermute(array, BOTH, pairs)]
    pallas_call x5 -> x7, Pallas kernels: 22.6 us -> 20.3 us  [the longest x5 17.7 us: block_grads(): pl.pallas_call(lambda *refs: grads_kernel(blocks, rows, experts, extra, *...]
    gather x3 -> x0, local copies, waits for them, and re-layouts: 2.03 us -> none  [the longest x2 1.48 us: ring_plan(): shares = lax.all_gather(dense, BOTH)[jnp.asarray(source_table)[me]]]
    select_n x3 -> x0, other arithmetic: 1.48 us -> none  [the longest x2 0.79 us: ring_plan(): shares = jnp.take(shares, places, axis=1).transpose(0, 2, 1)]
    ppermute x31 -> x29, starting transfers between devices: 30.3 us -> 29 us  [send(): return lax.ppermute(array, BOTH, pairs)]
    unnamed x27 -> x14, local copies, waits for them, and re-layouts: 5.99 us -> 7.08 us
  transfers between devices with their start and end apart: 31 -> 29, of which waited for: 7 -> 15; matrix products, arithmetic and copies ran while one was open for 5% -> 0% of each run, Pallas kernels for 18% -> 22%
where the time goes in v3:
time: 92.8 us; the launch traced here: 92.4 us
  waiting for transfers between devices  32 us (34%)
  starting transfers between devices  29 us (31%)
  Pallas kernels  22 us (24%)
  local copies, waits for them, and re-layouts  7.77 us (8%)
    ppermute x29, waiting for transfers between devices, send(): return lax.ppermute(array, BOTH, pairs)  32 us
    ppermute x29, starting transfers between devices, send(): return lax.ppermute(array, BOTH, pairs)  29 us
    pallas_call x5, Pallas kernels, block_grads(): pl.pallas_call(lambda *refs: grads_kernel(blocks, rows, experts, extra, *...  17.7 us
    unnamed x14, local copies, waits for them, and re-layouts  7.08 us
    pallas_call x1, Pallas kernels, merge_weights(): pl.pallas_call(merge_kernel, out_shape=pltpu.HBM((w_gate.shape[0], 3 * w_...  2.07 us
  transfers between devices with their start and end apart: 29, of which 15 were waited for; matrix products, arithmetic and copies ran while one was open for 0% of the time, Pallas kernels for 22%

profile of v3, /device:TPU:0, one launch (start us, length us, event | category | flops | bytes accessed | tf_op | source)
XLA Modules:
  0.0 92.4 jit_solution(15431726903346755250)
XLA Ops:
  2.4 3.1 %collective-permute-start.2 = (bf16[136,1024]{1,0:T(8,128)(2,1)S(1)}, bf16[136,1024]{1,0:T(8,128)(2,1)}, u32[]{:S(2)}, u32[]{:S(2)}) collective-permute-start(bf16[136,1024]{1,0:T(8,128)(2,1)S(1)} %constant_dynamic-update-slice_fusion.refs_2_), channel_id=1, source_target_pairs={{0,1},{4,5},{1,2},{5,6},{2,3},{6,7},{3,11},{7,15},{11,10},{15,14},... | collective-permute-start | bytes 835592 | tf_op jit(solution)/shard_map/ppermute | solution.py:285
  5.4 2.0 %collective-permute-start = (bf16[128,1024]{1,0:T(8,128)(2,1)}, bf16[128,1024]{1,0:T(8,128)(2,1)}, u32[]{:S(2)}, u32[]{:S(2)}) collective-permute-start(bf16[128,1024]{1,0:T(8,128)(2,1)} %refs_1_.1), channel_id=1, source_target_pairs={{0,1},{4,5},{1,2},{5,6},{2,3},{6,7},{3,11},{7,15},{11,10},{15,14},... | collective-permute-start | bytes 786440 | tf_op jit(solution)/shard_map/ppermute | solution.py:285
  11.2 2.1 %shard_map.86.refs_0_ = bf16[1024,1536]{1,0:T(8,128)(2,1)} custom-call(bf16[1024,512]{1,0:T(8,128)(2,1)S(1)} %bitcast.7, bf16[1024,512]{1,0:T(8,128)(2,1)S(1)} %bitcast.8, bf16[512,1024]{1,0:T(8,128)(2,1)S(1)} %bitcast.9), custom_call_target="tpu_custom_call" | custom-call | tf_op jit(solution)/shard_map/pallas_call | solution.py:142
  13.2 4.5 %collective-permute-done.refs_1_ = bf16[128,1024]{1,0:T(8,128)(2,1)} collective-permute-done((bf16[128,1024]{1,0:T(8,128)(2,1)}, bf16[128,1024]{1,0:T(8,128)(2,1)}, u32[]{:S(2)}, u32[]{:S(2)}) %collective-permute-start) | collective-permute-done | bytes 262176 | tf_op jit(solution)/shard_map/ppermute | solution.py:285
  19.3 1.6 %collective-permute-start.8 = (bf16[136,1024]{1,0:T(8,128)(2,1)}, bf16[136,1024]{1,0:T(8,128)(2,1)}, u32[]{:S(2)}, u32[]{:S(2)}) collective-permute-start(bf16[136,1024]{1,0:T(8,128)(2,1)} %collective-permute-done.2.refs_3_), channel_id=1, source_target_pairs={{0,1},{4,5},{1,2},{5,6},{2,3},{6,7},{3,11},{7,15},{11,10},{15,14},... | collective-permute-start | bytes 835592 | tf_op jit(solution)/shard_map/ppermute | solution.py:285
  21.4 1.6 %collective-permute-start.5 = (bf16[128,1024]{1,0:T(8,128)(2,1)}, bf16[128,1024]{1,0:T(8,128)(2,1)}, u32[]{:S(2)}, u32[]{:S(2)}) collective-permute-start(bf16[128,1024]{1,0:T(8,128)(2,1)} %collective-permute-done.refs_1_), channel_id=1, source_target_pairs={{0,1},{4,5},{1,2},{5,6},{2,3},{6,7},{3,11},{7,15},{11,10},{15,14},... | collective-permute-start | bytes 786440 | tf_op jit(solution)/shard_map/ppermute | solution.py:285
  23.5 1.7 %collective-permute-done.4.refs_1_ = bf16[1024,1536]{1,0:T(8,128)(2,1)S(1)} collective-permute-done((bf16[1024,1536]{1,0:T(8,128)(2,1)}, bf16[1024,1536]{1,0:T(8,128)(2,1)S(1)}, u32[]{:S(2)}, u32[]{:S(2)}) %collective-permute-start.4) | collective-permute-done | bytes 3145760 | tf_op jit(solution)/shard_map/ppermute | solution.py:285
  25.2 1.9 %copy-done = bf16[1024,1536]{1,0:T(8,128)(2,1)S(1)} copy-done((bf16[1024,1536]{1,0:T(8,128)(2,1)S(1)}, bf16[1024,1536]{1,0:T(8,128)(2,1)}, u32[]{:S(2)}) %copy-start) | copy-done | bytes 3145752
  28.0 2.6 %shard_map.88 = (f32[144,512]{1,0:T(8,128)S(1)}, f32[128,512]{1,0:T(8,128)S(1)}) custom-call(s32[1,2]{1,0:T(1,128)S(1)} %add_bitcast_fusion.refs_0_, bf16[128,1024]{1,0:T(8,128)(2,1)S(1)} %copy-done.4, bf16[136,1024]{1,0:T(8,128)(2,1)S(1)} %constant_dynamic-update-slice_fusion.refs_2_, bf16[1024,1536]{1,0:T(8,128)(2,1)S(1)} %get-tuple-element.52.refs_3_.refs_5_, ...), custom_call_target="tpu_custom_call" | custom-call | tf_op jit(solution)/shard_map/pallas_call | solution.py:217
  31.2 3.1 %collective-permute-done.5.refs_1_ = bf16[128,1024]{1,0:T(8,128)(2,1)} collective-permute-done((bf16[128,1024]{1,0:T(8,128)(2,1)}, bf16[128,1024]{1,0:T(8,128)(2,1)}, u32[]{:S(2)}, u32[]{:S(2)}) %collective-permute-start.5) | collective-permute-done | bytes 262176 | tf_op jit(solution)/shard_map/ppermute | solution.py:285
  34.3 2.1 %collective-permute-done.6.refs_2_ = bf16[128,1024]{1,0:T(8,128)(2,1)} collective-permute-done((bf16[128,1024]{1,0:T(8,128)(2,1)}, bf16[128,1024]{1,0:T(8,128)(2,1)}, u32[]{:S(2)}, u32[]{:S(2)}) %collective-permute-start.6) | collective-permute-done | bytes 262176 | tf_op jit(solution)/shard_map/ppermute | solution.py:285
  36.4 1.6 %collective-permute-start.7 = (bf16[128,1024]{1,0:T(8,128)(2,1)}, bf16[128,1024]{1,0:T(8,128)(2,1)S(1)}, u32[]{:S(2)}, u32[]{:S(2)}) collective-permute-start(bf16[128,1024]{1,0:T(8,128)(2,1)} %collective-permute-done.5.refs_1_), channel_id=1, source_target_pairs={{0,1},{4,5},{1,2},{5,6},{2,3},{6,7},{3,11},{7,15},{11,10},{15,14},... | collective-permute-start | bytes 786440 | tf_op jit(solution)/shard_map/ppermute | solution.py:285
  40.0 2.3 %collective-permute-done.13.refs_4_ = bf16[136,1024]{1,0:T(8,128)(2,1)S(1)} collective-permute-done((bf16[136,1024]{1,0:T(8,128)(2,1)}, bf16[136,1024]{1,0:T(8,128)(2,1)S(1)}, u32[]{:S(2)}, u32[]{:S(2)}) %collective-permute-start.13) | collective-permute-done | bytes 278560 | tf_op jit(solution)/shard_map/ppermute | solution.py:285
  42.7 4.6 %shard_map.89 = (f32[144,512]{1,0:T(8,128)S(1)}, f32[128,512]{1,0:T(8,128)S(1)}, f32[144,512]{1,0:T(8,128)S(1)}, f32[128,512]{1,0:T(8,128)S(1)}) custom-call(s32[1,2]{1,0:T(1,128)S(1)} %add_bitcast_fusion.refs_0_, bf16[128,1024]{1,0:T(8,128)(2,1)} %collective-permute-done.5.refs_1_, bf16[128,1024]{1,0:T(8,128)(2,1)} %collective-permute-done.6.refs_2_, ...), custom_call_target="tpu_custom_call" | custom-call | tf_op jit(solution)/shard_map/pallas_call | solution.py:217
  47.3 1.6 %collective-permute-start.10 = (bf16[128,1024]{1,0:T(8,128)(2,1)S(1)}, bf16[128,1024]{1,0:T(8,128)(2,1)S(1)}, u32[]{:S(2)}, u32[]{:S(2)}) collective-permute-start(bf16[128,1024]{1,0:T(8,128)(2,1)S(1)} %collective-permute-done.7.refs_1_), channel_id=1, source_target_pairs={{0,1},{4,5},{1,2},{5,6},{2,3},{6,7},{3,11},{7,15},{11,10},{15,14},... | collective-permute-start | bytes 786440 | tf_op jit(solution)/shard_map/ppermute | solution.py:285
  50.4 3.4 %shard_map.90 = (bf16[144,512]{1,0:T(8,128)(2,1)S(1)}, f32[128,512]{1,0:T(8,128)S(1)}, f32[144,512]{1,0:T(8,128)S(1)}, bf16[128,512]{1,0:T(8,128)(2,1)S(1)}) custom-call(s32[1,2]{1,0:T(1,128)S(1)} %add_bitcast_fusion.refs_0_, bf16[128,1024]{1,0:T(8,128)(2,1)S(1)} %collective-permute-done.7.refs_1_, bf16[128,1024]{1,0:T(8,128)(2,1)S(1)} %collective-permute-done.11.refs_2_, ...), custom_call_target="tpu_custom_call" | custom-call | tf_op jit(solution)/shard_map/pallas_call | solution.py:217
  54.3 1.6 %collective-permute-start.15 = (bf16[128,512]{1,0:T(8,128)(2,1)S(1)}, bf16[128,512]{1,0:T(8,128)(2,1)S(1)}, u32[]{:S(2)}, u32[]{:S(2)}) collective-permute-start(bf16[128,512]{1,0:T(8,128)(2,1)S(1)} %get-tuple-element.66), channel_id=1, source_target_pairs={{0,1},{4,5},{1,2},{5,6},{2,3},{6,7},{3,11},{7,15},{11,10},{15,14},... | collective-permute-start | bytes 393224 | tf_op jit(solution)/shard_map/ppermute | solution.py:285
  56.4 2.6 %shard_map.91 = (bf16[144,512]{1,0:T(8,128)(2,1)S(1)}, bf16[128,512]{1,0:T(8,128)(2,1)S(1)}) custom-call(s32[1,2]{1,0:T(1,128)S(1)} %add_bitcast_fusion.refs_0_, bf16[128,1024]{1,0:T(8,128)(2,1)S(1)} %collective-permute-done.10.refs_1_, bf16[136,1024]{1,0:T(8,128)(2,1)S(1)} %collective-permute-done.14.refs_2_, ...), custom_call_target="tpu_custom_call" | custom-call | tf_op jit(solution)/shard_map/pallas_call | solution.py:217
  61.9 4.6 %collective-permute-done.18.refs_2_ = bf16[128,512]{1,0:T(8,128)(2,1)S(1)} collective-permute-done((bf16[128,512]{1,0:T(8,128)(2,1)S(1)}, bf16[128,512]{1,0:T(8,128)(2,1)S(1)}, u32[]{:S(2)}, u32[]{:S(2)}) %collective-permute-start.18) | collective-permute-done | bytes 131104 | tf_op jit(solution)/shard_map/ppermute | solution.py:285
  66.5 2.4 %collective-permute-start.19 = (bf16[144,512]{1,0:T(8,128)(2,1)S(1)}, bf16[144,512]{1,0:T(8,128)(2,1)S(1)}, u32[]{:S(2)}, u32[]{:S(2)}) collective-permute-start(bf16[144,512]{1,0:T(8,128)(2,1)S(1)} %get-tuple-element.75), channel_id=1, source_target_pairs={{0,1},{4,5},{1,2},{5,6},{2,3},{6,7},{3,11},{7,15},{11,10},{15,14},... | collective-permute-start | bytes 442376 | tf_op jit(solution)/shard_map/ppermute | solution.py:285
  69.0 1.7 %collective-permute-start.21 = (bf16[128,512]{1,0:T(8,128)(2,1)S(1)}, bf16[128,512]{1,0:T(8,128)(2,1)S(1)}, u32[]{:S(2)}, u32[]{:S(2)}) collective-permute-start(bf16[128,512]{1,0:T(8,128)(2,1)S(1)} %get-tuple-element.70), channel_id=1, source_target_pairs={{0,1},{4,5},{1,2},{5,6},{2,3},{6,7},{3,11},{7,15},{11,10},{15,14},... | collective-permute-start | bytes 393224 | tf_op jit(solution)/shard_map/ppermute | solution.py:285
  71.0 4.6 %shard_map.94 = (f32[144,512]{1,0:T(8,128)S(1)}, f32[128,512]{1,0:T(8,128)S(1)}, f32[144,512]{1,0:T(8,128)S(1)}, f32[128,512]{1,0:T(8,128)S(1)}) custom-call(s32[1,2]{1,0:T(1,128)S(1)} %add_bitcast_fusion.refs_0_, bf16[128,1024]{1,0:T(8,128)(2,1)} %collective-permute-done.refs_1_, bf16[128,1024]{1,0:T(8,128)(2,1)} %collective-permute-done.1.refs_2_, ...), custom_call_target="tpu_custom_call" | custom-call | tf_op jit(solution)/shard_map/pallas_call | solution.py:217
  79.5 3.7 %collective-permute-done.24.refs_2_ = bf16[128,512]{1,0:T(8,128)(2,1)S(1)} collective-permute-done((bf16[128,512]{1,0:T(8,128)(2,1)S(1)}, bf16[128,512]{1,0:T(8,128)(2,1)S(1)}, u32[]{:S(2)}, u32[]{:S(2)}) %collective-permute-start.24) | collective-permute-done | bytes 131104 | tf_op jit(solution)/shard_map/ppermute | solution.py:285
  86.1 3.8 %collective-permute-done.26.right_a = bf16[128,512]{1,0:T(8,128)(2,1)S(1)} collective-permute-done((bf16[128,512]{1,0:T(8,128)(2,1)S(1)}, bf16[128,512]{1,0:T(8,128)(2,1)S(1)}, u32[]{:S(2)}, u32[]{:S(2)}) %collective-permute-start.26) | collective-permute-done | bytes 131104 | tf_op jit(solution)/shard_map/ppermute | solution.py:285
  (68 shorter events, 26.9 us)
Async XLA Ops:
  2.4 16.9 %collective-permute-start.2 = (bf16[136,1024]{1,0:T(8,128)(2,1)S(1)}, bf16[136,1024]{1,0:T(8,128)(2,1)}, u32[]{:S(2)}, u32[]{:S(2)}) collective-permute-start(bf16[136,1024]{1,0:T(8,128)(2,1)S(1)} %constant_dynamic-update-slice_fusion.refs_2_), channel_id=1, source_target_pairs={{0,1},{4,5},{1,2},{5,6},{2,3},{6,7},{3,11},{7,15},{11,10},{15,14},... | collective-permute-start | bytes 835592 | tf_op jit(solution)/shard_map/ppermute | solution.py:285
  5.4 13.8 %collective-permute-start.3 = (bf16[136,1024]{1,0:T(8,128)(2,1)S(1)}, bf16[136,1024]{1,0:T(8,128)(2,1)}, u32[]{:S(2)}, u32[]{:S(2)}) collective-permute-start(bf16[136,1024]{1,0:T(8,128)(2,1)S(1)} %constant_dynamic-update-slice_fusion.refs_2_), channel_id=1, source_target_pairs={{0,8},{4,12},{1,0},{5,4},{2,1},{6,5},{3,2},{7,6},{11,3},{15,7},{10... | collective-permute-start | bytes 835592 | tf_op jit(solution)/shard_map/ppermute | solution.py:285
  5.4 12.3 %collective-permute-start = (bf16[128,1024]{1,0:T(8,128)(2,1)}, bf16[128,1024]{1,0:T(8,128)(2,1)}, u32[]{:S(2)}, u32[]{:S(2)}) collective-permute-start(bf16[128,1024]{1,0:T(8,128)(2,1)} %refs_1_.1), channel_id=1, source_target_pairs={{0,1},{4,5},{1,2},{5,6},{2,3},{6,7},{3,11},{7,15},{11,10},{15,14},... | collective-permute-start | bytes 786440 | tf_op jit(solution)/shard_map/ppermute | solution.py:285
  7.5 11.8 %collective-permute-start.1 = (bf16[128,1024]{1,0:T(8,128)(2,1)}, bf16[128,1024]{1,0:T(8,128)(2,1)}, u32[]{:S(2)}, u32[]{:S(2)}) collective-permute-start(bf16[128,1024]{1,0:T(8,128)(2,1)} %refs_1_.1), channel_id=1, source_target_pairs={{0,8},{4,12},{1,0},{5,4},{2,1},{6,5},{3,2},{7,6},{11,3},{15,7},{10... | collective-permute-start | bytes 786440 | tf_op jit(solution)/shard_map/ppermute | solution.py:285
  19.3 11.3 %collective-permute-start.8 = (bf16[136,1024]{1,0:T(8,128)(2,1)}, bf16[136,1024]{1,0:T(8,128)(2,1)}, u32[]{:S(2)}, u32[]{:S(2)}) collective-permute-start(bf16[136,1024]{1,0:T(8,128)(2,1)} %collective-permute-done.2.refs_3_), channel_id=1, source_target_pairs={{0,1},{4,5},{1,2},{5,6},{2,3},{6,7},{3,11},{7,15},{11,10},{15,14},... | collective-permute-start | bytes 835592 | tf_op jit(solution)/shard_map/ppermute | solution.py:285
  20.9 9.8 %collective-permute-start.9 = (bf16[136,1024]{1,0:T(8,128)(2,1)}, bf16[136,1024]{1,0:T(8,128)(2,1)}, u32[]{:S(2)}, u32[]{:S(2)}) collective-permute-start(bf16[136,1024]{1,0:T(8,128)(2,1)} %collective-permute-done.3.refs_4_), channel_id=1, source_target_pairs={{0,8},{4,12},{1,0},{5,4},{2,1},{6,5},{3,2},{7,6},{11,3},{15,7},{10... | collective-permute-start | bytes 835592 | tf_op jit(solution)/shard_map/ppermute | solution.py:285
  21.4 12.9 %collective-permute-start.5 = (bf16[128,1024]{1,0:T(8,128)(2,1)}, bf16[128,1024]{1,0:T(8,128)(2,1)}, u32[]{:S(2)}, u32[]{:S(2)}) collective-permute-start(bf16[128,1024]{1,0:T(8,128)(2,1)} %collective-permute-done.refs_1_), channel_id=1, source_target_pairs={{0,1},{4,5},{1,2},{5,6},{2,3},{6,7},{3,11},{7,15},{11,10},{15,14},... | collective-permute-start | bytes 786440 | tf_op jit(solution)/shard_map/ppermute | solution.py:285
  23.0 13.4 %collective-permute-start.6 = (bf16[128,1024]{1,0:T(8,128)(2,1)}, bf16[128,1024]{1,0:T(8,128)(2,1)}, u32[]{:S(2)}, u32[]{:S(2)}) collective-permute-start(bf16[128,1024]{1,0:T(8,128)(2,1)} %collective-permute-done.1.refs_2_), channel_id=1, source_target_pairs={{0,8},{4,12},{1,0},{5,4},{2,1},{6,5},{3,2},{7,6},{11,3},{15,7},{10... | collective-permute-start | bytes 786440 | tf_op jit(solution)/shard_map/ppermute | solution.py:285
  30.7 11.5 %collective-permute-start.13 = (bf16[136,1024]{1,0:T(8,128)(2,1)}, bf16[136,1024]{1,0:T(8,128)(2,1)S(1)}, u32[]{:S(2)}, u32[]{:S(2)}) collective-permute-start(bf16[136,1024]{1,0:T(8,128)(2,1)} %collective-permute-done.9.refs_4_), channel_id=1, source_target_pairs={{0,8},{4,12},{1,0},{5,4},{2,1},{6,5},{3,2},{7,6},{11,3},{15,7},{10... | collective-permute-start | bytes 835592 | tf_op jit(solution)/shard_map/ppermute | solution.py:285
  36.4 10.9 %collective-permute-start.7 = (bf16[128,1024]{1,0:T(8,128)(2,1)}, bf16[128,1024]{1,0:T(8,128)(2,1)S(1)}, u32[]{:S(2)}, u32[]{:S(2)}) collective-permute-start(bf16[128,1024]{1,0:T(8,128)(2,1)} %collective-permute-done.5.refs_1_), channel_id=1, source_target_pairs={{0,1},{4,5},{1,2},{5,6},{2,3},{6,7},{3,11},{7,15},{11,10},{15,14},... | collective-permute-start | bytes 786440 | tf_op jit(solution)/shard_map/ppermute | solution.py:285
  37.9 12.4 %collective-permute-start.12 = (bf16[136,1024]{1,0:T(8,128)(2,1)}, bf16[136,1024]{1,0:T(8,128)(2,1)S(1)}, u32[]{:S(2)}, u32[]{:S(2)}) collective-permute-start(bf16[136,1024]{1,0:T(8,128)(2,1)} %collective-permute-done.8.refs_3_), channel_id=1, source_target_pairs={{0,1},{4,5},{1,2},{5,6},{2,3},{6,7},{3,11},{7,15},{11,10},{15,14},... | collective-permute-start | bytes 835592 | tf_op jit(solution)/shard_map/ppermute | solution.py:285
  39.4 9.5 %collective-permute-start.11 = (bf16[128,1024]{1,0:T(8,128)(2,1)}, bf16[128,1024]{1,0:T(8,128)(2,1)S(1)}, u32[]{:S(2)}, u32[]{:S(2)}) collective-permute-start(bf16[128,1024]{1,0:T(8,128)(2,1)} %collective-permute-done.6.refs_2_), channel_id=1, source_target_pairs={{0,8},{4,12},{1,0},{5,4},{2,1},{6,5},{3,2},{7,6},{11,3},{15,7},{10... | collective-permute-start | bytes 786440 | tf_op jit(solution)/shard_map/ppermute | solution.py:285
  42.2 14.1 %collective-permute-start.14 = (bf16[136,1024]{1,0:T(8,128)(2,1)S(1)}, bf16[136,1024]{1,0:T(8,128)(2,1)S(1)}, u32[]{:S(2)}, u32[]{:S(2)}) collective-permute-start(bf16[136,1024]{1,0:T(8,128)(2,1)S(1)} %collective-permute-done.13.refs_4_), channel_id=1, source_target_pairs={{0,8},{4,12},{1,0},{5,4},{2,1},{6,5},{3,2},{7,6},{11,3},{15,7},{10... | collective-permute-start | bytes 835592 | tf_op jit(solution)/shard_map/ppermute | solution.py:285
  47.3 9.1 %collective-permute-start.10 = (bf16[128,1024]{1,0:T(8,128)(2,1)S(1)}, bf16[128,1024]{1,0:T(8,128)(2,1)S(1)}, u32[]{:S(2)}, u32[]{:S(2)}) collective-permute-start(bf16[128,1024]{1,0:T(8,128)(2,1)S(1)} %collective-permute-done.7.refs_1_), channel_id=1, source_target_pairs={{0,1},{4,5},{1,2},{5,6},{2,3},{6,7},{3,11},{7,15},{11,10},{15,14},... | collective-permute-start | bytes 786440 | tf_op jit(solution)/shard_map/ppermute | solution.py:285
  53.8 5.9 %collective-permute-start.16 = (bf16[144,512]{1,0:T(8,128)(2,1)S(1)}, bf16[144,512]{1,0:T(8,128)(2,1)S(1)}, u32[]{:S(2)}, u32[]{:S(2)}) collective-permute-start(bf16[144,512]{1,0:T(8,128)(2,1)S(1)} %get-tuple-element.62), channel_id=1, source_target_pairs={{0,8},{4,12},{1,0},{5,4},{2,1},{6,5},{3,2},{7,6},{11,3},{15,7},{10... | collective-permute-start | bytes 442376 | tf_op jit(solution)/shard_map/ppermute | solution.py:285
  59.7 6.8 %collective-permute-start.17 = (bf16[144,512]{1,0:T(8,128)(2,1)S(1)}, bf16[144,512]{1,0:T(8,128)(2,1)S(1)}, u32[]{:S(2)}, u32[]{:S(2)}) collective-permute-start(bf16[144,512]{1,0:T(8,128)(2,1)S(1)} %get-tuple-element.67), channel_id=1, source_target_pairs={{0,1},{4,5},{1,2},{5,6},{2,3},{6,7},{3,11},{7,15},{11,10},{15,14},... | collective-permute-start | bytes 442376 | tf_op jit(solution)/shard_map/ppermute | solution.py:285
  61.8 13.8 %collective-permute-start.22 = (bf16[144,512]{1,0:T(8,128)(2,1)S(1)}, bf16[144,512]{1,0:T(8,128)(2,1)S(1)}, u32[]{:S(2)}, u32[]{:S(2)}) collective-permute-start(bf16[144,512]{1,0:T(8,128)(2,1)S(1)} %get-tuple-element.77), channel_id=1, source_target_pairs={{0,8},{4,12},{1,0},{5,4},{2,1},{6,5},{3,2},{7,6},{11,3},{15,7},{10... | collective-permute-start | bytes 442376 | tf_op jit(solution)/shard_map/ppermute | solution.py:285
  66.5 10.6 %collective-permute-start.19 = (bf16[144,512]{1,0:T(8,128)(2,1)S(1)}, bf16[144,512]{1,0:T(8,128)(2,1)S(1)}, u32[]{:S(2)}, u32[]{:S(2)}) collective-permute-start(bf16[144,512]{1,0:T(8,128)(2,1)S(1)} %get-tuple-element.75), channel_id=1, source_target_pairs={{0,1},{4,5},{1,2},{5,6},{2,3},{6,7},{3,11},{7,15},{11,10},{15,14},... | collective-permute-start | bytes 442376 | tf_op jit(solution)/shard_map/ppermute | solution.py:285
  69.0 6.6 %collective-permute-start.21 = (bf16[128,512]{1,0:T(8,128)(2,1)S(1)}, bf16[128,512]{1,0:T(8,128)(2,1)S(1)}, u32[]{:S(2)}, u32[]{:S(2)}) collective-permute-start(bf16[128,512]{1,0:T(8,128)(2,1)S(1)} %get-tuple-element.70), channel_id=1, source_target_pairs={{0,1},{4,5},{1,2},{5,6},{2,3},{6,7},{3,11},{7,15},{11,10},{15,14},... | collective-permute-start | bytes 393224 | tf_op jit(solution)/shard_map/ppermute | solution.py:285
  70.7 6.4 %collective-permute-start.20 = (bf16[128,512]{1,0:T(8,128)(2,1)S(1)}, bf16[128,512]{1,0:T(8,128)(2,1)S(1)}, u32[]{:S(2)}, u32[]{:S(2)}) collective-permute-start(bf16[128,512]{1,0:T(8,128)(2,1)S(1)} %get-tuple-element.76), channel_id=1, source_target_pairs={{0,8},{4,12},{1,0},{5,4},{2,1},{6,5},{3,2},{7,6},{11,3},{15,7},{10... | collective-permute-start | bytes 393224 | tf_op jit(solution)/shard_map/ppermute | solution.py:285
  77.2 6.0 %collective-permute-start.23 = (bf16[144,512]{1,0:T(8,128)(2,1)S(1)}, bf16[144,512]{1,0:T(8,128)(2,1)S(1)}, u32[]{:S(2)}, u32[]{:S(2)}) collective-permute-start(bf16[144,512]{1,0:T(8,128)(2,1)S(1)} %get-tuple-element.87), channel_id=1, source_target_pairs={{0,1},{4,5},{1,2},{5,6},{2,3},{6,7},{3,11},{7,15},{11,10},{15,14},... | collective-permute-start | bytes 442376 | tf_op jit(solution)/shard_map/ppermute | solution.py:285
  79.3 10.6 %collective-permute-start.27 = (bf16[144,512]{1,0:T(8,128)(2,1)S(1)}, bf16[144,512]{1,0:T(8,128)(2,1)S(1)}, u32[]{:S(2)}, u32[]{:S(2)}) collective-permute-start(bf16[144,512]{1,0:T(8,128)(2,1)S(1)} %get-tuple-element.94), channel_id=1, source_target_pairs={{0,8},{4,12},{1,0},{5,4},{2,1},{6,5},{3,2},{7,6},{11,3},{15,7},{10... | collective-permute-start | bytes 442376 | tf_op jit(solution)/shard_map/ppermute | solution.py:285
  83.3 7.0 %collective-permute-start.25 = (bf16[144,512]{1,0:T(8,128)(2,1)S(1)}, bf16[144,512]{1,0:T(8,128)(2,1)S(1)}, u32[]{:S(2)}, u32[]{:S(2)}) collective-permute-start(bf16[144,512]{1,0:T(8,128)(2,1)S(1)} %get-tuple-element.93), channel_id=1, source_target_pairs={{0,1},{4,5},{1,2},{5,6},{2,3},{6,7},{3,11},{7,15},{11,10},{15,14},... | collective-permute-start | bytes 442376 | tf_op jit(solution)/shard_map/ppermute | solution.py:285
  83.9 6.0 %collective-permute-start.26 = (bf16[128,512]{1,0:T(8,128)(2,1)S(1)}, bf16[128,512]{1,0:T(8,128)(2,1)S(1)}, u32[]{:S(2)}, u32[]{:S(2)}) collective-permute-start(bf16[128,512]{1,0:T(8,128)(2,1)S(1)} %get-tuple-element.82), channel_id=1, source_target_pairs={{0,1},{4,5},{1,2},{5,6},{2,3},{6,7},{3,11},{7,15},{11,10},{15,14},... | collective-permute-start | bytes 393224 | tf_op jit(solution)/shard_map/ppermute | solution.py:285
  (11 other events, 48.2 us)

commit v4 on v3

--- a/solution.py
+++ b/solution.py
@@ -7,6 +7,7 @@
 
 BOTH = ("grp", "ep")
 LIGHT = pl.CostEstimate(flops=0, transcendentals=0, bytes_accessed=0)
+ADD_COST = pl.CostEstimate(flops=10**9, transcendentals=0, bytes_accessed=0)
 CONTRACT_LAST = (((1,), (1,)), ((), ()))
 
 
@@ -111,9 +112,9 @@
 def bf16_pieces(values):
     pieces = []
     for unused in range(3):
-        piece = values.astype(jnp.bfloat16)
-        values = values - piece.astype(jnp.float32)
-        pieces.append(piece)
+        piece = lax.reduce_precision(values, exponent_bits=8, mantissa_bits=7)
+        values = values - piece
+        pieces.append(piece.astype(jnp.bfloat16))
     return pieces
 
 
@@ -131,22 +132,6 @@
     return jnp.sum(jnp.where(across == down, line, 0.0), axis=1, keepdims=True)
 
 
-def merge_kernel(gate, up, down, out):
-    hidden = gate.shape[1]
-    out[:, :hidden] = gate[...]
-    out[:, hidden : 2 * hidden] = up[...]
-    out[:, 2 * hidden :] = down[...].T
-
-
-def merge_weights(w_gate, w_up, w_down):
-    return pl.pallas_call(
-        merge_kernel,
-        out_shape=pltpu.HBM((w_gate.shape[0], 3 * w_gate.shape[1]), w_gate.dtype),
-        compiler_params=pltpu.CompilerParams(vmem_limit_bytes=24 << 20),
-        cost_estimate=LIGHT,
-    )(w_gate, w_up, w_down)
-
-
 def hold_kernel(count, pieces, *refs):
     sources, held, sems = refs[:count], refs[count : 2 * count], refs[-1]
     copies = []
@@ -164,29 +149,28 @@
 def hold(*arrays, pieces=4):
     return pl.pallas_call(
         lambda *refs: hold_kernel(len(arrays), pieces, *refs),
-        in_specs=[pl.BlockSpec(memory_space=pl.ANY)] * len(arrays),
+        in_specs=[pl.BlockSpec(memory_space=pltpu.HBM)] * len(arrays),
         out_shape=[pltpu.VMEM(array.shape, array.dtype) for array in arrays],
         scratch_shapes=[pltpu.SemaphoreType.DMA((len(arrays), pieces))],
         compiler_params=pltpu.CompilerParams(vmem_limit_bytes=24 << 20),
         cost_estimate=LIGHT,
-    )(*arrays)
+    )(*[pltpu.with_memory_space_constraint(array, pltpu.HBM) for array in arrays])
 
 
 def grads_kernel(blocks, rows, experts, extra, *refs):
     place_ref, refs = refs[0], refs[1:]
     token_refs, grad_refs, refs = refs[:blocks], refs[blocks : 2 * blocks], refs[2 * blocks :]
-    weights, outs = refs[:2], refs[2:]
+    weights, outs = (refs[:3], refs[3:6]), refs[6:]
     places = [jnp.max(place_ref[:, at : at + 1]) for at in range(2)]
     rows_in = jnp.concatenate([ref[...] for ref in token_refs], 0)
     with_lines = [ref[...] for ref in grad_refs]
     grads_in = jnp.concatenate([block[:rows] for block in with_lines], 0)
     total, spread = None, [None] * blocks
-    for at, merged in enumerate(weights):
-        hidden = merged.shape[1] // 3
-        w_gate, w_up, w_down = (merged[:, i * hidden : (i + 1) * hidden] for i in range(3))
+    for at, three in enumerate(weights):
+        w_gate, w_up, w_down = (w[...] for w in three)
         gate_pre = jnp.dot(rows_in, w_gate, preferred_element_type=jnp.float32)
         up_pre = jnp.dot(rows_in, w_up, preferred_element_type=jnp.float32)
-        hidden_grad = jnp.dot(grads_in, w_down, preferred_element_type=jnp.float32)
+        hidden_grad = lax.dot_general(grads_in, w_down, CONTRACT_LAST, preferred_element_type=jnp.float32)
         grad_gate, grad_up, weight_grad = hidden_grads(gate_pre, up_pre, hidden_grad)
         row_terms = both_terms(grad_gate, grad_up, w_gate, w_up)
         shares = [read_share(block[rows:], places[at], experts, rows) for block in with_lines]
@@ -236,7 +220,7 @@
         add_kernel,
         out_shape=[jax.ShapeDtypeStruct(came.shape, came.dtype) for came, own in pairs],
         compiler_params=pltpu.CompilerParams(vmem_limit_bytes=8 << 20),
-        cost_estimate=LIGHT,
+        cost_estimate=ADD_COST,
     )(*operands)
 
 
@@ -248,11 +232,10 @@
     tokens_out[:, :half] = left[:rows].astype(tokens_out.dtype)
     tokens_out[:, half:] = (right_own[...] + as_f32(right_a) + as_f32(right_b)).astype(tokens_out.dtype)
     grads = left[rows:, :rows]
-    by_token = jnp.concatenate([grads, jnp.zeros((rows - extra, rows), jnp.float32)], 0).T
-    lanes = lax.broadcasted_iota(jnp.int32, (rows, rows), 1)
-    for k in range(ids.shape[1]):
-        picked = jnp.where(lanes == ids[:, k : k + 1], by_token, 0.0)
-        weights_out[:, k : k + 1] = jnp.sum(picked, axis=1, keepdims=True).astype(weights_out.dtype)
+    experts = lax.broadcasted_iota(jnp.int32, grads.shape, 0)
+    for k in range(ids.shape[0]):
+        picked = jnp.where(experts == ids[k : k + 1, :], grads, 0.0)
+        weights_out[k : k + 1, :] = jnp.sum(picked, axis=0, keepdims=True).astype(weights_out.dtype)
 
 
 def ring_order(chips_x, lanes):
@@ -288,7 +271,6 @@
     other = jnp.where(lax.rem(lax.axis_index("grp"), 2) == 0, me + lanes, me - lanes)
     places = jnp.stack([me, other]).reshape(1, 2)
 
-    token_up, token_down = send(tokens, ahead), send(tokens, behind)
     expert_list = jnp.arange(devices, dtype=jnp.int32)
     chosen = expert_ids[None, :, :] == expert_list[:, None, None]
     dense = jnp.sum(jnp.where(chosen, route_weights[None], 0.0), axis=-1)
@@ -297,9 +279,11 @@
     lines = jnp.pad(lines, ((0, line_rows * width // rows - 3 * devices), (0, 0))).reshape(line_rows, width)
     cotangent = jnp.concatenate([cotangent, lines], 0)
     grad_up, grad_down = send(cotangent, ahead), send(cotangent, behind)
-    mine = merge_weights(w_gate[0], w_up[0], w_down[0])
-    mine = after_all(mine, token_up, token_down, grad_up, grad_down)[0]
-    weights = hold(mine, send(mine, across))
+    mine = (w_gate[0], w_up[0], w_down[0])
+    other = tuple(send(w, across) for w in mine)
+    second = after_all(tokens, *other)[0]
+    token_up, token_down = send(second, ahead), send(second, behind)
+    weights = hold(*mine, *other)
 
     sums = {}
 
@@ -317,40 +301,37 @@
     arrived = [[(0, tokens, cotangent)], [(1, token_up, grad_up), (chips - 1, token_down, grad_down)]]
     for step in range(2, far):
         if step == far - 1:
-            token_up, token_down = after_all(token_up, token_down, weights[0])[:2]
             grad_up, grad_down = after_all(grad_up, grad_down, compute(arrived[0]))[:2]
         token_up, token_down = send(token_up, ahead), send(token_down, behind)
         grad_up, grad_down = send(grad_up, ahead), send(grad_down, behind)
         arrived.append([(step, token_up, grad_up), (chips - step, token_down, grad_down)])
-    token_up = after_all(token_up, compute(arrived[far - 2]))[0]
+    grad_down = after_all(grad_down, grad_up, *[compute(arrived[o]) for o in range(1, far - 2)])[0]
+    token_up = after_all(token_up, token_down, compute(arrived[far - 2]))[0]
     token_up, grad_down = send(token_up, ahead), send(grad_down, behind)
     last = compute(arrived[far - 1])
 
     right_up, left_down = send(sums[chips - far + 1][1], ahead), send(sums[far - 1][0], behind)
     token_up = after_all(token_up, last)[0]
     compute([(far, token_up, grad_down)])
-    for o in range(far - 3, 0, -1):
-        compute(arrived[o])
     left_up, right_down = after_all(*sums[far], right_up, left_down)[:2]
     for step in range(far, 0, -1):
         left_up, right_down = send(left_up, ahead), send(right_down, behind)
         if step > 2:
             right_up, left_down = add_pairs((right_up, sums[chips - step + 2][1]), (left_down, sums[step - 2][0]))
-            turn = right_up
             right_up, left_down = send(right_up, ahead), send(left_down, behind)
         if step > 1:
-            left_up, right_down = after_all(left_up, right_down, turn)[:2]
             left_up, right_down = add_pairs((left_up, sums[chips - step + 1][0]), (right_down, sums[step - 1][1]))
-            right_up, left_down = after_all(right_up, left_down, left_up)[:2]
-
-    return pl.pallas_call(
+
+    grad_tokens, grad_weights = pl.pallas_call(
         finish_kernel,
         out_shape=[
             jax.ShapeDtypeStruct(tokens.shape, tokens.dtype),
-            jax.ShapeDtypeStruct(expert_ids.shape, jnp.bfloat16),
+            jax.ShapeDtypeStruct(expert_ids.shape[::-1], jnp.bfloat16),
         ],
         compiler_params=pltpu.CompilerParams(vmem_limit_bytes=8 << 20),
-    )(*sums[0], left_up, left_down, right_up, right_down, expert_ids)
+        cost_estimate=LIGHT,
+    )(*sums[0], left_up, left_down, right_up, right_down, expert_ids.T)
+    return (grad_tokens, grad_weights.T)
 
 
 def on_device(tokens, cotangent, expert_ids, route_weights, w_gate, w_up, w_down):

time: 92.8 us -> 84.7 us (0.913)
  local copies, waits for them, and re-layouts: 7.77 us -> 2.01 us
  Pallas kernels: 22 us -> 20 us
    unnamed x14 -> x7, local copies, waits for them, and re-layouts: 7.08 us -> 2 us
    pallas_call x1, Pallas kernels: 0.51 us -> 2.96 us  [hold(): pl.pallas_call(lambda *refs: hold_kernel(len(arrays), pieces, *refs), in_...]
    pallas_call x1 -> x0, Pallas kernels: 2.07 us -> none  [merge_weights(): pl.pallas_call(merge_kernel, out_shape=pltpu.HBM((w_gate.shape[0], 3 * w_...]
    pallas_call x5, Pallas kernels: 17.7 us -> 15.9 us  [block_grads(): pl.pallas_call(lambda *refs: grads_kernel(blocks, rows, experts, extra, *...]
    ppermute x29 -> x31, starting transfers between devices: 29 us -> 29.6 us  [send(): return lax.ppermute(array, BOTH, pairs)]
    ppermute x29 -> x31, waiting for transfers between devices: 32 us -> 31.4 us  [send(): return lax.ppermute(array, BOTH, pairs)]
  transfers between devices with their start and end apart: 29 -> 31, of which waited for: 15 -> 13; matrix products, arithmetic and copies ran while one was open for 0% -> 2% of each run, Pallas kernels for 22% -> 23%
where the time goes in v4:
time: 84.7 us; the launch traced here: 84.6 us
  waiting for transfers between devices  31.4 us (37%)
  starting transfers between devices  29.6 us (35%)
  Pallas kernels  20 us (24%)
  local copies, waits for them, and re-layouts  2.01 us (2%)
    ppermute x31, waiting for transfers between devices, send(): return lax.ppermute(array, BOTH, pairs)  31.4 us
    ppermute x31, starting transfers between devices, send(): return lax.ppermute(array, BOTH, pairs)  29.6 us
    pallas_call x5, Pallas kernels, block_grads(): pl.pallas_call(lambda *refs: grads_kernel(blocks, rows, experts, extra, *...  15.9 us
    pallas_call x1, Pallas kernels, hold(): pl.pallas_call(lambda *refs: hold_kernel(len(arrays), pieces, *refs), in_...  2.96 us
    unnamed x7, local copies, waits for them, and re-layouts  2 us
  transfers between devices with their start and end apart: 31, of which 13 were waited for; matrix products, arithmetic and copies ran while one was open for 2% of the time, Pallas kernels for 23%

profile of v4, /device:TPU:0, one launch (start us, length us, event | category | flops | bytes accessed | tf_op | source)
XLA Modules:
  0.0 84.6 jit_solution(1864278971695218439)
XLA Ops:
  3.4 2.7 %collective-permute-start.9 = (bf16[136,1024]{1,0:T(8,128)(2,1)S(1)}, bf16[136,1024]{1,0:T(8,128)(2,1)S(1)}, u32[]{:S(2)}, u32[]{:S(2)}) collective-permute-start(bf16[136,1024]{1,0:T(8,128)(2,1)S(1)} %constant_dynamic-update-slice_fusion.refs_2_), channel_id=1, source_target_pairs={{0,1},{4,5},{1,2},{5,6},{2,3},{6,7},{3,11},{7,15},{11,10},{15,14},... | collective-permute-start | bytes 835592 | tf_op jit(solution)/shard_map/ppermute | solution.py:268
  7.2 2.6 %collective-permute-start.3 = (bf16[128,1024]{1,0:T(8,128)(2,1)S(1)}, bf16[128,1024]{1,0:T(8,128)(2,1)S(1)}, u32[]{:S(2)}, u32[]{:S(2)}) collective-permute-start(bf16[128,1024]{1,0:T(8,128)(2,1)S(1)} %copy-done), channel_id=1, source_target_pairs={{0,1},{4,5},{1,2},{5,6},{2,3},{6,7},{3,11},{7,15},{11,10},{15,14},... | collective-permute-start | bytes 786440 | tf_op jit(solution)/shard_map/ppermute | solution.py:268
  9.7 3.9 %collective-permute-done.9.refs_3_ = bf16[136,1024]{1,0:T(8,128)(2,1)S(1)} collective-permute-done((bf16[136,1024]{1,0:T(8,128)(2,1)S(1)}, bf16[136,1024]{1,0:T(8,128)(2,1)S(1)}, u32[]{:S(2)}, u32[]{:S(2)}) %collective-permute-start.9) | collective-permute-done | bytes 278560 | tf_op jit(solution)/shard_map/ppermute | solution.py:268
  13.6 2.0 %collective-permute-start.10 = (bf16[136,1024]{1,0:T(8,128)(2,1)S(1)}, bf16[136,1024]{1,0:T(8,128)(2,1)S(1)}, u32[]{:S(2)}, u32[]{:S(2)}) collective-permute-start(bf16[136,1024]{1,0:T(8,128)(2,1)S(1)} %collective-permute-done.9.refs_3_), channel_id=1, source_target_pairs={{0,1},{4,5},{1,2},{5,6},{2,3},{6,7},{3,11},{7,15},{11,10},{15,14},... | collective-permute-start | bytes 835592 | tf_op jit(solution)/shard_map/ppermute | solution.py:268
  15.7 3.5 %collective-permute-done.3.refs_1_ = bf16[128,1024]{1,0:T(8,128)(2,1)S(1)} collective-permute-done((bf16[128,1024]{1,0:T(8,128)(2,1)S(1)}, bf16[128,1024]{1,0:T(8,128)(2,1)S(1)}, u32[]{:S(2)}, u32[]{:S(2)}) %collective-permute-start.3) | collective-permute-done | bytes 262176 | tf_op jit(solution)/shard_map/ppermute | solution.py:268
  19.2 2.0 %collective-permute-start.4 = (bf16[128,1024]{1,0:T(8,128)(2,1)S(1)}, bf16[128,1024]{1,0:T(8,128)(2,1)S(1)}, u32[]{:S(2)}, u32[]{:S(2)}) collective-permute-start(bf16[128,1024]{1,0:T(8,128)(2,1)S(1)} %collective-permute-done.3.refs_1_), channel_id=1, source_target_pairs={{0,1},{4,5},{1,2},{5,6},{2,3},{6,7},{3,11},{7,15},{11,10},{15,14},... | collective-permute-start | bytes 786440 | tf_op jit(solution)/shard_map/ppermute | solution.py:268
  21.4 3.0 %shard_map.86 = (bf16[1024,512]{1,0:T(8,128)(2,1)S(1)}, bf16[1024,512]{1,0:T(8,128)(2,1)S(1)}, bf16[512,1024]{1,0:T(8,128)(2,1)S(1)}, bf16[1024,512]{1,0:T(8,128...) custom-call(bf16[1024,512]{1,0:T(8,128)(2,1)} %bitcast.11, bf16[1024,512]{1,0:T(8,128)(2,1)} %bitcast.13, ...), custom_call_target="tpu_custom_call" | custom-call | tf_op jit(solution)/shard_map/pallas_call | solution.py:150
  24.3 2.9 %shard_map.87 = (f32[144,512]{1,0:T(8,128)S(1)}, f32[128,512]{1,0:T(8,128)S(1)}) custom-call(s32[1,2]{1,0:T(1,128)S(1)} %add_bitcast_fusion.refs_0_, bf16[128,1024]{1,0:T(8,128)(2,1)S(1)} %copy-done, bf16[136,1024]{1,0:T(8,128)(2,1)S(1)} %constant_dynamic-update-slice_fusion.refs_2_, bf16[1024,512]{1,0:T(8,128)(2,1)S(1)} %get-tuple-element.44.refs_3_.refs_5_, ...), custom_call_target="tpu_custom_call" | custom-call | tf_op jit(solution)/shard_map/pallas_call | solution.py:201
  27.3 2.1 %collective-permute-start.14 = (bf16[136,1024]{1,0:T(8,128)(2,1)S(1)}, bf16[136,1024]{1,0:T(8,128)(2,1)S(1)}, u32[]{:S(2)}, u32[]{:S(2)}) collective-permute-start(bf16[136,1024]{1,0:T(8,128)(2,1)S(1)} %collective-permute-done.10.refs_3_), channel_id=1, source_target_pairs={{0,1},{4,5},{1,2},{5,6},{2,3},{6,7},{3,11},{7,15},{11,10},{15,14},... | collective-permute-start | bytes 835592 | tf_op jit(solution)/shard_map/ppermute | solution.py:268
  30.8 2.0 %collective-permute-start.5 = (bf16[128,1024]{1,0:T(8,128)(2,1)S(1)}, bf16[128,1024]{1,0:T(8,128)(2,1)S(1)}, u32[]{:S(2)}, u32[]{:S(2)}) collective-permute-start(bf16[128,1024]{1,0:T(8,128)(2,1)S(1)} %collective-permute-done.4.refs_1_), channel_id=1, source_target_pairs={{0,1},{4,5},{1,2},{5,6},{2,3},{6,7},{3,11},{7,15},{11,10},{15,14},... | collective-permute-start | bytes 786440 | tf_op jit(solution)/shard_map/ppermute | solution.py:268
  32.9 3.3 %shard_map.90 = (f32[144,512]{1,0:T(8,128)S(1)}, f32[128,512]{1,0:T(8,128)S(1)}, f32[144,512]{1,0:T(8,128)S(1)}, f32[128,512]{1,0:T(8,128)S(1)}) custom-call(s32[1,2]{1,0:T(1,128)S(1)} %add_bitcast_fusion.refs_0_, bf16[128,1024]{1,0:T(8,128)(2,1)S(1)} %collective-permute-done.3.refs_1_, bf16[128,1024]{1,0:T(8,128)(2,1)S(1)} %collective-permute-done.6.refs_2_, ...), custom_call_target="tpu_custom_call" | custom-call | tf_op jit(solution)/shard_map/pallas_call | solution.py:201
  36.9 2.0 %collective-permute-done.15.refs_4_ = bf16[136,1024]{1,0:T(8,128)(2,1)S(1)} collective-permute-done((bf16[136,1024]{1,0:T(8,128)(2,1)S(1)}, bf16[136,1024]{1,0:T(8,128)(2,1)S(1)}, u32[]{:S(2)}, u32[]{:S(2)}) %collective-permute-start.15) | collective-permute-done | bytes 278560 | tf_op jit(solution)/shard_map/ppermute | solution.py:268
  39.0 3.3 %shard_map.88 = (f32[144,512]{1,0:T(8,128)S(1)}, f32[128,512]{1,0:T(8,128)S(1)}, f32[144,512]{1,0:T(8,128)S(1)}, f32[128,512]{1,0:T(8,128)S(1)}) custom-call(s32[1,2]{1,0:T(1,128)S(1)} %add_bitcast_fusion.refs_0_, bf16[128,1024]{1,0:T(8,128)(2,1)S(1)} %collective-permute-done.4.refs_1_, bf16[128,1024]{1,0:T(8,128)(2,1)S(1)} %collective-permute-done.7.refs_2_, ...), custom_call_target="tpu_custom_call" | custom-call | tf_op jit(solution)/shard_map/pallas_call | solution.py:201
  42.3 2.3 %collective-permute-done.8.refs_2_ = bf16[128,1024]{1,0:T(8,128)(2,1)S(1)} collective-permute-done((bf16[128,1024]{1,0:T(8,128)(2,1)S(1)}, bf16[128,1024]{1,0:T(8,128)(2,1)S(1)}, u32[]{:S(2)}, u32[]{:S(2)}) %collective-permute-start.8) | collective-permute-done | bytes 262176 | tf_op jit(solution)/shard_map/ppermute | solution.py:268
  46.2 3.3 %shard_map.89 = (bf16[144,512]{1,0:T(8,128)(2,1)S(1)}, f32[128,512]{1,0:T(8,128)S(1)}, f32[144,512]{1,0:T(8,128)S(1)}, bf16[128,512]{1,0:T(8,128)(2,1)S(1)}) custom-call(s32[1,2]{1,0:T(1,128)S(1)} %add_bitcast_fusion.refs_0_, bf16[128,1024]{1,0:T(8,128)(2,1)S(1)} %collective-permute-done.5.refs_1_, bf16[128,1024]{1,0:T(8,128)(2,1)S(1)} %collective-permute-done.8.refs_2_, ...), custom_call_target="tpu_custom_call" | custom-call | tf_op jit(solution)/shard_map/pallas_call | solution.py:201
  51.8 2.9 %shard_map.91 = (bf16[144,512]{1,0:T(8,128)(2,1)S(1)}, bf16[128,512]{1,0:T(8,128)(2,1)S(1)}) custom-call(s32[1,2]{1,0:T(1,128)S(1)} %add_bitcast_fusion.refs_0_, bf16[128,1024]{1,0:T(8,128)(2,1)S(1)} %collective-permute-done.13.refs_1_, bf16[136,1024]{1,0:T(8,128)(2,1)S(1)} %collective-permute-done.16.refs_2_, ...), custom_call_target="tpu_custom_call" | custom-call | tf_op jit(solution)/shard_map/pallas_call | solution.py:201
  55.0 1.6 %collective-permute-start.19 = (bf16[144,512]{1,0:T(8,128)(2,1)S(1)}, bf16[144,512]{1,0:T(8,128)(2,1)S(1)}, u32[]{:S(2)}, u32[]{:S(2)}) collective-permute-start(bf16[144,512]{1,0:T(8,128)(2,1)S(1)} %get-tuple-element.64), channel_id=1, source_target_pairs={{0,1},{4,5},{1,2},{5,6},{2,3},{6,7},{3,11},{7,15},{11,10},{15,14},... | collective-permute-start | bytes 442376 | tf_op jit(solution)/shard_map/ppermute | solution.py:268
  57.0 4.5 %collective-permute-done.20.refs_2_ = bf16[128,512]{1,0:T(8,128)(2,1)S(1)} collective-permute-done((bf16[128,512]{1,0:T(8,128)(2,1)S(1)}, bf16[128,512]{1,0:T(8,128)(2,1)S(1)}, u32[]{:S(2)}, u32[]{:S(2)}) %collective-permute-start.20) | collective-permute-done | bytes 131104 | tf_op jit(solution)/shard_map/ppermute | solution.py:268
  61.6 1.6 %collective-permute-start.21 = (bf16[144,512]{1,0:T(8,128)(2,1)S(1)}, bf16[144,512]{1,0:T(8,128)(2,1)S(1)}, u32[]{:S(2)}, u32[]{:S(2)}) collective-permute-start(bf16[144,512]{1,0:T(8,128)(2,1)S(1)} %get-tuple-element.68), channel_id=1, source_target_pairs={{0,1},{4,5},{1,2},{5,6},{2,3},{6,7},{3,11},{7,15},{11,10},{15,14},... | collective-permute-start | bytes 442376 | tf_op jit(solution)/shard_map/ppermute | solution.py:268
  63.8 1.9 %collective-permute-start.26 = (bf16[128,512]{1,0:T(8,128)(2,1)S(1)}, bf16[128,512]{1,0:T(8,128)(2,1)S(1)}, u32[]{:S(2)}, u32[]{:S(2)}) collective-permute-start(bf16[128,512]{1,0:T(8,128)(2,1)S(1)} %get-tuple-element.78), channel_id=1, source_target_pairs={{0,1},{4,5},{1,2},{5,6},{2,3},{6,7},{3,11},{7,15},{11,10},{15,14},... | collective-permute-start | bytes 393224 | tf_op jit(solution)/shard_map/ppermute | solution.py:268
  65.9 4.1 %collective-permute-done.22.refs_2_ = bf16[128,512]{1,0:T(8,128)(2,1)S(1)} collective-permute-done((bf16[128,512]{1,0:T(8,128)(2,1)S(1)}, bf16[128,512]{1,0:T(8,128)(2,1)S(1)}, u32[]{:S(2)}, u32[]{:S(2)}) %collective-permute-start.22) | collective-permute-done | bytes 131104 | tf_op jit(solution)/shard_map/ppermute | solution.py:268
  70.0 2.1 %collective-permute-start.23 = (bf16[144,512]{1,0:T(8,128)(2,1)S(1)}, bf16[144,512]{1,0:T(8,128)(2,1)S(1)}, u32[]{:S(2)}, u32[]{:S(2)}) collective-permute-start(bf16[144,512]{1,0:T(8,128)(2,1)S(1)} %get-tuple-element.72), channel_id=1, source_target_pairs={{0,1},{4,5},{1,2},{5,6},{2,3},{6,7},{3,11},{7,15},{11,10},{15,14},... | collective-permute-start | bytes 442376 | tf_op jit(solution)/shard_map/ppermute | solution.py:268
  73.3 3.7 %collective-permute-done.24.refs_2_ = bf16[128,512]{1,0:T(8,128)(2,1)S(1)} collective-permute-done((bf16[128,512]{1,0:T(8,128)(2,1)S(1)}, bf16[128,512]{1,0:T(8,128)(2,1)S(1)}, u32[]{:S(2)}, u32[]{:S(2)}) %collective-permute-start.24) | collective-permute-done | bytes 131104 | tf_op jit(solution)/shard_map/ppermute | solution.py:268
  79.9 3.8 %collective-permute-done.29.right_a = bf16[128,512]{1,0:T(8,128)(2,1)S(1)} collective-permute-done((bf16[128,512]{1,0:T(8,128)(2,1)S(1)}, bf16[128,512]{1,0:T(8,128)(2,1)S(1)}, u32[]{:S(2)}, u32[]{:S(2)}) %collective-permute-start.29) | collective-permute-done | bytes 131104 | tf_op jit(solution)/shard_map/ppermute | solution.py:268
  (63 shorter events, 16.4 us)
Async XLA Ops:
  1.2 5.9 %collective-permute-start.2 = (bf16[512,1024]{1,0:T(8,128)(2,1)}, bf16[512,1024]{1,0:T(8,128)(2,1)}, u32[]{:S(2)}, u32[]{:S(2)}) collective-permute-start(bf16[512,1024]{1,0:T(8,128)(2,1)} %bitcast.14), channel_id=1, source_target_pairs={{0,4},{4,0},{1,5},{5,1},{2,6},{6,2},{3,7},{7,3},{11,15},{15,11},{1... | collective-permute-start | bytes 3145736 | tf_op jit(solution)/shard_map/ppermute | solution.py:268
  3.4 10.1 %collective-permute-start.9 = (bf16[136,1024]{1,0:T(8,128)(2,1)S(1)}, bf16[136,1024]{1,0:T(8,128)(2,1)S(1)}, u32[]{:S(2)}, u32[]{:S(2)}) collective-permute-start(bf16[136,1024]{1,0:T(8,128)(2,1)S(1)} %constant_dynamic-update-slice_fusion.refs_2_), channel_id=1, source_target_pairs={{0,1},{4,5},{1,2},{5,6},{2,3},{6,7},{3,11},{7,15},{11,10},{15,14},... | collective-permute-start | bytes 835592 | tf_op jit(solution)/shard_map/ppermute | solution.py:268
  6.2 9.5 %collective-permute-start.11 = (bf16[136,1024]{1,0:T(8,128)(2,1)S(1)}, bf16[136,1024]{1,0:T(8,128)(2,1)S(1)}, u32[]{:S(2)}, u32[]{:S(2)}) collective-permute-start(bf16[136,1024]{1,0:T(8,128)(2,1)S(1)} %constant_dynamic-update-slice_fusion.refs_2_), channel_id=1, source_target_pairs={{0,8},{4,12},{1,0},{5,4},{2,1},{6,5},{3,2},{7,6},{11,3},{15,7},{10... | collective-permute-start | bytes 835592 | tf_op jit(solution)/shard_map/ppermute | solution.py:268
  7.2 12.0 %collective-permute-start.3 = (bf16[128,1024]{1,0:T(8,128)(2,1)S(1)}, bf16[128,1024]{1,0:T(8,128)(2,1)S(1)}, u32[]{:S(2)}, u32[]{:S(2)}) collective-permute-start(bf16[128,1024]{1,0:T(8,128)(2,1)S(1)} %copy-done), channel_id=1, source_target_pairs={{0,1},{4,5},{1,2},{5,6},{2,3},{6,7},{3,11},{7,15},{11,10},{15,14},... | collective-permute-start | bytes 786440 | tf_op jit(solution)/shard_map/ppermute | solution.py:268
  9.7 11.6 %collective-permute-start.6 = (bf16[128,1024]{1,0:T(8,128)(2,1)S(1)}, bf16[128,1024]{1,0:T(8,128)(2,1)S(1)}, u32[]{:S(2)}, u32[]{:S(2)}) collective-permute-start(bf16[128,1024]{1,0:T(8,128)(2,1)S(1)} %copy-done), channel_id=1, source_target_pairs={{0,8},{4,12},{1,0},{5,4},{2,1},{6,5},{3,2},{7,6},{11,3},{15,7},{10... | collective-permute-start | bytes 786440 | tf_op jit(solution)/shard_map/ppermute | solution.py:268
  13.6 13.7 %collective-permute-start.10 = (bf16[136,1024]{1,0:T(8,128)(2,1)S(1)}, bf16[136,1024]{1,0:T(8,128)(2,1)S(1)}, u32[]{:S(2)}, u32[]{:S(2)}) collective-permute-start(bf16[136,1024]{1,0:T(8,128)(2,1)S(1)} %collective-permute-done.9.refs_3_), channel_id=1, source_target_pairs={{0,1},{4,5},{1,2},{5,6},{2,3},{6,7},{3,11},{7,15},{11,10},{15,14},... | collective-permute-start | bytes 835592 | tf_op jit(solution)/shard_map/ppermute | solution.py:268
  15.7 11.6 %collective-permute-start.12 = (bf16[136,1024]{1,0:T(8,128)(2,1)S(1)}, bf16[136,1024]{1,0:T(8,128)(2,1)S(1)}, u32[]{:S(2)}, u32[]{:S(2)}) collective-permute-start(bf16[136,1024]{1,0:T(8,128)(2,1)S(1)} %collective-permute-done.11.refs_4_), channel_id=1, source_target_pairs={{0,8},{4,12},{1,0},{5,4},{2,1},{6,5},{3,2},{7,6},{11,3},{15,7},{10... | collective-permute-start | bytes 835592 | tf_op jit(solution)/shard_map/ppermute | solution.py:268
  19.2 11.6 %collective-permute-start.4 = (bf16[128,1024]{1,0:T(8,128)(2,1)S(1)}, bf16[128,1024]{1,0:T(8,128)(2,1)S(1)}, u32[]{:S(2)}, u32[]{:S(2)}) collective-permute-start(bf16[128,1024]{1,0:T(8,128)(2,1)S(1)} %collective-permute-done.3.refs_1_), channel_id=1, source_target_pairs={{0,1},{4,5},{1,2},{5,6},{2,3},{6,7},{3,11},{7,15},{11,10},{15,14},... | collective-permute-start | bytes 786440 | tf_op jit(solution)/shard_map/ppermute | solution.py:268
  21.3 11.6 %collective-permute-start.7 = (bf16[128,1024]{1,0:T(8,128)(2,1)S(1)}, bf16[128,1024]{1,0:T(8,128)(2,1)S(1)}, u32[]{:S(2)}, u32[]{:S(2)}) collective-permute-start(bf16[128,1024]{1,0:T(8,128)(2,1)S(1)} %collective-permute-done.6.refs_2_), channel_id=1, source_target_pairs={{0,8},{4,12},{1,0},{5,4},{2,1},{6,5},{3,2},{7,6},{11,3},{15,7},{10... | collective-permute-start | bytes 786440 | tf_op jit(solution)/shard_map/ppermute | solution.py:268
  27.3 9.6 %collective-permute-start.14 = (bf16[136,1024]{1,0:T(8,128)(2,1)S(1)}, bf16[136,1024]{1,0:T(8,128)(2,1)S(1)}, u32[]{:S(2)}, u32[]{:S(2)}) collective-permute-start(bf16[136,1024]{1,0:T(8,128)(2,1)S(1)} %collective-permute-done.10.refs_3_), channel_id=1, source_target_pairs={{0,1},{4,5},{1,2},{5,6},{2,3},{6,7},{3,11},{7,15},{11,10},{15,14},... | collective-permute-start | bytes 835592 | tf_op jit(solution)/shard_map/ppermute | solution.py:268
  29.4 9.6 %collective-permute-start.15 = (bf16[136,1024]{1,0:T(8,128)(2,1)S(1)}, bf16[136,1024]{1,0:T(8,128)(2,1)S(1)}, u32[]{:S(2)}, u32[]{:S(2)}) collective-permute-start(bf16[136,1024]{1,0:T(8,128)(2,1)S(1)} %collective-permute-done.12.refs_4_), channel_id=1, source_target_pairs={{0,8},{4,12},{1,0},{5,4},{2,1},{6,5},{3,2},{7,6},{11,3},{15,7},{10... | collective-permute-start | bytes 835592 | tf_op jit(solution)/shard_map/ppermute | solution.py:268
  30.8 11.5 %collective-permute-start.5 = (bf16[128,1024]{1,0:T(8,128)(2,1)S(1)}, bf16[128,1024]{1,0:T(8,128)(2,1)S(1)}, u32[]{:S(2)}, u32[]{:S(2)}) collective-permute-start(bf16[128,1024]{1,0:T(8,128)(2,1)S(1)} %collective-permute-done.4.refs_1_), channel_id=1, source_target_pairs={{0,1},{4,5},{1,2},{5,6},{2,3},{6,7},{3,11},{7,15},{11,10},{15,14},... | collective-permute-start | bytes 786440 | tf_op jit(solution)/shard_map/ppermute | solution.py:268
  32.9 11.7 %collective-permute-start.8 = (bf16[128,1024]{1,0:T(8,128)(2,1)S(1)}, bf16[128,1024]{1,0:T(8,128)(2,1)S(1)}, u32[]{:S(2)}, u32[]{:S(2)}) collective-permute-start(bf16[128,1024]{1,0:T(8,128)(2,1)S(1)} %collective-permute-done.7.refs_2_), channel_id=1, source_target_pairs={{0,8},{4,12},{1,0},{5,4},{2,1},{6,5},{3,2},{7,6},{11,3},{15,7},{10... | collective-permute-start | bytes 786440 | tf_op jit(solution)/shard_map/ppermute | solution.py:268
  39.0 12.8 %collective-permute-start.16 = (bf16[136,1024]{1,0:T(8,128)(2,1)S(1)}, bf16[136,1024]{1,0:T(8,128)(2,1)S(1)}, u32[]{:S(2)}, u32[]{:S(2)}) collective-permute-start(bf16[136,1024]{1,0:T(8,128)(2,1)S(1)} %collective-permute-done.15.refs_4_), channel_id=1, source_target_pairs={{0,8},{4,12},{1,0},{5,4},{2,1},{6,5},{3,2},{7,6},{11,3},{15,7},{10... | collective-permute-start | bytes 835592 | tf_op jit(solution)/shard_map/ppermute | solution.py:268
  44.6 7.2 %collective-permute-start.13 = (bf16[128,1024]{1,0:T(8,128)(2,1)S(1)}, bf16[128,1024]{1,0:T(8,128)(2,1)S(1)}, u32[]{:S(2)}, u32[]{:S(2)}) collective-permute-start(bf16[128,1024]{1,0:T(8,128)(2,1)S(1)} %collective-permute-done.5.refs_1_), channel_id=1, source_target_pairs={{0,1},{4,5},{1,2},{5,6},{2,3},{6,7},{3,11},{7,15},{11,10},{15,14},... | collective-permute-start | bytes 786440 | tf_op jit(solution)/shard_map/ppermute | solution.py:268
  55.0 6.6 %collective-permute-start.19 = (bf16[144,512]{1,0:T(8,128)(2,1)S(1)}, bf16[144,512]{1,0:T(8,128)(2,1)S(1)}, u32[]{:S(2)}, u32[]{:S(2)}) collective-permute-start(bf16[144,512]{1,0:T(8,128)(2,1)S(1)} %get-tuple-element.64), channel_id=1, source_target_pairs={{0,1},{4,5},{1,2},{5,6},{2,3},{6,7},{3,11},{7,15},{11,10},{15,14},... | collective-permute-start | bytes 442376 | tf_op jit(solution)/shard_map/ppermute | solution.py:268
  61.6 8.3 %collective-permute-start.21 = (bf16[144,512]{1,0:T(8,128)(2,1)S(1)}, bf16[144,512]{1,0:T(8,128)(2,1)S(1)}, u32[]{:S(2)}, u32[]{:S(2)}) collective-permute-start(bf16[144,512]{1,0:T(8,128)(2,1)S(1)} %get-tuple-element.68), channel_id=1, source_target_pairs={{0,1},{4,5},{1,2},{5,6},{2,3},{6,7},{3,11},{7,15},{11,10},{15,14},... | collective-permute-start | bytes 442376 | tf_op jit(solution)/shard_map/ppermute | solution.py:268
  63.3 6.7 %collective-permute-start.22 = (bf16[128,512]{1,0:T(8,128)(2,1)S(1)}, bf16[128,512]{1,0:T(8,128)(2,1)S(1)}, u32[]{:S(2)}, u32[]{:S(2)}) collective-permute-start(bf16[128,512]{1,0:T(8,128)(2,1)S(1)} %get-tuple-element.70), channel_id=1, source_target_pairs={{0,8},{4,12},{1,0},{5,4},{2,1},{6,5},{3,2},{7,6},{11,3},{15,7},{10... | collective-permute-start | bytes 393224 | tf_op jit(solution)/shard_map/ppermute | solution.py:268
  63.8 8.3 %collective-permute-start.26 = (bf16[128,512]{1,0:T(8,128)(2,1)S(1)}, bf16[128,512]{1,0:T(8,128)(2,1)S(1)}, u32[]{:S(2)}, u32[]{:S(2)}) collective-permute-start(bf16[128,512]{1,0:T(8,128)(2,1)S(1)} %get-tuple-element.78), channel_id=1, source_target_pairs={{0,1},{4,5},{1,2},{5,6},{2,3},{6,7},{3,11},{7,15},{11,10},{15,14},... | collective-permute-start | bytes 393224 | tf_op jit(solution)/shard_map/ppermute | solution.py:268
  65.7 7.2 %collective-permute-start.27 = (bf16[144,512]{1,0:T(8,128)(2,1)S(1)}, bf16[144,512]{1,0:T(8,128)(2,1)S(1)}, u32[]{:S(2)}, u32[]{:S(2)}) collective-permute-start(bf16[144,512]{1,0:T(8,128)(2,1)S(1)} %get-tuple-element.80), channel_id=1, source_target_pairs={{0,8},{4,12},{1,0},{5,4},{2,1},{6,5},{3,2},{7,6},{11,3},{15,7},{10... | collective-permute-start | bytes 442376 | tf_op jit(solution)/shard_map/ppermute | solution.py:268
  70.0 7.0 %collective-permute-start.23 = (bf16[144,512]{1,0:T(8,128)(2,1)S(1)}, bf16[144,512]{1,0:T(8,128)(2,1)S(1)}, u32[]{:S(2)}, u32[]{:S(2)}) collective-permute-start(bf16[144,512]{1,0:T(8,128)(2,1)S(1)} %get-tuple-element.72), channel_id=1, source_target_pairs={{0,1},{4,5},{1,2},{5,6},{2,3},{6,7},{3,11},{7,15},{11,10},{15,14},... | collective-permute-start | bytes 442376 | tf_op jit(solution)/shard_map/ppermute | solution.py:268
  72.9 10.8 %collective-permute-start.28 = (bf16[144,512]{1,0:T(8,128)(2,1)S(1)}, bf16[144,512]{1,0:T(8,128)(2,1)S(1)}, u32[]{:S(2)}, u32[]{:S(2)}) collective-permute-start(bf16[144,512]{1,0:T(8,128)(2,1)S(1)} %get-tuple-element.81), channel_id=1, source_target_pairs={{0,8},{4,12},{1,0},{5,4},{2,1},{6,5},{3,2},{7,6},{11,3},{15,7},{10... | collective-permute-start | bytes 442376 | tf_op jit(solution)/shard_map/ppermute | solution.py:268
  77.1 6.6 %collective-permute-start.25 = (bf16[144,512]{1,0:T(8,128)(2,1)S(1)}, bf16[144,512]{1,0:T(8,128)(2,1)S(1)}, u32[]{:S(2)}, u32[]{:S(2)}) collective-permute-start(bf16[144,512]{1,0:T(8,128)(2,1)S(1)} %get-tuple-element.76), channel_id=1, source_target_pairs={{0,1},{4,5},{1,2},{5,6},{2,3},{6,7},{3,11},{7,15},{11,10},{15,14},... | collective-permute-start | bytes 442376 | tf_op jit(solution)/shard_map/ppermute | solution.py:268
  77.9 5.9 %collective-permute-start.29 = (bf16[128,512]{1,0:T(8,128)(2,1)S(1)}, bf16[128,512]{1,0:T(8,128)(2,1)S(1)}, u32[]{:S(2)}, u32[]{:S(2)}) collective-permute-start(bf16[128,512]{1,0:T(8,128)(2,1)S(1)} %get-tuple-element.82), channel_id=1, source_target_pairs={{0,1},{4,5},{1,2},{5,6},{2,3},{6,7},{3,11},{7,15},{11,10},{15,14},... | collective-permute-start | bytes 393224 | tf_op jit(solution)/shard_map/ppermute | solution.py:268
  (10 other events, 42.8 us)

commit v5 on v4

--- a/solution.py
+++ b/solution.py
@@ -9,6 +9,7 @@
 LIGHT = pl.CostEstimate(flops=0, transcendentals=0, bytes_accessed=0)
 ADD_COST = pl.CostEstimate(flops=10**9, transcendentals=0, bytes_accessed=0)
 CONTRACT_LAST = (((1,), (1,)), ((), ()))
+LINES = 8
 
 
 def expert_grads(rows_in, grads_in, w_gate, w_up, w_down):
@@ -109,22 +110,38 @@
     return jnp.where(lax.broadcasted_iota(jnp.int32, (extra, rows), 0) == row_of, line, 0.0)
 
 
-def bf16_pieces(values):
-    pieces = []
-    for unused in range(3):
-        piece = lax.reduce_precision(values, exponent_bits=8, mantissa_bits=7)
-        values = values - piece
-        pieces.append(piece.astype(jnp.bfloat16))
-    return pieces
-
-
-def read_share(lines, expert, experts, rows):
+def lines_kernel(ids, weights, cotangent, out):
+    rows, experts = cotangent.shape[0], LINES * (cotangent.shape[1] // (3 * cotangent.shape[0]))
+    out[:rows, :] = cotangent[...]
+    out[rows:, :] = jnp.zeros((LINES, out.shape[1]), out.dtype)
+    expert = lax.broadcasted_iota(jnp.int32, (experts, rows), 0)
+    left = jnp.zeros((experts, rows), jnp.float32)
+    for k in range(ids.shape[0]):
+        left += jnp.where(expert == ids[k : k + 1, :], weights[k : k + 1, :], 0.0)
+    for piece in range(3):
+        part = left.astype(jnp.bfloat16)
+        left -= part.astype(jnp.float32)
+        for h in range(experts // LINES):
+            at = (piece * (experts // LINES) + h) * rows
+            out[rows:, at : at + rows] = part[h * LINES : (h + 1) * LINES]
+
+
+def with_lines(ids, weights, cotangent):
+    return pl.pallas_call(
+        lines_kernel,
+        out_shape=jax.ShapeDtypeStruct((cotangent.shape[0] + LINES, cotangent.shape[1]), cotangent.dtype),
+        compiler_params=pltpu.CompilerParams(vmem_limit_bytes=8 << 20),
+        cost_estimate=LIGHT,
+    )(ids.T, weights.T, cotangent)
+
+
+def read_share(lines, expert, rows):
     pieces = lines.astype(jnp.float32)
     groups = pieces.shape[1] // rows
-    slot = lax.broadcasted_iota(jnp.int32, pieces.shape, 0) * groups
-    slot = slot + lax.broadcasted_iota(jnp.int32, pieces.shape, 1) // rows
-    wanted = (slot == expert) | (slot == expert + experts) | (slot == expert + 2 * experts)
-    kept = jnp.where(wanted, pieces, 0.0)
+    sets = groups // 3
+    group = lax.broadcasted_iota(jnp.int32, pieces.shape, 1) // rows
+    line = lax.broadcasted_iota(jnp.int32, pieces.shape, 0) + LINES * (group % sets)
+    kept = jnp.where((line == expert) & (group < 3 * sets), pieces, 0.0)
     line = sum(kept[:, g * rows : (g + 1) * rows] for g in range(groups))
     line = jnp.sum(line, axis=0, keepdims=True)
     across = lax.broadcasted_iota(jnp.int32, (rows, rows), 1)
@@ -157,14 +174,14 @@
     )(*[pltpu.with_memory_space_constraint(array, pltpu.HBM) for array in arrays])
 
 
-def grads_kernel(blocks, rows, experts, extra, *refs):
+def grads_kernel(blocks, rows, extra, *refs):
     place_ref, refs = refs[0], refs[1:]
     token_refs, grad_refs, refs = refs[:blocks], refs[blocks : 2 * blocks], refs[2 * blocks :]
     weights, outs = (refs[:3], refs[3:6]), refs[6:]
     places = [jnp.max(place_ref[:, at : at + 1]) for at in range(2)]
     rows_in = jnp.concatenate([ref[...] for ref in token_refs], 0)
-    with_lines = [ref[...] for ref in grad_refs]
-    grads_in = jnp.concatenate([block[:rows] for block in with_lines], 0)
+    blocks_in = [ref[...] for ref in grad_refs]
+    grads_in = jnp.concatenate([block[:rows] for block in blocks_in], 0)
     total, spread = None, [None] * blocks
     for at, three in enumerate(weights):
         w_gate, w_up, w_down = (w[...] for w in three)
@@ -173,7 +190,7 @@
         hidden_grad = lax.dot_general(grads_in, w_down, CONTRACT_LAST, preferred_element_type=jnp.float32)
         grad_gate, grad_up, weight_grad = hidden_grads(gate_pre, up_pre, hidden_grad)
         row_terms = both_terms(grad_gate, grad_up, w_gate, w_up)
-        shares = [read_share(block[rows:], places[at], experts, rows) for block in with_lines]
+        shares = [read_share(block[rows:], places[at], rows) for block in blocks_in]
         scaled = jnp.concatenate(shares, 0) * row_terms.astype(jnp.float32)
         total = scaled if total is None else total + scaled
         for i in range(blocks):
@@ -189,7 +206,7 @@
         right[...] = block[:, half:].astype(right.dtype)
 
 
-def block_grads(places, blocks_in, weights, experts, extra, kinds):
+def block_grads(places, blocks_in, weights, extra, kinds):
     tokens, grads = zip(*blocks_in)
     blocks = len(tokens)
     rows, width = tokens[0].shape
@@ -199,7 +216,7 @@
         outs.append(jax.ShapeDtypeStruct((rows, width // 2), right))
     weights = [pltpu.with_memory_space_constraint(w, pltpu.VMEM) for w in weights]
     out = pl.pallas_call(
-        lambda *refs: grads_kernel(blocks, rows, experts, extra, *refs),
+        lambda *refs: grads_kernel(blocks, rows, extra, *refs),
         out_shape=outs,
         compiler_params=pltpu.CompilerParams(vmem_limit_bytes=24 << 20),
         cost_estimate=LIGHT,
@@ -271,17 +288,11 @@
     other = jnp.where(lax.rem(lax.axis_index("grp"), 2) == 0, me + lanes, me - lanes)
     places = jnp.stack([me, other]).reshape(1, 2)
 
-    expert_list = jnp.arange(devices, dtype=jnp.int32)
-    chosen = expert_ids[None, :, :] == expert_list[:, None, None]
-    dense = jnp.sum(jnp.where(chosen, route_weights[None], 0.0), axis=-1)
-    lines = jnp.concatenate(bf16_pieces(dense), 0)
-    line_rows = -(-3 * devices * rows // (8 * width)) * 8
-    lines = jnp.pad(lines, ((0, line_rows * width // rows - 3 * devices), (0, 0))).reshape(line_rows, width)
-    cotangent = jnp.concatenate([cotangent, lines], 0)
+    cotangent = with_lines(expert_ids, route_weights, cotangent)
     grad_up, grad_down = send(cotangent, ahead), send(cotangent, behind)
     mine = (w_gate[0], w_up[0], w_down[0])
     other = tuple(send(w, across) for w in mine)
-    second = after_all(tokens, *other)[0]
+    second = after_all(tokens, *other[:2])[0]
     token_up, token_down = send(second, ahead), send(second, behind)
     weights = hold(*mine, *other)
 
@@ -293,7 +304,7 @@
             left = jnp.bfloat16 if o in (far, far - 1) else jnp.float32
             right = jnp.bfloat16 if o in (far, chips - far + 1) else jnp.float32
             kinds.append((left, right))
-        out = block_grads(places, [(t, g) for o, t, g in blocks], weights, devices, extra, kinds)
+        out = block_grads(places, [(t, g) for o, t, g in blocks], weights, extra, kinds)
         for (o, *unused), pair in zip(blocks, out):
             sums[o] = pair
         return out[0][0]
@@ -306,7 +317,7 @@
         grad_up, grad_down = send(grad_up, ahead), send(grad_down, behind)
         arrived.append([(step, token_up, grad_up), (chips - step, token_down, grad_down)])
     grad_down = after_all(grad_down, grad_up, *[compute(arrived[o]) for o in range(1, far - 2)])[0]
-    token_up = after_all(token_up, token_down, compute(arrived[far - 2]))[0]
+    token_up = after_all(token_up, compute(arrived[far - 2]))[0]
     token_up, grad_down = send(token_up, ahead), send(grad_down, behind)
     last = compute(arrived[far - 1])
 
@@ -339,8 +350,11 @@
     experts = group_count * lax.axis_size("ep")
     rows, top_count = expert_ids.shape
     capacity = 2 * rows * top_count // experts
-    fits = rows % 128 == 0 and experts <= rows <= tokens.shape[1] // 2 and group_count % 2 == 0 and experts >= 8 and tokens.shape[1] % rows == 0
-    plan = ring_plan if fits and 2 * capacity >= rows else routed_plan
+    width = tokens.shape[1]
+    fits = rows % 128 == 0 and width % (2 * rows) == 0 and experts <= rows
+    fits = fits and experts >= 8 and experts % LINES == 0 and experts <= LINES * (width // rows // 3)
+    fits = fits and group_count % 2 == 0 and 2 * capacity >= rows
+    plan = ring_plan if fits else routed_plan
     return plan(tokens, cotangent, expert_ids, route_weights, w_gate, w_up, w_down)
 
 

time: 84.7 us -> 83.5 us (0.986)
  waiting for transfers between devices: 31.4 us -> 29 us
  starting transfers between devices: 29.6 us -> 31.3 us
    ppermute x31, waiting for transfers between devices: 31.4 us -> 29 us  [send(): return lax.ppermute(array, BOTH, pairs)]
    ppermute x31, starting transfers between devices: 29.6 us -> 31.3 us  [send(): return lax.ppermute(array, BOTH, pairs)]
    pallas_call x5 -> x6, Pallas kernels: 15.9 us -> 16.1 us  [the longest x5 16.1 us: block_grads(): pl.pallas_call(lambda *refs: grads_kernel(blocks, rows, extra, *refs), ou...]
    unnamed x7 -> x12, local copies, waits for them, and re-layouts: 2 us -> 1.97 us
  transfers between devices with their start and end apart: 31 -> 31, of which waited for: 13 -> 13; matrix products, arithmetic and copies ran while one was open for 2% -> 0% of each run, Pallas kernels for 23% -> 23%
where the time goes in v5:
time: 83.5 us; the launch traced here: 83.3 us
  starting transfers between devices  31.3 us (37%)
  waiting for transfers between devices  29 us (35%)
  Pallas kernels  20.2 us (24%)
  local copies, waits for them, and re-layouts  1.97 us (2%)
    ppermute x31, starting transfers between devices, send(): return lax.ppermute(array, BOTH, pairs)  31.3 us
    ppermute x31, waiting for transfers between devices, send(): return lax.ppermute(array, BOTH, pairs)  29 us
    pallas_call x5, Pallas kernels, block_grads(): pl.pallas_call(lambda *refs: grads_kernel(blocks, rows, extra, *refs), ou...  16.1 us
    pallas_call x1, Pallas kernels, hold(): pl.pallas_call(lambda *refs: hold_kernel(len(arrays), pieces, *refs), in_...  2.97 us
    unnamed x12, local copies, waits for them, and re-layouts  1.97 us
  transfers between devices with their start and end apart: 31, of which 13 were waited for; matrix products, arithmetic and copies ran while one was open for 0% of the time, Pallas kernels for 23%

profile of v5, /device:TPU:0, one launch (start us, length us, event | category | flops | bytes accessed | tf_op | source)
XLA Modules:
  0.0 83.3 jit_solution(6487316160062722693)
XLA Ops:
  2.7 2.7 %collective-permute-start.8 = (bf16[136,1024]{1,0:T(8,128)(2,1)S(1)}, bf16[136,1024]{1,0:T(8,128)(2,1)S(1)}, u32[]{:S(2)}, u32[]{:S(2)}) collective-permute-start(bf16[136,1024]{1,0:T(8,128)(2,1)S(1)} %shard_map.86.refs_2_), channel_id=1, source_target_pairs={{0,1},{4,5},{1,2},{5,6},{2,3},{6,7},{3,11},{7,15},{11,10},{15,14},... | collective-permute-start | bytes 835592 | tf_op jit(solution)/shard_map/ppermute | solution.py:285
  6.7 2.9 %collective-permute-start.3 = (bf16[128,1024]{1,0:T(8,128)(2,1)S(1)}, bf16[128,1024]{1,0:T(8,128)(2,1)S(1)}, u32[]{:S(2)}, u32[]{:S(2)}) collective-permute-start(bf16[128,1024]{1,0:T(8,128)(2,1)S(1)} %copy-done), channel_id=1, source_target_pairs={{0,1},{4,5},{1,2},{5,6},{2,3},{6,7},{3,11},{7,15},{11,10},{15,14},... | collective-permute-start | bytes 786440 | tf_op jit(solution)/shard_map/ppermute | solution.py:285
  9.6 3.2 %collective-permute-done.8.refs_3_ = bf16[136,1024]{1,0:T(8,128)(2,1)S(1)} collective-permute-done((bf16[136,1024]{1,0:T(8,128)(2,1)S(1)}, bf16[136,1024]{1,0:T(8,128)(2,1)S(1)}, u32[]{:S(2)}, u32[]{:S(2)}) %collective-permute-start.8) | collective-permute-done | bytes 278560 | tf_op jit(solution)/shard_map/ppermute | solution.py:285
  12.8 2.0 %collective-permute-start.9 = (bf16[136,1024]{1,0:T(8,128)(2,1)S(1)}, bf16[136,1024]{1,0:T(8,128)(2,1)S(1)}, u32[]{:S(2)}, u32[]{:S(2)}) collective-permute-start(bf16[136,1024]{1,0:T(8,128)(2,1)S(1)} %collective-permute-done.8.refs_3_), channel_id=1, source_target_pairs={{0,1},{4,5},{1,2},{5,6},{2,3},{6,7},{3,11},{7,15},{11,10},{15,14},... | collective-permute-start | bytes 835592 | tf_op jit(solution)/shard_map/ppermute | solution.py:285
  14.9 3.5 %collective-permute-done.3.refs_1_ = bf16[128,1024]{1,0:T(8,128)(2,1)S(1)} collective-permute-done((bf16[128,1024]{1,0:T(8,128)(2,1)S(1)}, bf16[128,1024]{1,0:T(8,128)(2,1)S(1)}, u32[]{:S(2)}, u32[]{:S(2)}) %collective-permute-start.3) | collective-permute-done | bytes 262176 | tf_op jit(solution)/shard_map/ppermute | solution.py:285
  18.4 2.0 %collective-permute-start.4 = (bf16[128,1024]{1,0:T(8,128)(2,1)S(1)}, bf16[128,1024]{1,0:T(8,128)(2,1)S(1)}, u32[]{:S(2)}, u32[]{:S(2)}) collective-permute-start(bf16[128,1024]{1,0:T(8,128)(2,1)S(1)} %collective-permute-done.3.refs_1_), channel_id=1, source_target_pairs={{0,1},{4,5},{1,2},{5,6},{2,3},{6,7},{3,11},{7,15},{11,10},{15,14},... | collective-permute-start | bytes 786440 | tf_op jit(solution)/shard_map/ppermute | solution.py:285
  20.6 3.0 %shard_map.87 = (bf16[1024,512]{1,0:T(8,128)(2,1)S(1)}, bf16[1024,512]{1,0:T(8,128)(2,1)S(1)}, bf16[512,1024]{1,0:T(8,128)(2,1)S(1)}, bf16[1024,512]{1,0:T(8,128...) custom-call(bf16[1024,512]{1,0:T(8,128)(2,1)} %bitcast.14, bf16[1024,512]{1,0:T(8,128)(2,1)} %bitcast.16, ...), custom_call_target="tpu_custom_call" | custom-call | tf_op jit(solution)/shard_map/pallas_call | solution.py:167
  23.6 2.9 %shard_map.88 = (f32[144,512]{1,0:T(8,128)S(1)}, f32[128,512]{1,0:T(8,128)S(1)}) custom-call(s32[1,2]{1,0:T(1,128)S(1)} %add_bitcast_fusion.refs_0_, bf16[128,1024]{1,0:T(8,128)(2,1)S(1)} %copy-done, bf16[136,1024]{1,0:T(8,128)(2,1)S(1)} %shard_map.86.refs_2_, bf16[1024,512]{1,0:T(8,128)(2,1)S(1)} %get-tuple-element.44.refs_3_.refs_5_, ...), custom_call_target="tpu_custom_call" | custom-call | tf_op jit(solution)/shard_map/pallas_call | solution.py:218
  26.5 2.1 %collective-permute-start.14 = (bf16[136,1024]{1,0:T(8,128)(2,1)S(1)}, bf16[136,1024]{1,0:T(8,128)(2,1)S(1)}, u32[]{:S(2)}, u32[]{:S(2)}) collective-permute-start(bf16[136,1024]{1,0:T(8,128)(2,1)S(1)} %collective-permute-done.9.refs_3_), channel_id=1, source_target_pairs={{0,1},{4,5},{1,2},{5,6},{2,3},{6,7},{3,11},{7,15},{11,10},{15,14},... | collective-permute-start | bytes 835592 | tf_op jit(solution)/shard_map/ppermute | solution.py:285
  30.0 2.0 %collective-permute-start.5 = (bf16[128,1024]{1,0:T(8,128)(2,1)S(1)}, bf16[128,1024]{1,0:T(8,128)(2,1)S(1)}, u32[]{:S(2)}, u32[]{:S(2)}) collective-permute-start(bf16[128,1024]{1,0:T(8,128)(2,1)S(1)} %collective-permute-done.4.refs_1_), channel_id=1, source_target_pairs={{0,1},{4,5},{1,2},{5,6},{2,3},{6,7},{3,11},{7,15},{11,10},{15,14},... | collective-permute-start | bytes 786440 | tf_op jit(solution)/shard_map/ppermute | solution.py:285
  32.1 3.4 %shard_map.91 = (f32[144,512]{1,0:T(8,128)S(1)}, f32[128,512]{1,0:T(8,128)S(1)}, f32[144,512]{1,0:T(8,128)S(1)}, f32[128,512]{1,0:T(8,128)S(1)}) custom-call(s32[1,2]{1,0:T(1,128)S(1)} %add_bitcast_fusion.refs_0_, bf16[128,1024]{1,0:T(8,128)(2,1)S(1)} %collective-permute-done.3.refs_1_, bf16[128,1024]{1,0:T(8,128)(2,1)S(1)} %collective-permute-done.6.refs_2_, ...), custom_call_target="tpu_custom_call" | custom-call | tf_op jit(solution)/shard_map/pallas_call | solution.py:218
  36.2 2.0 %collective-permute-done.15.refs_4_ = bf16[136,1024]{1,0:T(8,128)(2,1)S(1)} collective-permute-done((bf16[136,1024]{1,0:T(8,128)(2,1)S(1)}, bf16[136,1024]{1,0:T(8,128)(2,1)S(1)}, u32[]{:S(2)}, u32[]{:S(2)}) %collective-permute-start.15) | collective-permute-done | bytes 278560 | tf_op jit(solution)/shard_map/ppermute | solution.py:285
  38.2 3.4 %shard_map.89 = (f32[144,512]{1,0:T(8,128)S(1)}, f32[128,512]{1,0:T(8,128)S(1)}, f32[144,512]{1,0:T(8,128)S(1)}, f32[128,512]{1,0:T(8,128)S(1)}) custom-call(s32[1,2]{1,0:T(1,128)S(1)} %add_bitcast_fusion.refs_0_, bf16[128,1024]{1,0:T(8,128)(2,1)S(1)} %collective-permute-done.4.refs_1_, bf16[128,1024]{1,0:T(8,128)(2,1)S(1)} %collective-permute-done.7.refs_2_, ...), custom_call_target="tpu_custom_call" | custom-call | tf_op jit(solution)/shard_map/pallas_call | solution.py:218
  41.6 2.3 %collective-permute-start.12 = (bf16[128,1024]{1,0:T(8,128)(2,1)S(1)}, bf16[128,1024]{1,0:T(8,128)(2,1)S(1)}, u32[]{:S(2)}, u32[]{:S(2)}) collective-permute-start(bf16[128,1024]{1,0:T(8,128)(2,1)S(1)} %collective-permute-done.5.refs_1_), channel_id=1, source_target_pairs={{0,1},{4,5},{1,2},{5,6},{2,3},{6,7},{3,11},{7,15},{11,10},{15,14},... | collective-permute-start | bytes 786440 | tf_op jit(solution)/shard_map/ppermute | solution.py:285
  43.9 3.4 %shard_map.90 = (bf16[144,512]{1,0:T(8,128)(2,1)S(1)}, f32[128,512]{1,0:T(8,128)S(1)}, f32[144,512]{1,0:T(8,128)S(1)}, bf16[128,512]{1,0:T(8,128)(2,1)S(1)}) custom-call(s32[1,2]{1,0:T(1,128)S(1)} %add_bitcast_fusion.refs_0_, bf16[128,1024]{1,0:T(8,128)(2,1)S(1)} %collective-permute-done.5.refs_1_, bf16[128,1024]{1,0:T(8,128)(2,1)S(1)} %collective-permute-done.13.refs_2_, ...), custom_call_target="tpu_custom_call" | custom-call | tf_op jit(solution)/shard_map/pallas_call | solution.py:218
  47.4 2.0 %collective-permute-start.17 = (bf16[128,512]{1,0:T(8,128)(2,1)S(1)}, bf16[128,512]{1,0:T(8,128)(2,1)S(1)}, u32[]{:S(2)}, u32[]{:S(2)}) collective-permute-start(bf16[128,512]{1,0:T(8,128)(2,1)S(1)} %get-tuple-element.63), channel_id=1, source_target_pairs={{0,1},{4,5},{1,2},{5,6},{2,3},{6,7},{3,11},{7,15},{11,10},{15,14},... | collective-permute-start | bytes 393224 | tf_op jit(solution)/shard_map/ppermute | solution.py:285
  49.8 2.9 %shard_map.92 = (bf16[144,512]{1,0:T(8,128)(2,1)S(1)}, bf16[128,512]{1,0:T(8,128)(2,1)S(1)}) custom-call(s32[1,2]{1,0:T(1,128)S(1)} %add_bitcast_fusion.refs_0_, bf16[128,1024]{1,0:T(8,128)(2,1)S(1)} %collective-permute-done.12.refs_1_, bf16[136,1024]{1,0:T(8,128)(2,1)S(1)} %collective-permute-done.16.refs_2_, ...), custom_call_target="tpu_custom_call" | custom-call | tf_op jit(solution)/shard_map/pallas_call | solution.py:218
  52.8 1.7 %collective-permute-start.19 = (bf16[144,512]{1,0:T(8,128)(2,1)S(1)}, bf16[144,512]{1,0:T(8,128)(2,1)S(1)}, u32[]{:S(2)}, u32[]{:S(2)}) collective-permute-start(bf16[144,512]{1,0:T(8,128)(2,1)S(1)} %get-tuple-element.64), channel_id=1, source_target_pairs={{0,1},{4,5},{1,2},{5,6},{2,3},{6,7},{3,11},{7,15},{11,10},{15,14},... | collective-permute-start | bytes 442376 | tf_op jit(solution)/shard_map/ppermute | solution.py:285
  54.9 4.6 %collective-permute-done.20.refs_2_ = bf16[128,512]{1,0:T(8,128)(2,1)S(1)} collective-permute-done((bf16[128,512]{1,0:T(8,128)(2,1)S(1)}, bf16[128,512]{1,0:T(8,128)(2,1)S(1)}, u32[]{:S(2)}, u32[]{:S(2)}) %collective-permute-start.20) | collective-permute-done | bytes 131104 | tf_op jit(solution)/shard_map/ppermute | solution.py:285
  59.5 1.6 %collective-permute-start.21 = (bf16[144,512]{1,0:T(8,128)(2,1)S(1)}, bf16[144,512]{1,0:T(8,128)(2,1)S(1)}, u32[]{:S(2)}, u32[]{:S(2)}) collective-permute-start(bf16[144,512]{1,0:T(8,128)(2,1)S(1)} %get-tuple-element.68), channel_id=1, source_target_pairs={{0,1},{4,5},{1,2},{5,6},{2,3},{6,7},{3,11},{7,15},{11,10},{15,14},... | collective-permute-start | bytes 442376 | tf_op jit(solution)/shard_map/ppermute | solution.py:285
  63.8 3.2 %collective-permute-done.22.refs_2_ = bf16[128,512]{1,0:T(8,128)(2,1)S(1)} collective-permute-done((bf16[128,512]{1,0:T(8,128)(2,1)S(1)}, bf16[128,512]{1,0:T(8,128)(2,1)S(1)}, u32[]{:S(2)}, u32[]{:S(2)}) %collective-permute-start.22) | collective-permute-done | bytes 131104 | tf_op jit(solution)/shard_map/ppermute | solution.py:285
  67.0 2.1 %collective-permute-start.23 = (bf16[144,512]{1,0:T(8,128)(2,1)S(1)}, bf16[144,512]{1,0:T(8,128)(2,1)S(1)}, u32[]{:S(2)}, u32[]{:S(2)}) collective-permute-start(bf16[144,512]{1,0:T(8,128)(2,1)S(1)} %get-tuple-element.72), channel_id=1, source_target_pairs={{0,1},{4,5},{1,2},{5,6},{2,3},{6,7},{3,11},{7,15},{11,10},{15,14},... | collective-permute-start | bytes 442376 | tf_op jit(solution)/shard_map/ppermute | solution.py:285
  70.6 4.5 %collective-permute-done.24.refs_2_ = bf16[128,512]{1,0:T(8,128)(2,1)S(1)} collective-permute-done((bf16[128,512]{1,0:T(8,128)(2,1)S(1)}, bf16[128,512]{1,0:T(8,128)(2,1)S(1)}, u32[]{:S(2)}, u32[]{:S(2)}) %collective-permute-start.24) | collective-permute-done | bytes 131104 | tf_op jit(solution)/shard_map/ppermute | solution.py:285
  78.5 3.3 %collective-permute-done.29.right_a = bf16[128,512]{1,0:T(8,128)(2,1)S(1)} collective-permute-done((bf16[128,512]{1,0:T(8,128)(2,1)S(1)}, bf16[128,512]{1,0:T(8,128)(2,1)S(1)}, u32[]{:S(2)}, u32[]{:S(2)}) %collective-permute-start.29) | collective-permute-done | bytes 131104 | tf_op jit(solution)/shard_map/ppermute | solution.py:285
  (64 shorter events, 15.5 us)
Async XLA Ops:
  1.2 19.3 %collective-permute-start.2 = (bf16[512,1024]{1,0:T(8,128)(2,1)}, bf16[512,1024]{1,0:T(8,128)(2,1)}, u32[]{:S(2)}, u32[]{:S(2)}) collective-permute-start(bf16[512,1024]{1,0:T(8,128)(2,1)} %bitcast.17), channel_id=1, source_target_pairs={{0,4},{4,0},{1,5},{5,1},{2,6},{6,2},{3,7},{7,3},{11,15},{15,11},{1... | collective-permute-start | bytes 3145736 | tf_op jit(solution)/shard_map/ppermute | solution.py:285
  2.7 10.1 %collective-permute-start.8 = (bf16[136,1024]{1,0:T(8,128)(2,1)S(1)}, bf16[136,1024]{1,0:T(8,128)(2,1)S(1)}, u32[]{:S(2)}, u32[]{:S(2)}) collective-permute-start(bf16[136,1024]{1,0:T(8,128)(2,1)S(1)} %shard_map.86.refs_2_), channel_id=1, source_target_pairs={{0,1},{4,5},{1,2},{5,6},{2,3},{6,7},{3,11},{7,15},{11,10},{15,14},... | collective-permute-start | bytes 835592 | tf_op jit(solution)/shard_map/ppermute | solution.py:285
  5.4 9.5 %collective-permute-start.10 = (bf16[136,1024]{1,0:T(8,128)(2,1)S(1)}, bf16[136,1024]{1,0:T(8,128)(2,1)S(1)}, u32[]{:S(2)}, u32[]{:S(2)}) collective-permute-start(bf16[136,1024]{1,0:T(8,128)(2,1)S(1)} %shard_map.86.refs_2_), channel_id=1, source_target_pairs={{0,8},{4,12},{1,0},{5,4},{2,1},{6,5},{3,2},{7,6},{11,3},{15,7},{10... | collective-permute-start | bytes 835592 | tf_op jit(solution)/shard_map/ppermute | solution.py:285
  6.7 11.8 %collective-permute-start.3 = (bf16[128,1024]{1,0:T(8,128)(2,1)S(1)}, bf16[128,1024]{1,0:T(8,128)(2,1)S(1)}, u32[]{:S(2)}, u32[]{:S(2)}) collective-permute-start(bf16[128,1024]{1,0:T(8,128)(2,1)S(1)} %copy-done), channel_id=1, source_target_pairs={{0,1},{4,5},{1,2},{5,6},{2,3},{6,7},{3,11},{7,15},{11,10},{15,14},... | collective-permute-start | bytes 786440 | tf_op jit(solution)/shard_map/ppermute | solution.py:285
  9.6 10.9 %collective-permute-start.6 = (bf16[128,1024]{1,0:T(8,128)(2,1)S(1)}, bf16[128,1024]{1,0:T(8,128)(2,1)S(1)}, u32[]{:S(2)}, u32[]{:S(2)}) collective-permute-start(bf16[128,1024]{1,0:T(8,128)(2,1)S(1)} %copy-done), channel_id=1, source_target_pairs={{0,8},{4,12},{1,0},{5,4},{2,1},{6,5},{3,2},{7,6},{11,3},{15,7},{10... | collective-permute-start | bytes 786440 | tf_op jit(solution)/shard_map/ppermute | solution.py:285
  12.8 13.7 %collective-permute-start.9 = (bf16[136,1024]{1,0:T(8,128)(2,1)S(1)}, bf16[136,1024]{1,0:T(8,128)(2,1)S(1)}, u32[]{:S(2)}, u32[]{:S(2)}) collective-permute-start(bf16[136,1024]{1,0:T(8,128)(2,1)S(1)} %collective-permute-done.8.refs_3_), channel_id=1, source_target_pairs={{0,1},{4,5},{1,2},{5,6},{2,3},{6,7},{3,11},{7,15},{11,10},{15,14},... | collective-permute-start | bytes 835592 | tf_op jit(solution)/shard_map/ppermute | solution.py:285
  14.9 11.6 %collective-permute-start.11 = (bf16[136,1024]{1,0:T(8,128)(2,1)S(1)}, bf16[136,1024]{1,0:T(8,128)(2,1)S(1)}, u32[]{:S(2)}, u32[]{:S(2)}) collective-permute-start(bf16[136,1024]{1,0:T(8,128)(2,1)S(1)} %collective-permute-done.10.refs_4_), channel_id=1, source_target_pairs={{0,8},{4,12},{1,0},{5,4},{2,1},{6,5},{3,2},{7,6},{11,3},{15,7},{10... | collective-permute-start | bytes 835592 | tf_op jit(solution)/shard_map/ppermute | solution.py:285
  18.4 11.6 %collective-permute-start.4 = (bf16[128,1024]{1,0:T(8,128)(2,1)S(1)}, bf16[128,1024]{1,0:T(8,128)(2,1)S(1)}, u32[]{:S(2)}, u32[]{:S(2)}) collective-permute-start(bf16[128,1024]{1,0:T(8,128)(2,1)S(1)} %collective-permute-done.3.refs_1_), channel_id=1, source_target_pairs={{0,1},{4,5},{1,2},{5,6},{2,3},{6,7},{3,11},{7,15},{11,10},{15,14},... | collective-permute-start | bytes 786440 | tf_op jit(solution)/shard_map/ppermute | solution.py:285
  20.5 11.6 %collective-permute-start.7 = (bf16[128,1024]{1,0:T(8,128)(2,1)S(1)}, bf16[128,1024]{1,0:T(8,128)(2,1)S(1)}, u32[]{:S(2)}, u32[]{:S(2)}) collective-permute-start(bf16[128,1024]{1,0:T(8,128)(2,1)S(1)} %collective-permute-done.6.refs_2_), channel_id=1, source_target_pairs={{0,8},{4,12},{1,0},{5,4},{2,1},{6,5},{3,2},{7,6},{11,3},{15,7},{10... | collective-permute-start | bytes 786440 | tf_op jit(solution)/shard_map/ppermute | solution.py:285
  26.5 9.6 %collective-permute-start.14 = (bf16[136,1024]{1,0:T(8,128)(2,1)S(1)}, bf16[136,1024]{1,0:T(8,128)(2,1)S(1)}, u32[]{:S(2)}, u32[]{:S(2)}) collective-permute-start(bf16[136,1024]{1,0:T(8,128)(2,1)S(1)} %collective-permute-done.9.refs_3_), channel_id=1, source_target_pairs={{0,1},{4,5},{1,2},{5,6},{2,3},{6,7},{3,11},{7,15},{11,10},{15,14},... | collective-permute-start | bytes 835592 | tf_op jit(solution)/shard_map/ppermute | solution.py:285
  28.6 9.6 %collective-permute-start.15 = (bf16[136,1024]{1,0:T(8,128)(2,1)S(1)}, bf16[136,1024]{1,0:T(8,128)(2,1)S(1)}, u32[]{:S(2)}, u32[]{:S(2)}) collective-permute-start(bf16[136,1024]{1,0:T(8,128)(2,1)S(1)} %collective-permute-done.11.refs_4_), channel_id=1, source_target_pairs={{0,8},{4,12},{1,0},{5,4},{2,1},{6,5},{3,2},{7,6},{11,3},{15,7},{10... | collective-permute-start | bytes 835592 | tf_op jit(solution)/shard_map/ppermute | solution.py:285
  30.0 11.6 %collective-permute-start.5 = (bf16[128,1024]{1,0:T(8,128)(2,1)S(1)}, bf16[128,1024]{1,0:T(8,128)(2,1)S(1)}, u32[]{:S(2)}, u32[]{:S(2)}) collective-permute-start(bf16[128,1024]{1,0:T(8,128)(2,1)S(1)} %collective-permute-done.4.refs_1_), channel_id=1, source_target_pairs={{0,1},{4,5},{1,2},{5,6},{2,3},{6,7},{3,11},{7,15},{11,10},{15,14},... | collective-permute-start | bytes 786440 | tf_op jit(solution)/shard_map/ppermute | solution.py:285
  32.1 11.8 %collective-permute-start.13 = (bf16[128,1024]{1,0:T(8,128)(2,1)S(1)}, bf16[128,1024]{1,0:T(8,128)(2,1)S(1)}, u32[]{:S(2)}, u32[]{:S(2)}) collective-permute-start(bf16[128,1024]{1,0:T(8,128)(2,1)S(1)} %collective-permute-done.7.refs_2_), channel_id=1, source_target_pairs={{0,8},{4,12},{1,0},{5,4},{2,1},{6,5},{3,2},{7,6},{11,3},{15,7},{10... | collective-permute-start | bytes 786440 | tf_op jit(solution)/shard_map/ppermute | solution.py:285
  38.2 11.6 %collective-permute-start.16 = (bf16[136,1024]{1,0:T(8,128)(2,1)S(1)}, bf16[136,1024]{1,0:T(8,128)(2,1)S(1)}, u32[]{:S(2)}, u32[]{:S(2)}) collective-permute-start(bf16[136,1024]{1,0:T(8,128)(2,1)S(1)} %collective-permute-done.15.refs_4_), channel_id=1, source_target_pairs={{0,8},{4,12},{1,0},{5,4},{2,1},{6,5},{3,2},{7,6},{11,3},{15,7},{10... | collective-permute-start | bytes 835592 | tf_op jit(solution)/shard_map/ppermute | solution.py:285
  41.6 8.2 %collective-permute-start.12 = (bf16[128,1024]{1,0:T(8,128)(2,1)S(1)}, bf16[128,1024]{1,0:T(8,128)(2,1)S(1)}, u32[]{:S(2)}, u32[]{:S(2)}) collective-permute-start(bf16[128,1024]{1,0:T(8,128)(2,1)S(1)} %collective-permute-done.5.refs_1_), channel_id=1, source_target_pairs={{0,1},{4,5},{1,2},{5,6},{2,3},{6,7},{3,11},{7,15},{11,10},{15,14},... | collective-permute-start | bytes 786440 | tf_op jit(solution)/shard_map/ppermute | solution.py:285
  52.8 6.7 %collective-permute-start.19 = (bf16[144,512]{1,0:T(8,128)(2,1)S(1)}, bf16[144,512]{1,0:T(8,128)(2,1)S(1)}, u32[]{:S(2)}, u32[]{:S(2)}) collective-permute-start(bf16[144,512]{1,0:T(8,128)(2,1)S(1)} %get-tuple-element.64), channel_id=1, source_target_pairs={{0,1},{4,5},{1,2},{5,6},{2,3},{6,7},{3,11},{7,15},{11,10},{15,14},... | collective-permute-start | bytes 442376 | tf_op jit(solution)/shard_map/ppermute | solution.py:285
  59.5 7.4 %collective-permute-start.21 = (bf16[144,512]{1,0:T(8,128)(2,1)S(1)}, bf16[144,512]{1,0:T(8,128)(2,1)S(1)}, u32[]{:S(2)}, u32[]{:S(2)}) collective-permute-start(bf16[144,512]{1,0:T(8,128)(2,1)S(1)} %get-tuple-element.68), channel_id=1, source_target_pairs={{0,1},{4,5},{1,2},{5,6},{2,3},{6,7},{3,11},{7,15},{11,10},{15,14},... | collective-permute-start | bytes 442376 | tf_op jit(solution)/shard_map/ppermute | solution.py:285
  61.2 5.8 %collective-permute-start.22 = (bf16[128,512]{1,0:T(8,128)(2,1)S(1)}, bf16[128,512]{1,0:T(8,128)(2,1)S(1)}, u32[]{:S(2)}, u32[]{:S(2)}) collective-permute-start(bf16[128,512]{1,0:T(8,128)(2,1)S(1)} %get-tuple-element.70), channel_id=1, source_target_pairs={{0,8},{4,12},{1,0},{5,4},{2,1},{6,5},{3,2},{7,6},{11,3},{15,7},{10... | collective-permute-start | bytes 393224 | tf_op jit(solution)/shard_map/ppermute | solution.py:285
  61.7 7.5 %collective-permute-start.26 = (bf16[128,512]{1,0:T(8,128)(2,1)S(1)}, bf16[128,512]{1,0:T(8,128)(2,1)S(1)}, u32[]{:S(2)}, u32[]{:S(2)}) collective-permute-start(bf16[128,512]{1,0:T(8,128)(2,1)S(1)} %get-tuple-element.78), channel_id=1, source_target_pairs={{0,1},{4,5},{1,2},{5,6},{2,3},{6,7},{3,11},{7,15},{11,10},{15,14},... | collective-permute-start | bytes 393224 | tf_op jit(solution)/shard_map/ppermute | solution.py:285
  63.3 6.8 %collective-permute-start.27 = (bf16[144,512]{1,0:T(8,128)(2,1)S(1)}, bf16[144,512]{1,0:T(8,128)(2,1)S(1)}, u32[]{:S(2)}, u32[]{:S(2)}) collective-permute-start(bf16[144,512]{1,0:T(8,128)(2,1)S(1)} %get-tuple-element.80), channel_id=1, source_target_pairs={{0,8},{4,12},{1,0},{5,4},{2,1},{6,5},{3,2},{7,6},{11,3},{15,7},{10... | collective-permute-start | bytes 442376 | tf_op jit(solution)/shard_map/ppermute | solution.py:285
  67.0 8.1 %collective-permute-start.23 = (bf16[144,512]{1,0:T(8,128)(2,1)S(1)}, bf16[144,512]{1,0:T(8,128)(2,1)S(1)}, u32[]{:S(2)}, u32[]{:S(2)}) collective-permute-start(bf16[144,512]{1,0:T(8,128)(2,1)S(1)} %get-tuple-element.72), channel_id=1, source_target_pairs={{0,1},{4,5},{1,2},{5,6},{2,3},{6,7},{3,11},{7,15},{11,10},{15,14},... | collective-permute-start | bytes 442376 | tf_op jit(solution)/shard_map/ppermute | solution.py:285
  69.2 5.9 %collective-permute-start.24 = (bf16[128,512]{1,0:T(8,128)(2,1)S(1)}, bf16[128,512]{1,0:T(8,128)(2,1)S(1)}, u32[]{:S(2)}, u32[]{:S(2)}) collective-permute-start(bf16[128,512]{1,0:T(8,128)(2,1)S(1)} %get-tuple-element.74), channel_id=1, source_target_pairs={{0,8},{4,12},{1,0},{5,4},{2,1},{6,5},{3,2},{7,6},{11,3},{15,7},{10... | collective-permute-start | bytes 393224 | tf_op jit(solution)/shard_map/ppermute | solution.py:285
  70.2 11.6 %collective-permute-start.28 = (bf16[144,512]{1,0:T(8,128)(2,1)S(1)}, bf16[144,512]{1,0:T(8,128)(2,1)S(1)}, u32[]{:S(2)}, u32[]{:S(2)}) collective-permute-start(bf16[144,512]{1,0:T(8,128)(2,1)S(1)} %get-tuple-element.81), channel_id=1, source_target_pairs={{0,8},{4,12},{1,0},{5,4},{2,1},{6,5},{3,2},{7,6},{11,3},{15,7},{10... | collective-permute-start | bytes 442376 | tf_op jit(solution)/shard_map/ppermute | solution.py:285
  75.2 7.3 %collective-permute-start.25 = (bf16[144,512]{1,0:T(8,128)(2,1)S(1)}, bf16[144,512]{1,0:T(8,128)(2,1)S(1)}, u32[]{:S(2)}, u32[]{:S(2)}) collective-permute-start(bf16[144,512]{1,0:T(8,128)(2,1)S(1)} %get-tuple-element.76), channel_id=1, source_target_pairs={{0,1},{4,5},{1,2},{5,6},{2,3},{6,7},{3,11},{7,15},{11,10},{15,14},... | collective-permute-start | bytes 442376 | tf_op jit(solution)/shard_map/ppermute | solution.py:285
  (13 other events, 58.3 us)

commit v6 on v5

--- a/solution.py
+++ b/solution.py
@@ -9,7 +9,7 @@
 LIGHT = pl.CostEstimate(flops=0, transcendentals=0, bytes_accessed=0)
 ADD_COST = pl.CostEstimate(flops=10**9, transcendentals=0, bytes_accessed=0)
 CONTRACT_LAST = (((1,), (1,)), ((), ()))
-LINES = 8
+LINES = 16
 
 
 def expert_grads(rows_in, grads_in, w_gate, w_up, w_down):
@@ -250,9 +250,9 @@
     tokens_out[:, half:] = (right_own[...] + as_f32(right_a) + as_f32(right_b)).astype(tokens_out.dtype)
     grads = left[rows:, :rows]
     experts = lax.broadcasted_iota(jnp.int32, grads.shape, 0)
-    for k in range(ids.shape[0]):
-        picked = jnp.where(experts == ids[k : k + 1, :], grads, 0.0)
-        weights_out[k : k + 1, :] = jnp.sum(picked, axis=0, keepdims=True).astype(weights_out.dtype)
+    picked = [jnp.where(experts == ids[k : k + 1, :], grads, 0.0) for k in range(ids.shape[0])]
+    picked = jnp.concatenate([jnp.sum(lines, axis=0, keepdims=True) for lines in picked], 0)
+    weights_out[...] = picked.astype(weights_out.dtype)
 
 
 def ring_order(chips_x, lanes):

time: 83.5 us -> 84.7 us (1.014)
  waiting for transfers between devices: 29 us -> 30.7 us
  local copies, waits for them, and re-layouts: 1.97 us -> 0.97 us
    ppermute x31, waiting for transfers between devices: 29 us -> 30.7 us  [send(): return lax.ppermute(array, BOTH, pairs)]
    unnamed x12, local copies, waits for them, and re-layouts: 1.97 us -> 0.97 us
  transfers between devices with their start and end apart: 31 -> 31, of which waited for: 13 -> 14; matrix products, arithmetic and copies ran while one was open for 0% -> 0% of each run, Pallas kernels for 23% -> 23%
where the time goes in v6:
time: 84.7 us; the launch traced here: 84.6 us
  starting transfers between devices  31.8 us (38%)
  waiting for transfers between devices  30.7 us (36%)
  Pallas kernels  20.3 us (24%)
  local copies, waits for them, and re-layouts  0.97 us (1%)
    ppermute x31, starting transfers between devices, send(): return lax.ppermute(array, BOTH, pairs)  31.8 us
    ppermute x31, waiting for transfers between devices, send(): return lax.ppermute(array, BOTH, pairs)  30.7 us
    pallas_call x5, Pallas kernels, block_grads(): pl.pallas_call(lambda *refs: grads_kernel(blocks, rows, extra, *refs), ou...  16.1 us
    pallas_call x1, Pallas kernels, hold(): pl.pallas_call(lambda *refs: hold_kernel(len(arrays), pieces, *refs), in_...  2.97 us
  transfers between devices with their start and end apart: 31, of which 14 were waited for; matrix products, arithmetic and copies ran while one was open for 0% of the time, Pallas kernels for 23%

profile of v6, /device:TPU:0, one launch (start us, length us, event | category | flops | bytes accessed | tf_op | source)
XLA Modules:
  0.0 84.6 jit_solution(2655663985598684894)
XLA Ops:
  2.7 2.7 %collective-permute-start.8 = (bf16[144,1024]{1,0:T(8,128)(2,1)S(1)}, bf16[144,1024]{1,0:T(8,128)(2,1)S(1)}, u32[]{:S(2)}, u32[]{:S(2)}) collective-permute-start(bf16[144,1024]{1,0:T(8,128)(2,1)S(1)} %shard_map.86.refs_2_), channel_id=1, source_target_pairs={{0,1},{4,5},{1,2},{5,6},{2,3},{6,7},{3,11},{7,15},{11,10},{15,14},... | collective-permute-start | bytes 884744 | tf_op jit(solution)/shard_map/ppermute | solution.py:285
  6.7 2.9 %collective-permute-start.3 = (bf16[128,1024]{1,0:T(8,128)(2,1)S(1)}, bf16[128,1024]{1,0:T(8,128)(2,1)S(1)}, u32[]{:S(2)}, u32[]{:S(2)}) collective-permute-start(bf16[128,1024]{1,0:T(8,128)(2,1)S(1)} %copy-done), channel_id=1, source_target_pairs={{0,1},{4,5},{1,2},{5,6},{2,3},{6,7},{3,11},{7,15},{11,10},{15,14},... | collective-permute-start | bytes 786440 | tf_op jit(solution)/shard_map/ppermute | solution.py:285
  9.6 3.6 %collective-permute-done.8.refs_3_ = bf16[144,1024]{1,0:T(8,128)(2,1)S(1)} collective-permute-done((bf16[144,1024]{1,0:T(8,128)(2,1)S(1)}, bf16[144,1024]{1,0:T(8,128)(2,1)S(1)}, u32[]{:S(2)}, u32[]{:S(2)}) %collective-permute-start.8) | collective-permute-done | bytes 294944 | tf_op jit(solution)/shard_map/ppermute | solution.py:285
  13.2 2.0 %collective-permute-start.9 = (bf16[144,1024]{1,0:T(8,128)(2,1)S(1)}, bf16[144,1024]{1,0:T(8,128)(2,1)S(1)}, u32[]{:S(2)}, u32[]{:S(2)}) collective-permute-start(bf16[144,1024]{1,0:T(8,128)(2,1)S(1)} %collective-permute-done.8.refs_3_), channel_id=1, source_target_pairs={{0,1},{4,5},{1,2},{5,6},{2,3},{6,7},{3,11},{7,15},{11,10},{15,14},... | collective-permute-start | bytes 884744 | tf_op jit(solution)/shard_map/ppermute | solution.py:285
  15.3 3.5 %collective-permute-done.3.refs_1_ = bf16[128,1024]{1,0:T(8,128)(2,1)S(1)} collective-permute-done((bf16[128,1024]{1,0:T(8,128)(2,1)S(1)}, bf16[128,1024]{1,0:T(8,128)(2,1)S(1)}, u32[]{:S(2)}, u32[]{:S(2)}) %collective-permute-start.3) | collective-permute-done | bytes 262176 | tf_op jit(solution)/shard_map/ppermute | solution.py:285
  18.8 2.0 %collective-permute-start.4 = (bf16[128,1024]{1,0:T(8,128)(2,1)S(1)}, bf16[128,1024]{1,0:T(8,128)(2,1)S(1)}, u32[]{:S(2)}, u32[]{:S(2)}) collective-permute-start(bf16[128,1024]{1,0:T(8,128)(2,1)S(1)} %collective-permute-done.3.refs_1_), channel_id=1, source_target_pairs={{0,1},{4,5},{1,2},{5,6},{2,3},{6,7},{3,11},{7,15},{11,10},{15,14},... | collective-permute-start | bytes 786440 | tf_op jit(solution)/shard_map/ppermute | solution.py:285
  20.9 3.0 %shard_map.87 = (bf16[1024,512]{1,0:T(8,128)(2,1)S(1)}, bf16[1024,512]{1,0:T(8,128)(2,1)S(1)}, bf16[512,1024]{1,0:T(8,128)(2,1)S(1)}, bf16[1024,512]{1,0:T(8,128...) custom-call(bf16[1024,512]{1,0:T(8,128)(2,1)} %bitcast.14, bf16[1024,512]{1,0:T(8,128)(2,1)} %bitcast.16, ...), custom_call_target="tpu_custom_call" | custom-call | tf_op jit(solution)/shard_map/pallas_call | solution.py:167
  23.9 2.9 %shard_map.88 = (f32[144,512]{1,0:T(8,128)S(1)}, f32[128,512]{1,0:T(8,128)S(1)}) custom-call(s32[1,2]{1,0:T(1,128)S(1)} %add_bitcast_fusion.refs_0_, bf16[128,1024]{1,0:T(8,128)(2,1)S(1)} %copy-done, bf16[144,1024]{1,0:T(8,128)(2,1)S(1)} %shard_map.86.refs_2_, bf16[1024,512]{1,0:T(8,128)(2,1)S(1)} %get-tuple-element.44.refs_3_.refs_5_, ...), custom_call_target="tpu_custom_call" | custom-call | tf_op jit(solution)/shard_map/pallas_call | solution.py:218
  27.2 1.8 %collective-permute-start.14 = (bf16[144,1024]{1,0:T(8,128)(2,1)S(1)}, bf16[144,1024]{1,0:T(8,128)(2,1)S(1)}, u32[]{:S(2)}, u32[]{:S(2)}) collective-permute-start(bf16[144,1024]{1,0:T(8,128)(2,1)S(1)} %collective-permute-done.9.refs_3_), channel_id=1, source_target_pairs={{0,1},{4,5},{1,2},{5,6},{2,3},{6,7},{3,11},{7,15},{11,10},{15,14},... | collective-permute-start | bytes 884744 | tf_op jit(solution)/shard_map/ppermute | solution.py:285
  30.7 2.0 %collective-permute-start.5 = (bf16[128,1024]{1,0:T(8,128)(2,1)S(1)}, bf16[128,1024]{1,0:T(8,128)(2,1)S(1)}, u32[]{:S(2)}, u32[]{:S(2)}) collective-permute-start(bf16[128,1024]{1,0:T(8,128)(2,1)S(1)} %collective-permute-done.4.refs_1_), channel_id=1, source_target_pairs={{0,1},{4,5},{1,2},{5,6},{2,3},{6,7},{3,11},{7,15},{11,10},{15,14},... | collective-permute-start | bytes 786440 | tf_op jit(solution)/shard_map/ppermute | solution.py:285
  32.8 3.4 %shard_map.91 = (f32[144,512]{1,0:T(8,128)S(1)}, f32[128,512]{1,0:T(8,128)S(1)}, f32[144,512]{1,0:T(8,128)S(1)}, f32[128,512]{1,0:T(8,128)S(1)}) custom-call(s32[1,2]{1,0:T(1,128)S(1)} %add_bitcast_fusion.refs_0_, bf16[128,1024]{1,0:T(8,128)(2,1)S(1)} %collective-permute-done.3.refs_1_, bf16[128,1024]{1,0:T(8,128)(2,1)S(1)} %collective-permute-done.6.refs_2_, ...), custom_call_target="tpu_custom_call" | custom-call | tf_op jit(solution)/shard_map/pallas_call | solution.py:218
  37.1 2.0 %collective-permute-done.15.refs_4_ = bf16[144,1024]{1,0:T(8,128)(2,1)S(1)} collective-permute-done((bf16[144,1024]{1,0:T(8,128)(2,1)S(1)}, bf16[144,1024]{1,0:T(8,128)(2,1)S(1)}, u32[]{:S(2)}, u32[]{:S(2)}) %collective-permute-start.15) | collective-permute-done | bytes 294944 | tf_op jit(solution)/shard_map/ppermute | solution.py:285
  39.2 3.4 %shard_map.89 = (f32[144,512]{1,0:T(8,128)S(1)}, f32[128,512]{1,0:T(8,128)S(1)}, f32[144,512]{1,0:T(8,128)S(1)}, f32[128,512]{1,0:T(8,128)S(1)}) custom-call(s32[1,2]{1,0:T(1,128)S(1)} %add_bitcast_fusion.refs_0_, bf16[128,1024]{1,0:T(8,128)(2,1)S(1)} %collective-permute-done.4.refs_1_, bf16[128,1024]{1,0:T(8,128)(2,1)S(1)} %collective-permute-done.7.refs_2_, ...), custom_call_target="tpu_custom_call" | custom-call | tf_op jit(solution)/shard_map/pallas_call | solution.py:218
  42.6 2.2 %collective-permute-start.12 = (bf16[128,1024]{1,0:T(8,128)(2,1)S(1)}, bf16[128,1024]{1,0:T(8,128)(2,1)S(1)}, u32[]{:S(2)}, u32[]{:S(2)}) collective-permute-start(bf16[128,1024]{1,0:T(8,128)(2,1)S(1)} %collective-permute-done.5.refs_1_), channel_id=1, source_target_pairs={{0,1},{4,5},{1,2},{5,6},{2,3},{6,7},{3,11},{7,15},{11,10},{15,14},... | collective-permute-start | bytes 786440 | tf_op jit(solution)/shard_map/ppermute | solution.py:285
  44.8 3.4 %shard_map.90 = (bf16[144,512]{1,0:T(8,128)(2,1)S(1)}, f32[128,512]{1,0:T(8,128)S(1)}, f32[144,512]{1,0:T(8,128)S(1)}, bf16[128,512]{1,0:T(8,128)(2,1)S(1)}) custom-call(s32[1,2]{1,0:T(1,128)S(1)} %add_bitcast_fusion.refs_0_, bf16[128,1024]{1,0:T(8,128)(2,1)S(1)} %collective-permute-done.5.refs_1_, bf16[128,1024]{1,0:T(8,128)(2,1)S(1)} %collective-permute-done.13.refs_2_, ...), custom_call_target="tpu_custom_call" | custom-call | tf_op jit(solution)/shard_map/pallas_call | solution.py:218
  48.3 2.0 %collective-permute-start.17 = (bf16[128,512]{1,0:T(8,128)(2,1)S(1)}, bf16[128,512]{1,0:T(8,128)(2,1)S(1)}, u32[]{:S(2)}, u32[]{:S(2)}) collective-permute-start(bf16[128,512]{1,0:T(8,128)(2,1)S(1)} %get-tuple-element.63), channel_id=1, source_target_pairs={{0,1},{4,5},{1,2},{5,6},{2,3},{6,7},{3,11},{7,15},{11,10},{15,14},... | collective-permute-start | bytes 393224 | tf_op jit(solution)/shard_map/ppermute | solution.py:285
  50.9 2.9 %shard_map.92 = (bf16[144,512]{1,0:T(8,128)(2,1)S(1)}, bf16[128,512]{1,0:T(8,128)(2,1)S(1)}) custom-call(s32[1,2]{1,0:T(1,128)S(1)} %add_bitcast_fusion.refs_0_, bf16[128,1024]{1,0:T(8,128)(2,1)S(1)} %collective-permute-done.12.refs_1_, bf16[144,1024]{1,0:T(8,128)(2,1)S(1)} %collective-permute-done.16.refs_2_, ...), custom_call_target="tpu_custom_call" | custom-call | tf_op jit(solution)/shard_map/pallas_call | solution.py:218
  53.8 1.9 %collective-permute-start.19 = (bf16[144,512]{1,0:T(8,128)(2,1)S(1)}, bf16[144,512]{1,0:T(8,128)(2,1)S(1)}, u32[]{:S(2)}, u32[]{:S(2)}) collective-permute-start(bf16[144,512]{1,0:T(8,128)(2,1)S(1)} %get-tuple-element.64), channel_id=1, source_target_pairs={{0,1},{4,5},{1,2},{5,6},{2,3},{6,7},{3,11},{7,15},{11,10},{15,14},... | collective-permute-start | bytes 442376 | tf_op jit(solution)/shard_map/ppermute | solution.py:285
  55.9 4.7 %collective-permute-done.20.refs_2_ = bf16[128,512]{1,0:T(8,128)(2,1)S(1)} collective-permute-done((bf16[128,512]{1,0:T(8,128)(2,1)S(1)}, bf16[128,512]{1,0:T(8,128)(2,1)S(1)}, u32[]{:S(2)}, u32[]{:S(2)}) %collective-permute-start.20) | collective-permute-done | bytes 131104 | tf_op jit(solution)/shard_map/ppermute | solution.py:285
  62.9 1.7 %collective-permute-start.26 = (bf16[128,512]{1,0:T(8,128)(2,1)S(1)}, bf16[128,512]{1,0:T(8,128)(2,1)S(1)}, u32[]{:S(2)}, u32[]{:S(2)}) collective-permute-start(bf16[128,512]{1,0:T(8,128)(2,1)S(1)} %get-tuple-element.78), channel_id=1, source_target_pairs={{0,1},{4,5},{1,2},{5,6},{2,3},{6,7},{3,11},{7,15},{11,10},{15,14},... | collective-permute-start | bytes 393224 | tf_op jit(solution)/shard_map/ppermute | solution.py:285
  65.0 2.5 %collective-permute-done.22.refs_2_ = bf16[128,512]{1,0:T(8,128)(2,1)S(1)} collective-permute-done((bf16[128,512]{1,0:T(8,128)(2,1)S(1)}, bf16[128,512]{1,0:T(8,128)(2,1)S(1)}, u32[]{:S(2)}, u32[]{:S(2)}) %collective-permute-start.22) | collective-permute-done | bytes 131104 | tf_op jit(solution)/shard_map/ppermute | solution.py:285
  67.5 2.7 %collective-permute-start.23 = (bf16[144,512]{1,0:T(8,128)(2,1)S(1)}, bf16[144,512]{1,0:T(8,128)(2,1)S(1)}, u32[]{:S(2)}, u32[]{:S(2)}) collective-permute-start(bf16[144,512]{1,0:T(8,128)(2,1)S(1)} %get-tuple-element.72), channel_id=1, source_target_pairs={{0,1},{4,5},{1,2},{5,6},{2,3},{6,7},{3,11},{7,15},{11,10},{15,14},... | collective-permute-start | bytes 442376 | tf_op jit(solution)/shard_map/ppermute | solution.py:285
  71.8 4.6 %collective-permute-done.24.refs_2_ = bf16[128,512]{1,0:T(8,128)(2,1)S(1)} collective-permute-done((bf16[128,512]{1,0:T(8,128)(2,1)S(1)}, bf16[128,512]{1,0:T(8,128)(2,1)S(1)}, u32[]{:S(2)}, u32[]{:S(2)}) %collective-permute-start.24) | collective-permute-done | bytes 131104 | tf_op jit(solution)/shard_map/ppermute | solution.py:285
  79.6 3.4 %collective-permute-done.29.right_a = bf16[128,512]{1,0:T(8,128)(2,1)S(1)} collective-permute-done((bf16[128,512]{1,0:T(8,128)(2,1)S(1)}, bf16[128,512]{1,0:T(8,128)(2,1)S(1)}, u32[]{:S(2)}, u32[]{:S(2)}) %collective-permute-start.29) | collective-permute-done | bytes 131104 | tf_op jit(solution)/shard_map/ppermute | solution.py:285
  (64 shorter events, 16.4 us)
Async XLA Ops:
  1.2 19.7 %collective-permute-start.2 = (bf16[512,1024]{1,0:T(8,128)(2,1)}, bf16[512,1024]{1,0:T(8,128)(2,1)}, u32[]{:S(2)}, u32[]{:S(2)}) collective-permute-start(bf16[512,1024]{1,0:T(8,128)(2,1)} %bitcast.17), channel_id=1, source_target_pairs={{0,4},{4,0},{1,5},{5,1},{2,6},{6,2},{3,7},{7,3},{11,15},{15,11},{1... | collective-permute-start | bytes 3145736 | tf_op jit(solution)/shard_map/ppermute | solution.py:285
  2.7 10.5 %collective-permute-start.8 = (bf16[144,1024]{1,0:T(8,128)(2,1)S(1)}, bf16[144,1024]{1,0:T(8,128)(2,1)S(1)}, u32[]{:S(2)}, u32[]{:S(2)}) collective-permute-start(bf16[144,1024]{1,0:T(8,128)(2,1)S(1)} %shard_map.86.refs_2_), channel_id=1, source_target_pairs={{0,1},{4,5},{1,2},{5,6},{2,3},{6,7},{3,11},{7,15},{11,10},{15,14},... | collective-permute-start | bytes 884744 | tf_op jit(solution)/shard_map/ppermute | solution.py:285
  5.4 9.9 %collective-permute-start.10 = (bf16[144,1024]{1,0:T(8,128)(2,1)S(1)}, bf16[144,1024]{1,0:T(8,128)(2,1)S(1)}, u32[]{:S(2)}, u32[]{:S(2)}) collective-permute-start(bf16[144,1024]{1,0:T(8,128)(2,1)S(1)} %shard_map.86.refs_2_), channel_id=1, source_target_pairs={{0,8},{4,12},{1,0},{5,4},{2,1},{6,5},{3,2},{7,6},{11,3},{15,7},{10... | collective-permute-start | bytes 884744 | tf_op jit(solution)/shard_map/ppermute | solution.py:285
  6.7 12.1 %collective-permute-start.3 = (bf16[128,1024]{1,0:T(8,128)(2,1)S(1)}, bf16[128,1024]{1,0:T(8,128)(2,1)S(1)}, u32[]{:S(2)}, u32[]{:S(2)}) collective-permute-start(bf16[128,1024]{1,0:T(8,128)(2,1)S(1)} %copy-done), channel_id=1, source_target_pairs={{0,1},{4,5},{1,2},{5,6},{2,3},{6,7},{3,11},{7,15},{11,10},{15,14},... | collective-permute-start | bytes 786440 | tf_op jit(solution)/shard_map/ppermute | solution.py:285
  9.6 11.3 %collective-permute-start.6 = (bf16[128,1024]{1,0:T(8,128)(2,1)S(1)}, bf16[128,1024]{1,0:T(8,128)(2,1)S(1)}, u32[]{:S(2)}, u32[]{:S(2)}) collective-permute-start(bf16[128,1024]{1,0:T(8,128)(2,1)S(1)} %copy-done), channel_id=1, source_target_pairs={{0,8},{4,12},{1,0},{5,4},{2,1},{6,5},{3,2},{7,6},{11,3},{15,7},{10... | collective-permute-start | bytes 786440 | tf_op jit(solution)/shard_map/ppermute | solution.py:285
  13.2 13.7 %collective-permute-start.9 = (bf16[144,1024]{1,0:T(8,128)(2,1)S(1)}, bf16[144,1024]{1,0:T(8,128)(2,1)S(1)}, u32[]{:S(2)}, u32[]{:S(2)}) collective-permute-start(bf16[144,1024]{1,0:T(8,128)(2,1)S(1)} %collective-permute-done.8.refs_3_), channel_id=1, source_target_pairs={{0,1},{4,5},{1,2},{5,6},{2,3},{6,7},{3,11},{7,15},{11,10},{15,14},... | collective-permute-start | bytes 884744 | tf_op jit(solution)/shard_map/ppermute | solution.py:285
  15.2 11.9 %collective-permute-start.11 = (bf16[144,1024]{1,0:T(8,128)(2,1)S(1)}, bf16[144,1024]{1,0:T(8,128)(2,1)S(1)}, u32[]{:S(2)}, u32[]{:S(2)}) collective-permute-start(bf16[144,1024]{1,0:T(8,128)(2,1)S(1)} %collective-permute-done.10.refs_4_), channel_id=1, source_target_pairs={{0,8},{4,12},{1,0},{5,4},{2,1},{6,5},{3,2},{7,6},{11,3},{15,7},{10... | collective-permute-start | bytes 884744 | tf_op jit(solution)/shard_map/ppermute | solution.py:285
  18.8 11.9 %collective-permute-start.4 = (bf16[128,1024]{1,0:T(8,128)(2,1)S(1)}, bf16[128,1024]{1,0:T(8,128)(2,1)S(1)}, u32[]{:S(2)}, u32[]{:S(2)}) collective-permute-start(bf16[128,1024]{1,0:T(8,128)(2,1)S(1)} %collective-permute-done.3.refs_1_), channel_id=1, source_target_pairs={{0,1},{4,5},{1,2},{5,6},{2,3},{6,7},{3,11},{7,15},{11,10},{15,14},... | collective-permute-start | bytes 786440 | tf_op jit(solution)/shard_map/ppermute | solution.py:285
  20.9 11.9 %collective-permute-start.7 = (bf16[128,1024]{1,0:T(8,128)(2,1)S(1)}, bf16[128,1024]{1,0:T(8,128)(2,1)S(1)}, u32[]{:S(2)}, u32[]{:S(2)}) collective-permute-start(bf16[128,1024]{1,0:T(8,128)(2,1)S(1)} %collective-permute-done.6.refs_2_), channel_id=1, source_target_pairs={{0,8},{4,12},{1,0},{5,4},{2,1},{6,5},{3,2},{7,6},{11,3},{15,7},{10... | collective-permute-start | bytes 786440 | tf_op jit(solution)/shard_map/ppermute | solution.py:285
  27.2 9.9 %collective-permute-start.14 = (bf16[144,1024]{1,0:T(8,128)(2,1)S(1)}, bf16[144,1024]{1,0:T(8,128)(2,1)S(1)}, u32[]{:S(2)}, u32[]{:S(2)}) collective-permute-start(bf16[144,1024]{1,0:T(8,128)(2,1)S(1)} %collective-permute-done.9.refs_3_), channel_id=1, source_target_pairs={{0,1},{4,5},{1,2},{5,6},{2,3},{6,7},{3,11},{7,15},{11,10},{15,14},... | collective-permute-start | bytes 884744 | tf_op jit(solution)/shard_map/ppermute | solution.py:285
  29.0 10.2 %collective-permute-start.15 = (bf16[144,1024]{1,0:T(8,128)(2,1)S(1)}, bf16[144,1024]{1,0:T(8,128)(2,1)S(1)}, u32[]{:S(2)}, u32[]{:S(2)}) collective-permute-start(bf16[144,1024]{1,0:T(8,128)(2,1)S(1)} %collective-permute-done.11.refs_4_), channel_id=1, source_target_pairs={{0,8},{4,12},{1,0},{5,4},{2,1},{6,5},{3,2},{7,6},{11,3},{15,7},{10... | collective-permute-start | bytes 884744 | tf_op jit(solution)/shard_map/ppermute | solution.py:285
  30.7 11.8 %collective-permute-start.5 = (bf16[128,1024]{1,0:T(8,128)(2,1)S(1)}, bf16[128,1024]{1,0:T(8,128)(2,1)S(1)}, u32[]{:S(2)}, u32[]{:S(2)}) collective-permute-start(bf16[128,1024]{1,0:T(8,128)(2,1)S(1)} %collective-permute-done.4.refs_1_), channel_id=1, source_target_pairs={{0,1},{4,5},{1,2},{5,6},{2,3},{6,7},{3,11},{7,15},{11,10},{15,14},... | collective-permute-start | bytes 786440 | tf_op jit(solution)/shard_map/ppermute | solution.py:285
  32.8 12.0 %collective-permute-start.13 = (bf16[128,1024]{1,0:T(8,128)(2,1)S(1)}, bf16[128,1024]{1,0:T(8,128)(2,1)S(1)}, u32[]{:S(2)}, u32[]{:S(2)}) collective-permute-start(bf16[128,1024]{1,0:T(8,128)(2,1)S(1)} %collective-permute-done.7.refs_2_), channel_id=1, source_target_pairs={{0,8},{4,12},{1,0},{5,4},{2,1},{6,5},{3,2},{7,6},{11,3},{15,7},{10... | collective-permute-start | bytes 786440 | tf_op jit(solution)/shard_map/ppermute | solution.py:285
  39.1 11.7 %collective-permute-start.16 = (bf16[144,1024]{1,0:T(8,128)(2,1)S(1)}, bf16[144,1024]{1,0:T(8,128)(2,1)S(1)}, u32[]{:S(2)}, u32[]{:S(2)}) collective-permute-start(bf16[144,1024]{1,0:T(8,128)(2,1)S(1)} %collective-permute-done.15.refs_4_), channel_id=1, source_target_pairs={{0,8},{4,12},{1,0},{5,4},{2,1},{6,5},{3,2},{7,6},{11,3},{15,7},{10... | collective-permute-start | bytes 884744 | tf_op jit(solution)/shard_map/ppermute | solution.py:285
  42.6 8.3 %collective-permute-start.12 = (bf16[128,1024]{1,0:T(8,128)(2,1)S(1)}, bf16[128,1024]{1,0:T(8,128)(2,1)S(1)}, u32[]{:S(2)}, u32[]{:S(2)}) collective-permute-start(bf16[128,1024]{1,0:T(8,128)(2,1)S(1)} %collective-permute-done.5.refs_1_), channel_id=1, source_target_pairs={{0,1},{4,5},{1,2},{5,6},{2,3},{6,7},{3,11},{7,15},{11,10},{15,14},... | collective-permute-start | bytes 786440 | tf_op jit(solution)/shard_map/ppermute | solution.py:285
  48.2 5.6 %collective-permute-start.18 = (bf16[144,512]{1,0:T(8,128)(2,1)S(1)}, bf16[144,512]{1,0:T(8,128)(2,1)S(1)}, u32[]{:S(2)}, u32[]{:S(2)}) collective-permute-start(bf16[144,512]{1,0:T(8,128)(2,1)S(1)} %get-tuple-element.57), channel_id=1, source_target_pairs={{0,8},{4,12},{1,0},{5,4},{2,1},{6,5},{3,2},{7,6},{11,3},{15,7},{10... | collective-permute-start | bytes 442376 | tf_op jit(solution)/shard_map/ppermute | solution.py:285
  53.8 6.8 %collective-permute-start.19 = (bf16[144,512]{1,0:T(8,128)(2,1)S(1)}, bf16[144,512]{1,0:T(8,128)(2,1)S(1)}, u32[]{:S(2)}, u32[]{:S(2)}) collective-permute-start(bf16[144,512]{1,0:T(8,128)(2,1)S(1)} %get-tuple-element.64), channel_id=1, source_target_pairs={{0,1},{4,5},{1,2},{5,6},{2,3},{6,7},{3,11},{7,15},{11,10},{15,14},... | collective-permute-start | bytes 442376 | tf_op jit(solution)/shard_map/ppermute | solution.py:285
  60.7 6.7 %collective-permute-start.21 = (bf16[144,512]{1,0:T(8,128)(2,1)S(1)}, bf16[144,512]{1,0:T(8,128)(2,1)S(1)}, u32[]{:S(2)}, u32[]{:S(2)}) collective-permute-start(bf16[144,512]{1,0:T(8,128)(2,1)S(1)} %get-tuple-element.68), channel_id=1, source_target_pairs={{0,1},{4,5},{1,2},{5,6},{2,3},{6,7},{3,11},{7,15},{11,10},{15,14},... | collective-permute-start | bytes 442376 | tf_op jit(solution)/shard_map/ppermute | solution.py:285
  62.9 7.4 %collective-permute-start.26 = (bf16[128,512]{1,0:T(8,128)(2,1)S(1)}, bf16[128,512]{1,0:T(8,128)(2,1)S(1)}, u32[]{:S(2)}, u32[]{:S(2)}) collective-permute-start(bf16[128,512]{1,0:T(8,128)(2,1)S(1)} %get-tuple-element.78), channel_id=1, source_target_pairs={{0,1},{4,5},{1,2},{5,6},{2,3},{6,7},{3,11},{7,15},{11,10},{15,14},... | collective-permute-start | bytes 393224 | tf_op jit(solution)/shard_map/ppermute | solution.py:285
  64.5 6.7 %collective-permute-start.27 = (bf16[144,512]{1,0:T(8,128)(2,1)S(1)}, bf16[144,512]{1,0:T(8,128)(2,1)S(1)}, u32[]{:S(2)}, u32[]{:S(2)}) collective-permute-start(bf16[144,512]{1,0:T(8,128)(2,1)S(1)} %get-tuple-element.80), channel_id=1, source_target_pairs={{0,8},{4,12},{1,0},{5,4},{2,1},{6,5},{3,2},{7,6},{11,3},{15,7},{10... | collective-permute-start | bytes 442376 | tf_op jit(solution)/shard_map/ppermute | solution.py:285
  67.5 8.8 %collective-permute-start.23 = (bf16[144,512]{1,0:T(8,128)(2,1)S(1)}, bf16[144,512]{1,0:T(8,128)(2,1)S(1)}, u32[]{:S(2)}, u32[]{:S(2)}) collective-permute-start(bf16[144,512]{1,0:T(8,128)(2,1)S(1)} %get-tuple-element.72), channel_id=1, source_target_pairs={{0,1},{4,5},{1,2},{5,6},{2,3},{6,7},{3,11},{7,15},{11,10},{15,14},... | collective-permute-start | bytes 442376 | tf_op jit(solution)/shard_map/ppermute | solution.py:285
  70.2 6.1 %collective-permute-start.24 = (bf16[128,512]{1,0:T(8,128)(2,1)S(1)}, bf16[128,512]{1,0:T(8,128)(2,1)S(1)}, u32[]{:S(2)}, u32[]{:S(2)}) collective-permute-start(bf16[128,512]{1,0:T(8,128)(2,1)S(1)} %get-tuple-element.74), channel_id=1, source_target_pairs={{0,8},{4,12},{1,0},{5,4},{2,1},{6,5},{3,2},{7,6},{11,3},{15,7},{10... | collective-permute-start | bytes 393224 | tf_op jit(solution)/shard_map/ppermute | solution.py:285
  71.3 11.7 %collective-permute-start.28 = (bf16[144,512]{1,0:T(8,128)(2,1)S(1)}, bf16[144,512]{1,0:T(8,128)(2,1)S(1)}, u32[]{:S(2)}, u32[]{:S(2)}) collective-permute-start(bf16[144,512]{1,0:T(8,128)(2,1)S(1)} %get-tuple-element.81), channel_id=1, source_target_pairs={{0,8},{4,12},{1,0},{5,4},{2,1},{6,5},{3,2},{7,6},{11,3},{15,7},{10... | collective-permute-start | bytes 442376 | tf_op jit(solution)/shard_map/ppermute | solution.py:285
  76.4 7.3 %collective-permute-start.25 = (bf16[144,512]{1,0:T(8,128)(2,1)S(1)}, bf16[144,512]{1,0:T(8,128)(2,1)S(1)}, u32[]{:S(2)}, u32[]{:S(2)}) collective-permute-start(bf16[144,512]{1,0:T(8,128)(2,1)S(1)} %get-tuple-element.76), channel_id=1, source_target_pairs={{0,1},{4,5},{1,2},{5,6},{2,3},{6,7},{3,11},{7,15},{11,10},{15,14},... | collective-permute-start | bytes 442376 | tf_op jit(solution)/shard_map/ppermute | solution.py:285
  (13 other events, 70.8 us)

commit v7 on v6

--- a/solution.py
+++ b/solution.py
@@ -9,7 +9,7 @@
 LIGHT = pl.CostEstimate(flops=0, transcendentals=0, bytes_accessed=0)
 ADD_COST = pl.CostEstimate(flops=10**9, transcendentals=0, bytes_accessed=0)
 CONTRACT_LAST = (((1,), (1,)), ((), ()))
-LINES = 16
+LINES = 8
 
 
 def expert_grads(rows_in, grads_in, w_gate, w_up, w_down):
@@ -112,18 +112,18 @@
 
 def lines_kernel(ids, weights, cotangent, out):
     rows, experts = cotangent.shape[0], LINES * (cotangent.shape[1] // (3 * cotangent.shape[0]))
-    out[:rows, :] = cotangent[...]
-    out[rows:, :] = jnp.zeros((LINES, out.shape[1]), out.dtype)
     expert = lax.broadcasted_iota(jnp.int32, (experts, rows), 0)
     left = jnp.zeros((experts, rows), jnp.float32)
     for k in range(ids.shape[0]):
         left += jnp.where(expert == ids[k : k + 1, :], weights[k : k + 1, :], 0.0)
-    for piece in range(3):
-        part = left.astype(jnp.bfloat16)
-        left -= part.astype(jnp.float32)
-        for h in range(experts // LINES):
-            at = (piece * (experts // LINES) + h) * rows
-            out[rows:, at : at + rows] = part[h * LINES : (h + 1) * LINES]
+    parts = []
+    for unused in range(3):
+        part = left.astype(jnp.bfloat16).astype(jnp.float32)
+        left -= part
+        parts += [part[at : at + LINES] for at in range(0, experts, LINES)]
+    room = out.shape[1] - len(parts) * rows
+    lines = jnp.concatenate(parts + [jnp.zeros((LINES, room), jnp.float32)] * (room > 0), 1)
+    out[...] = jnp.concatenate([cotangent[...], lines.astype(out.dtype)], 0)
 
 
 def with_lines(ids, weights, cotangent):

time: 84.7 us -> 83.5 us (0.986)
  waiting for transfers between devices: 30.7 us -> 29 us
  local copies, waits for them, and re-layouts: 0.97 us -> 1.97 us
    ppermute x31, waiting for transfers between devices: 30.7 us -> 29 us  [send(): return lax.ppermute(array, BOTH, pairs)]
    unnamed x12, local copies, waits for them, and re-layouts: 0.97 us -> 1.97 us
  transfers between devices with their start and end apart: 31 -> 31, of which waited for: 14 -> 13; matrix products, arithmetic and copies ran while one was open for 0% -> 0% of each run, Pallas kernels for 23% -> 23%
where the time goes in v7:
time: 83.5 us; the launch traced here: 83.3 us
  starting transfers between devices  31.3 us (37%)
  waiting for transfers between devices  29 us (35%)
  Pallas kernels  20.2 us (24%)
  local copies, waits for them, and re-layouts  1.97 us (2%)
    ppermute x31, starting transfers between devices, send(): return lax.ppermute(array, BOTH, pairs)  31.3 us
    ppermute x31, waiting for transfers between devices, send(): return lax.ppermute(array, BOTH, pairs)  29 us
    pallas_call x5, Pallas kernels, block_grads(): pl.pallas_call(lambda *refs: grads_kernel(blocks, rows, extra, *refs), ou...  16.1 us
    pallas_call x1, Pallas kernels, hold(): pl.pallas_call(lambda *refs: hold_kernel(len(arrays), pieces, *refs), in_...  2.97 us
    unnamed x12, local copies, waits for them, and re-layouts  1.97 us
  transfers between devices with their start and end apart: 31, of which 13 were waited for; matrix products, arithmetic and copies ran while one was open for 0% of the time, Pallas kernels for 23%

profile of v7, /device:TPU:0, one launch (start us, length us, event | category | flops | bytes accessed | tf_op | source)
XLA Modules:
  0.0 83.3 jit_solution(5199731036435005807)
XLA Ops:
  2.7 2.7 %collective-permute-start.8 = (bf16[136,1024]{1,0:T(8,128)(2,1)S(1)}, bf16[136,1024]{1,0:T(8,128)(2,1)S(1)}, u32[]{:S(2)}, u32[]{:S(2)}) collective-permute-start(bf16[136,1024]{1,0:T(8,128)(2,1)S(1)} %shard_map.86.refs_2_), channel_id=1, source_target_pairs={{0,1},{4,5},{1,2},{5,6},{2,3},{6,7},{3,11},{7,15},{11,10},{15,14},... | collective-permute-start | bytes 835592 | tf_op jit(solution)/shard_map/ppermute | solution.py:285
  6.7 2.9 %collective-permute-start.3 = (bf16[128,1024]{1,0:T(8,128)(2,1)S(1)}, bf16[128,1024]{1,0:T(8,128)(2,1)S(1)}, u32[]{:S(2)}, u32[]{:S(2)}) collective-permute-start(bf16[128,1024]{1,0:T(8,128)(2,1)S(1)} %copy-done), channel_id=1, source_target_pairs={{0,1},{4,5},{1,2},{5,6},{2,3},{6,7},{3,11},{7,15},{11,10},{15,14},... | collective-permute-start | bytes 786440 | tf_op jit(solution)/shard_map/ppermute | solution.py:285
  9.6 3.2 %collective-permute-done.8.refs_3_ = bf16[136,1024]{1,0:T(8,128)(2,1)S(1)} collective-permute-done((bf16[136,1024]{1,0:T(8,128)(2,1)S(1)}, bf16[136,1024]{1,0:T(8,128)(2,1)S(1)}, u32[]{:S(2)}, u32[]{:S(2)}) %collective-permute-start.8) | collective-permute-done | bytes 278560 | tf_op jit(solution)/shard_map/ppermute | solution.py:285
  12.8 2.0 %collective-permute-start.9 = (bf16[136,1024]{1,0:T(8,128)(2,1)S(1)}, bf16[136,1024]{1,0:T(8,128)(2,1)S(1)}, u32[]{:S(2)}, u32[]{:S(2)}) collective-permute-start(bf16[136,1024]{1,0:T(8,128)(2,1)S(1)} %collective-permute-done.8.refs_3_), channel_id=1, source_target_pairs={{0,1},{4,5},{1,2},{5,6},{2,3},{6,7},{3,11},{7,15},{11,10},{15,14},... | collective-permute-start | bytes 835592 | tf_op jit(solution)/shard_map/ppermute | solution.py:285
  14.9 3.5 %collective-permute-done.3.refs_1_ = bf16[128,1024]{1,0:T(8,128)(2,1)S(1)} collective-permute-done((bf16[128,1024]{1,0:T(8,128)(2,1)S(1)}, bf16[128,1024]{1,0:T(8,128)(2,1)S(1)}, u32[]{:S(2)}, u32[]{:S(2)}) %collective-permute-start.3) | collective-permute-done | bytes 262176 | tf_op jit(solution)/shard_map/ppermute | solution.py:285
  18.4 2.0 %collective-permute-start.4 = (bf16[128,1024]{1,0:T(8,128)(2,1)S(1)}, bf16[128,1024]{1,0:T(8,128)(2,1)S(1)}, u32[]{:S(2)}, u32[]{:S(2)}) collective-permute-start(bf16[128,1024]{1,0:T(8,128)(2,1)S(1)} %collective-permute-done.3.refs_1_), channel_id=1, source_target_pairs={{0,1},{4,5},{1,2},{5,6},{2,3},{6,7},{3,11},{7,15},{11,10},{15,14},... | collective-permute-start | bytes 786440 | tf_op jit(solution)/shard_map/ppermute | solution.py:285
  20.6 3.0 %shard_map.87 = (bf16[1024,512]{1,0:T(8,128)(2,1)S(1)}, bf16[1024,512]{1,0:T(8,128)(2,1)S(1)}, bf16[512,1024]{1,0:T(8,128)(2,1)S(1)}, bf16[1024,512]{1,0:T(8,128...) custom-call(bf16[1024,512]{1,0:T(8,128)(2,1)} %bitcast.14, bf16[1024,512]{1,0:T(8,128)(2,1)} %bitcast.16, ...), custom_call_target="tpu_custom_call" | custom-call | tf_op jit(solution)/shard_map/pallas_call | solution.py:167
  23.6 2.9 %shard_map.88 = (f32[144,512]{1,0:T(8,128)S(1)}, f32[128,512]{1,0:T(8,128)S(1)}) custom-call(s32[1,2]{1,0:T(1,128)S(1)} %add_bitcast_fusion.refs_0_, bf16[128,1024]{1,0:T(8,128)(2,1)S(1)} %copy-done, bf16[136,1024]{1,0:T(8,128)(2,1)S(1)} %shard_map.86.refs_2_, bf16[1024,512]{1,0:T(8,128)(2,1)S(1)} %get-tuple-element.44.refs_3_.refs_5_, ...), custom_call_target="tpu_custom_call" | custom-call | tf_op jit(solution)/shard_map/pallas_call | solution.py:218
  26.5 2.1 %collective-permute-start.14 = (bf16[136,1024]{1,0:T(8,128)(2,1)S(1)}, bf16[136,1024]{1,0:T(8,128)(2,1)S(1)}, u32[]{:S(2)}, u32[]{:S(2)}) collective-permute-start(bf16[136,1024]{1,0:T(8,128)(2,1)S(1)} %collective-permute-done.9.refs_3_), channel_id=1, source_target_pairs={{0,1},{4,5},{1,2},{5,6},{2,3},{6,7},{3,11},{7,15},{11,10},{15,14},... | collective-permute-start | bytes 835592 | tf_op jit(solution)/shard_map/ppermute | solution.py:285
  30.0 2.0 %collective-permute-start.5 = (bf16[128,1024]{1,0:T(8,128)(2,1)S(1)}, bf16[128,1024]{1,0:T(8,128)(2,1)S(1)}, u32[]{:S(2)}, u32[]{:S(2)}) collective-permute-start(bf16[128,1024]{1,0:T(8,128)(2,1)S(1)} %collective-permute-done.4.refs_1_), channel_id=1, source_target_pairs={{0,1},{4,5},{1,2},{5,6},{2,3},{6,7},{3,11},{7,15},{11,10},{15,14},... | collective-permute-start | bytes 786440 | tf_op jit(solution)/shard_map/ppermute | solution.py:285
  32.1 3.4 %shard_map.91 = (f32[144,512]{1,0:T(8,128)S(1)}, f32[128,512]{1,0:T(8,128)S(1)}, f32[144,512]{1,0:T(8,128)S(1)}, f32[128,512]{1,0:T(8,128)S(1)}) custom-call(s32[1,2]{1,0:T(1,128)S(1)} %add_bitcast_fusion.refs_0_, bf16[128,1024]{1,0:T(8,128)(2,1)S(1)} %collective-permute-done.3.refs_1_, bf16[128,1024]{1,0:T(8,128)(2,1)S(1)} %collective-permute-done.6.refs_2_, ...), custom_call_target="tpu_custom_call" | custom-call | tf_op jit(solution)/shard_map/pallas_call | solution.py:218
  36.2 2.0 %collective-permute-done.15.refs_4_ = bf16[136,1024]{1,0:T(8,128)(2,1)S(1)} collective-permute-done((bf16[136,1024]{1,0:T(8,128)(2,1)S(1)}, bf16[136,1024]{1,0:T(8,128)(2,1)S(1)}, u32[]{:S(2)}, u32[]{:S(2)}) %collective-permute-start.15) | collective-permute-done | bytes 278560 | tf_op jit(solution)/shard_map/ppermute | solution.py:285
  38.2 3.4 %shard_map.89 = (f32[144,512]{1,0:T(8,128)S(1)}, f32[128,512]{1,0:T(8,128)S(1)}, f32[144,512]{1,0:T(8,128)S(1)}, f32[128,512]{1,0:T(8,128)S(1)}) custom-call(s32[1,2]{1,0:T(1,128)S(1)} %add_bitcast_fusion.refs_0_, bf16[128,1024]{1,0:T(8,128)(2,1)S(1)} %collective-permute-done.4.refs_1_, bf16[128,1024]{1,0:T(8,128)(2,1)S(1)} %collective-permute-done.7.refs_2_, ...), custom_call_target="tpu_custom_call" | custom-call | tf_op jit(solution)/shard_map/pallas_call | solution.py:218
  41.6 2.3 %collective-permute-start.12 = (bf16[128,1024]{1,0:T(8,128)(2,1)S(1)}, bf16[128,1024]{1,0:T(8,128)(2,1)S(1)}, u32[]{:S(2)}, u32[]{:S(2)}) collective-permute-start(bf16[128,1024]{1,0:T(8,128)(2,1)S(1)} %collective-permute-done.5.refs_1_), channel_id=1, source_target_pairs={{0,1},{4,5},{1,2},{5,6},{2,3},{6,7},{3,11},{7,15},{11,10},{15,14},... | collective-permute-start | bytes 786440 | tf_op jit(solution)/shard_map/ppermute | solution.py:285
  43.9 3.4 %shard_map.90 = (bf16[144,512]{1,0:T(8,128)(2,1)S(1)}, f32[128,512]{1,0:T(8,128)S(1)}, f32[144,512]{1,0:T(8,128)S(1)}, bf16[128,512]{1,0:T(8,128)(2,1)S(1)}) custom-call(s32[1,2]{1,0:T(1,128)S(1)} %add_bitcast_fusion.refs_0_, bf16[128,1024]{1,0:T(8,128)(2,1)S(1)} %collective-permute-done.5.refs_1_, bf16[128,1024]{1,0:T(8,128)(2,1)S(1)} %collective-permute-done.13.refs_2_, ...), custom_call_target="tpu_custom_call" | custom-call | tf_op jit(solution)/shard_map/pallas_call | solution.py:218
  47.4 2.0 %collective-permute-start.17 = (bf16[128,512]{1,0:T(8,128)(2,1)S(1)}, bf16[128,512]{1,0:T(8,128)(2,1)S(1)}, u32[]{:S(2)}, u32[]{:S(2)}) collective-permute-start(bf16[128,512]{1,0:T(8,128)(2,1)S(1)} %get-tuple-element.63), channel_id=1, source_target_pairs={{0,1},{4,5},{1,2},{5,6},{2,3},{6,7},{3,11},{7,15},{11,10},{15,14},... | collective-permute-start | bytes 393224 | tf_op jit(solution)/shard_map/ppermute | solution.py:285
  49.8 2.9 %shard_map.92 = (bf16[144,512]{1,0:T(8,128)(2,1)S(1)}, bf16[128,512]{1,0:T(8,128)(2,1)S(1)}) custom-call(s32[1,2]{1,0:T(1,128)S(1)} %add_bitcast_fusion.refs_0_, bf16[128,1024]{1,0:T(8,128)(2,1)S(1)} %collective-permute-done.12.refs_1_, bf16[136,1024]{1,0:T(8,128)(2,1)S(1)} %collective-permute-done.16.refs_2_, ...), custom_call_target="tpu_custom_call" | custom-call | tf_op jit(solution)/shard_map/pallas_call | solution.py:218
  52.8 1.7 %collective-permute-start.19 = (bf16[144,512]{1,0:T(8,128)(2,1)S(1)}, bf16[144,512]{1,0:T(8,128)(2,1)S(1)}, u32[]{:S(2)}, u32[]{:S(2)}) collective-permute-start(bf16[144,512]{1,0:T(8,128)(2,1)S(1)} %get-tuple-element.64), channel_id=1, source_target_pairs={{0,1},{4,5},{1,2},{5,6},{2,3},{6,7},{3,11},{7,15},{11,10},{15,14},... | collective-permute-start | bytes 442376 | tf_op jit(solution)/shard_map/ppermute | solution.py:285
  54.9 4.6 %collective-permute-done.20.refs_2_ = bf16[128,512]{1,0:T(8,128)(2,1)S(1)} collective-permute-done((bf16[128,512]{1,0:T(8,128)(2,1)S(1)}, bf16[128,512]{1,0:T(8,128)(2,1)S(1)}, u32[]{:S(2)}, u32[]{:S(2)}) %collective-permute-start.20) | collective-permute-done | bytes 131104 | tf_op jit(solution)/shard_map/ppermute | solution.py:285
  59.5 1.6 %collective-permute-start.21 = (bf16[144,512]{1,0:T(8,128)(2,1)S(1)}, bf16[144,512]{1,0:T(8,128)(2,1)S(1)}, u32[]{:S(2)}, u32[]{:S(2)}) collective-permute-start(bf16[144,512]{1,0:T(8,128)(2,1)S(1)} %get-tuple-element.68), channel_id=1, source_target_pairs={{0,1},{4,5},{1,2},{5,6},{2,3},{6,7},{3,11},{7,15},{11,10},{15,14},... | collective-permute-start | bytes 442376 | tf_op jit(solution)/shard_map/ppermute | solution.py:285
  63.8 3.2 %collective-permute-done.22.refs_2_ = bf16[128,512]{1,0:T(8,128)(2,1)S(1)} collective-permute-done((bf16[128,512]{1,0:T(8,128)(2,1)S(1)}, bf16[128,512]{1,0:T(8,128)(2,1)S(1)}, u32[]{:S(2)}, u32[]{:S(2)}) %collective-permute-start.22) | collective-permute-done | bytes 131104 | tf_op jit(solution)/shard_map/ppermute | solution.py:285
  67.0 2.1 %collective-permute-start.23 = (bf16[144,512]{1,0:T(8,128)(2,1)S(1)}, bf16[144,512]{1,0:T(8,128)(2,1)S(1)}, u32[]{:S(2)}, u32[]{:S(2)}) collective-permute-start(bf16[144,512]{1,0:T(8,128)(2,1)S(1)} %get-tuple-element.72), channel_id=1, source_target_pairs={{0,1},{4,5},{1,2},{5,6},{2,3},{6,7},{3,11},{7,15},{11,10},{15,14},... | collective-permute-start | bytes 442376 | tf_op jit(solution)/shard_map/ppermute | solution.py:285
  70.6 4.5 %collective-permute-done.24.refs_2_ = bf16[128,512]{1,0:T(8,128)(2,1)S(1)} collective-permute-done((bf16[128,512]{1,0:T(8,128)(2,1)S(1)}, bf16[128,512]{1,0:T(8,128)(2,1)S(1)}, u32[]{:S(2)}, u32[]{:S(2)}) %collective-permute-start.24) | collective-permute-done | bytes 131104 | tf_op jit(solution)/shard_map/ppermute | solution.py:285
  78.5 3.3 %collective-permute-done.29.right_a = bf16[128,512]{1,0:T(8,128)(2,1)S(1)} collective-permute-done((bf16[128,512]{1,0:T(8,128)(2,1)S(1)}, bf16[128,512]{1,0:T(8,128)(2,1)S(1)}, u32[]{:S(2)}, u32[]{:S(2)}) %collective-permute-start.29) | collective-permute-done | bytes 131104 | tf_op jit(solution)/shard_map/ppermute | solution.py:285
  (64 shorter events, 15.5 us)
Async XLA Ops:
  1.2 19.3 %collective-permute-start.2 = (bf16[512,1024]{1,0:T(8,128)(2,1)}, bf16[512,1024]{1,0:T(8,128)(2,1)}, u32[]{:S(2)}, u32[]{:S(2)}) collective-permute-start(bf16[512,1024]{1,0:T(8,128)(2,1)} %bitcast.17), channel_id=1, source_target_pairs={{0,4},{4,0},{1,5},{5,1},{2,6},{6,2},{3,7},{7,3},{11,15},{15,11},{1... | collective-permute-start | bytes 3145736 | tf_op jit(solution)/shard_map/ppermute | solution.py:285
  2.7 10.1 %collective-permute-start.8 = (bf16[136,1024]{1,0:T(8,128)(2,1)S(1)}, bf16[136,1024]{1,0:T(8,128)(2,1)S(1)}, u32[]{:S(2)}, u32[]{:S(2)}) collective-permute-start(bf16[136,1024]{1,0:T(8,128)(2,1)S(1)} %shard_map.86.refs_2_), channel_id=1, source_target_pairs={{0,1},{4,5},{1,2},{5,6},{2,3},{6,7},{3,11},{7,15},{11,10},{15,14},... | collective-permute-start | bytes 835592 | tf_op jit(solution)/shard_map/ppermute | solution.py:285
  5.4 9.5 %collective-permute-start.10 = (bf16[136,1024]{1,0:T(8,128)(2,1)S(1)}, bf16[136,1024]{1,0:T(8,128)(2,1)S(1)}, u32[]{:S(2)}, u32[]{:S(2)}) collective-permute-start(bf16[136,1024]{1,0:T(8,128)(2,1)S(1)} %shard_map.86.refs_2_), channel_id=1, source_target_pairs={{0,8},{4,12},{1,0},{5,4},{2,1},{6,5},{3,2},{7,6},{11,3},{15,7},{10... | collective-permute-start | bytes 835592 | tf_op jit(solution)/shard_map/ppermute | solution.py:285
  6.7 11.8 %collective-permute-start.3 = (bf16[128,1024]{1,0:T(8,128)(2,1)S(1)}, bf16[128,1024]{1,0:T(8,128)(2,1)S(1)}, u32[]{:S(2)}, u32[]{:S(2)}) collective-permute-start(bf16[128,1024]{1,0:T(8,128)(2,1)S(1)} %copy-done), channel_id=1, source_target_pairs={{0,1},{4,5},{1,2},{5,6},{2,3},{6,7},{3,11},{7,15},{11,10},{15,14},... | collective-permute-start | bytes 786440 | tf_op jit(solution)/shard_map/ppermute | solution.py:285
  9.6 10.9 %collective-permute-start.6 = (bf16[128,1024]{1,0:T(8,128)(2,1)S(1)}, bf16[128,1024]{1,0:T(8,128)(2,1)S(1)}, u32[]{:S(2)}, u32[]{:S(2)}) collective-permute-start(bf16[128,1024]{1,0:T(8,128)(2,1)S(1)} %copy-done), channel_id=1, source_target_pairs={{0,8},{4,12},{1,0},{5,4},{2,1},{6,5},{3,2},{7,6},{11,3},{15,7},{10... | collective-permute-start | bytes 786440 | tf_op jit(solution)/shard_map/ppermute | solution.py:285
  12.8 13.7 %collective-permute-start.9 = (bf16[136,1024]{1,0:T(8,128)(2,1)S(1)}, bf16[136,1024]{1,0:T(8,128)(2,1)S(1)}, u32[]{:S(2)}, u32[]{:S(2)}) collective-permute-start(bf16[136,1024]{1,0:T(8,128)(2,1)S(1)} %collective-permute-done.8.refs_3_), channel_id=1, source_target_pairs={{0,1},{4,5},{1,2},{5,6},{2,3},{6,7},{3,11},{7,15},{11,10},{15,14},... | collective-permute-start | bytes 835592 | tf_op jit(solution)/shard_map/ppermute | solution.py:285
  14.9 11.6 %collective-permute-start.11 = (bf16[136,1024]{1,0:T(8,128)(2,1)S(1)}, bf16[136,1024]{1,0:T(8,128)(2,1)S(1)}, u32[]{:S(2)}, u32[]{:S(2)}) collective-permute-start(bf16[136,1024]{1,0:T(8,128)(2,1)S(1)} %collective-permute-done.10.refs_4_), channel_id=1, source_target_pairs={{0,8},{4,12},{1,0},{5,4},{2,1},{6,5},{3,2},{7,6},{11,3},{15,7},{10... | collective-permute-start | bytes 835592 | tf_op jit(solution)/shard_map/ppermute | solution.py:285
  18.4 11.6 %collective-permute-start.4 = (bf16[128,1024]{1,0:T(8,128)(2,1)S(1)}, bf16[128,1024]{1,0:T(8,128)(2,1)S(1)}, u32[]{:S(2)}, u32[]{:S(2)}) collective-permute-start(bf16[128,1024]{1,0:T(8,128)(2,1)S(1)} %collective-permute-done.3.refs_1_), channel_id=1, source_target_pairs={{0,1},{4,5},{1,2},{5,6},{2,3},{6,7},{3,11},{7,15},{11,10},{15,14},... | collective-permute-start | bytes 786440 | tf_op jit(solution)/shard_map/ppermute | solution.py:285
  20.5 11.6 %collective-permute-start.7 = (bf16[128,1024]{1,0:T(8,128)(2,1)S(1)}, bf16[128,1024]{1,0:T(8,128)(2,1)S(1)}, u32[]{:S(2)}, u32[]{:S(2)}) collective-permute-start(bf16[128,1024]{1,0:T(8,128)(2,1)S(1)} %collective-permute-done.6.refs_2_), channel_id=1, source_target_pairs={{0,8},{4,12},{1,0},{5,4},{2,1},{6,5},{3,2},{7,6},{11,3},{15,7},{10... | collective-permute-start | bytes 786440 | tf_op jit(solution)/shard_map/ppermute | solution.py:285
  26.5 9.6 %collective-permute-start.14 = (bf16[136,1024]{1,0:T(8,128)(2,1)S(1)}, bf16[136,1024]{1,0:T(8,128)(2,1)S(1)}, u32[]{:S(2)}, u32[]{:S(2)}) collective-permute-start(bf16[136,1024]{1,0:T(8,128)(2,1)S(1)} %collective-permute-done.9.refs_3_), channel_id=1, source_target_pairs={{0,1},{4,5},{1,2},{5,6},{2,3},{6,7},{3,11},{7,15},{11,10},{15,14},... | collective-permute-start | bytes 835592 | tf_op jit(solution)/shard_map/ppermute | solution.py:285
  28.6 9.6 %collective-permute-start.15 = (bf16[136,1024]{1,0:T(8,128)(2,1)S(1)}, bf16[136,1024]{1,0:T(8,128)(2,1)S(1)}, u32[]{:S(2)}, u32[]{:S(2)}) collective-permute-start(bf16[136,1024]{1,0:T(8,128)(2,1)S(1)} %collective-permute-done.11.refs_4_), channel_id=1, source_target_pairs={{0,8},{4,12},{1,0},{5,4},{2,1},{6,5},{3,2},{7,6},{11,3},{15,7},{10... | collective-permute-start | bytes 835592 | tf_op jit(solution)/shard_map/ppermute | solution.py:285
  30.0 11.6 %collective-permute-start.5 = (bf16[128,1024]{1,0:T(8,128)(2,1)S(1)}, bf16[128,1024]{1,0:T(8,128)(2,1)S(1)}, u32[]{:S(2)}, u32[]{:S(2)}) collective-permute-start(bf16[128,1024]{1,0:T(8,128)(2,1)S(1)} %collective-permute-done.4.refs_1_), channel_id=1, source_target_pairs={{0,1},{4,5},{1,2},{5,6},{2,3},{6,7},{3,11},{7,15},{11,10},{15,14},... | collective-permute-start | bytes 786440 | tf_op jit(solution)/shard_map/ppermute | solution.py:285
  32.1 11.8 %collective-permute-start.13 = (bf16[128,1024]{1,0:T(8,128)(2,1)S(1)}, bf16[128,1024]{1,0:T(8,128)(2,1)S(1)}, u32[]{:S(2)}, u32[]{:S(2)}) collective-permute-start(bf16[128,1024]{1,0:T(8,128)(2,1)S(1)} %collective-permute-done.7.refs_2_), channel_id=1, source_target_pairs={{0,8},{4,12},{1,0},{5,4},{2,1},{6,5},{3,2},{7,6},{11,3},{15,7},{10... | collective-permute-start | bytes 786440 | tf_op jit(solution)/shard_map/ppermute | solution.py:285
  38.2 11.6 %collective-permute-start.16 = (bf16[136,1024]{1,0:T(8,128)(2,1)S(1)}, bf16[136,1024]{1,0:T(8,128)(2,1)S(1)}, u32[]{:S(2)}, u32[]{:S(2)}) collective-permute-start(bf16[136,1024]{1,0:T(8,128)(2,1)S(1)} %collective-permute-done.15.refs_4_), channel_id=1, source_target_pairs={{0,8},{4,12},{1,0},{5,4},{2,1},{6,5},{3,2},{7,6},{11,3},{15,7},{10... | collective-permute-start | bytes 835592 | tf_op jit(solution)/shard_map/ppermute | solution.py:285
  41.6 8.2 %collective-permute-start.12 = (bf16[128,1024]{1,0:T(8,128)(2,1)S(1)}, bf16[128,1024]{1,0:T(8,128)(2,1)S(1)}, u32[]{:S(2)}, u32[]{:S(2)}) collective-permute-start(bf16[128,1024]{1,0:T(8,128)(2,1)S(1)} %collective-permute-done.5.refs_1_), channel_id=1, source_target_pairs={{0,1},{4,5},{1,2},{5,6},{2,3},{6,7},{3,11},{7,15},{11,10},{15,14},... | collective-permute-start | bytes 786440 | tf_op jit(solution)/shard_map/ppermute | solution.py:285
  52.8 6.7 %collective-permute-start.19 = (bf16[144,512]{1,0:T(8,128)(2,1)S(1)}, bf16[144,512]{1,0:T(8,128)(2,1)S(1)}, u32[]{:S(2)}, u32[]{:S(2)}) collective-permute-start(bf16[144,512]{1,0:T(8,128)(2,1)S(1)} %get-tuple-element.64), channel_id=1, source_target_pairs={{0,1},{4,5},{1,2},{5,6},{2,3},{6,7},{3,11},{7,15},{11,10},{15,14},... | collective-permute-start | bytes 442376 | tf_op jit(solution)/shard_map/ppermute | solution.py:285
  59.5 7.4 %collective-permute-start.21 = (bf16[144,512]{1,0:T(8,128)(2,1)S(1)}, bf16[144,512]{1,0:T(8,128)(2,1)S(1)}, u32[]{:S(2)}, u32[]{:S(2)}) collective-permute-start(bf16[144,512]{1,0:T(8,128)(2,1)S(1)} %get-tuple-element.68), channel_id=1, source_target_pairs={{0,1},{4,5},{1,2},{5,6},{2,3},{6,7},{3,11},{7,15},{11,10},{15,14},... | collective-permute-start | bytes 442376 | tf_op jit(solution)/shard_map/ppermute | solution.py:285
  61.2 5.8 %collective-permute-start.22 = (bf16[128,512]{1,0:T(8,128)(2,1)S(1)}, bf16[128,512]{1,0:T(8,128)(2,1)S(1)}, u32[]{:S(2)}, u32[]{:S(2)}) collective-permute-start(bf16[128,512]{1,0:T(8,128)(2,1)S(1)} %get-tuple-element.70), channel_id=1, source_target_pairs={{0,8},{4,12},{1,0},{5,4},{2,1},{6,5},{3,2},{7,6},{11,3},{15,7},{10... | collective-permute-start | bytes 393224 | tf_op jit(solution)/shard_map/ppermute | solution.py:285
  61.7 7.5 %collective-permute-start.26 = (bf16[128,512]{1,0:T(8,128)(2,1)S(1)}, bf16[128,512]{1,0:T(8,128)(2,1)S(1)}, u32[]{:S(2)}, u32[]{:S(2)}) collective-permute-start(bf16[128,512]{1,0:T(8,128)(2,1)S(1)} %get-tuple-element.78), channel_id=1, source_target_pairs={{0,1},{4,5},{1,2},{5,6},{2,3},{6,7},{3,11},{7,15},{11,10},{15,14},... | collective-permute-start | bytes 393224 | tf_op jit(solution)/shard_map/ppermute | solution.py:285
  63.3 6.8 %collective-permute-start.27 = (bf16[144,512]{1,0:T(8,128)(2,1)S(1)}, bf16[144,512]{1,0:T(8,128)(2,1)S(1)}, u32[]{:S(2)}, u32[]{:S(2)}) collective-permute-start(bf16[144,512]{1,0:T(8,128)(2,1)S(1)} %get-tuple-element.80), channel_id=1, source_target_pairs={{0,8},{4,12},{1,0},{5,4},{2,1},{6,5},{3,2},{7,6},{11,3},{15,7},{10... | collective-permute-start | bytes 442376 | tf_op jit(solution)/shard_map/ppermute | solution.py:285
  67.0 8.1 %collective-permute-start.23 = (bf16[144,512]{1,0:T(8,128)(2,1)S(1)}, bf16[144,512]{1,0:T(8,128)(2,1)S(1)}, u32[]{:S(2)}, u32[]{:S(2)}) collective-permute-start(bf16[144,512]{1,0:T(8,128)(2,1)S(1)} %get-tuple-element.72), channel_id=1, source_target_pairs={{0,1},{4,5},{1,2},{5,6},{2,3},{6,7},{3,11},{7,15},{11,10},{15,14},... | collective-permute-start | bytes 442376 | tf_op jit(solution)/shard_map/ppermute | solution.py:285
  69.2 5.9 %collective-permute-start.24 = (bf16[128,512]{1,0:T(8,128)(2,1)S(1)}, bf16[128,512]{1,0:T(8,128)(2,1)S(1)}, u32[]{:S(2)}, u32[]{:S(2)}) collective-permute-start(bf16[128,512]{1,0:T(8,128)(2,1)S(1)} %get-tuple-element.74), channel_id=1, source_target_pairs={{0,8},{4,12},{1,0},{5,4},{2,1},{6,5},{3,2},{7,6},{11,3},{15,7},{10... | collective-permute-start | bytes 393224 | tf_op jit(solution)/shard_map/ppermute | solution.py:285
  70.2 11.6 %collective-permute-start.28 = (bf16[144,512]{1,0:T(8,128)(2,1)S(1)}, bf16[144,512]{1,0:T(8,128)(2,1)S(1)}, u32[]{:S(2)}, u32[]{:S(2)}) collective-permute-start(bf16[144,512]{1,0:T(8,128)(2,1)S(1)} %get-tuple-element.81), channel_id=1, source_target_pairs={{0,8},{4,12},{1,0},{5,4},{2,1},{6,5},{3,2},{7,6},{11,3},{15,7},{10... | collective-permute-start | bytes 442376 | tf_op jit(solution)/shard_map/ppermute | solution.py:285
  75.2 7.3 %collective-permute-start.25 = (bf16[144,512]{1,0:T(8,128)(2,1)S(1)}, bf16[144,512]{1,0:T(8,128)(2,1)S(1)}, u32[]{:S(2)}, u32[]{:S(2)}) collective-permute-start(bf16[144,512]{1,0:T(8,128)(2,1)S(1)} %get-tuple-element.76), channel_id=1, source_target_pairs={{0,1},{4,5},{1,2},{5,6},{2,3},{6,7},{3,11},{7,15},{11,10},{15,14},... | collective-permute-start | bytes 442376 | tf_op jit(solution)/shard_map/ppermute | solution.py:285
  (13 other events, 58.3 us)

commit v8 on v7

--- a/solution.py
+++ b/solution.py
@@ -163,7 +163,7 @@
         copy.wait()
 
 
-def hold(*arrays, pieces=4):
+def hold(*arrays, pieces=8):
     return pl.pallas_call(
         lambda *refs: hold_kernel(len(arrays), pieces, *refs),
         in_specs=[pl.BlockSpec(memory_space=pltpu.HBM)] * len(arrays),

time: 83.5 us -> 83.5 us (level)
  waiting for transfers between devices: 29 us -> 27.8 us
  starting transfers between devices: 31.3 us -> 32.2 us
    ppermute x31, waiting for transfers between devices: 29 us -> 27.8 us  [send(): return lax.ppermute(array, BOTH, pairs)]
    ppermute x31, starting transfers between devices: 31.3 us -> 32.2 us  [send(): return lax.ppermute(array, BOTH, pairs)]
  transfers between devices with their start and end apart: 31 -> 31, of which waited for: 13 -> 14; matrix products, arithmetic and copies ran while one was open for 0% -> 0% of each run, Pallas kernels for 23% -> 24%
where the time goes in v8:
time: 83.5 us; the launch traced here: 83.3 us
  starting transfers between devices  32.2 us (39%)
  waiting for transfers between devices  27.8 us (33%)
  Pallas kernels  20.5 us (25%)
  local copies, waits for them, and re-layouts  1.97 us (2%)
    ppermute x31, starting transfers between devices, send(): return lax.ppermute(array, BOTH, pairs)  32.2 us
    ppermute x31, waiting for transfers between devices, send(): return lax.ppermute(array, BOTH, pairs)  27.8 us
    pallas_call x5, Pallas kernels, block_grads(): pl.pallas_call(lambda *refs: grads_kernel(blocks, rows, extra, *refs), ou...  16.1 us
    pallas_call x1, Pallas kernels, hold(): pl.pallas_call(lambda *refs: hold_kernel(len(arrays), pieces, *refs), in_...  3.27 us
    unnamed x12, local copies, waits for them, and re-layouts  1.97 us
  transfers between devices with their start and end apart: 31, of which 14 were waited for; matrix products, arithmetic and copies ran while one was open for 0% of the time, Pallas kernels for 24%

profile of v8, /device:TPU:0, one launch (start us, length us, event | category | flops | bytes accessed | tf_op | source)
XLA Modules:
  0.0 83.3 jit_solution(6955005121891158221)
XLA Ops:
  2.7 2.7 %collective-permute-start.8 = (bf16[136,1024]{1,0:T(8,128)(2,1)S(1)}, bf16[136,1024]{1,0:T(8,128)(2,1)S(1)}, u32[]{:S(2)}, u32[]{:S(2)}) collective-permute-start(bf16[136,1024]{1,0:T(8,128)(2,1)S(1)} %shard_map.86.refs_2_), channel_id=1, source_target_pairs={{0,1},{4,5},{1,2},{5,6},{2,3},{6,7},{3,11},{7,15},{11,10},{15,14},... | collective-permute-start | bytes 835592 | tf_op jit(solution)/shard_map/ppermute | solution.py:285
  6.7 2.9 %collective-permute-start.3 = (bf16[128,1024]{1,0:T(8,128)(2,1)S(1)}, bf16[128,1024]{1,0:T(8,128)(2,1)S(1)}, u32[]{:S(2)}, u32[]{:S(2)}) collective-permute-start(bf16[128,1024]{1,0:T(8,128)(2,1)S(1)} %copy-done), channel_id=1, source_target_pairs={{0,1},{4,5},{1,2},{5,6},{2,3},{6,7},{3,11},{7,15},{11,10},{15,14},... | collective-permute-start | bytes 786440 | tf_op jit(solution)/shard_map/ppermute | solution.py:285
  9.6 3.2 %collective-permute-done.8.refs_3_ = bf16[136,1024]{1,0:T(8,128)(2,1)S(1)} collective-permute-done((bf16[136,1024]{1,0:T(8,128)(2,1)S(1)}, bf16[136,1024]{1,0:T(8,128)(2,1)S(1)}, u32[]{:S(2)}, u32[]{:S(2)}) %collective-permute-start.8) | collective-permute-done | bytes 278560 | tf_op jit(solution)/shard_map/ppermute | solution.py:285
  12.8 2.0 %collective-permute-start.9 = (bf16[136,1024]{1,0:T(8,128)(2,1)S(1)}, bf16[136,1024]{1,0:T(8,128)(2,1)S(1)}, u32[]{:S(2)}, u32[]{:S(2)}) collective-permute-start(bf16[136,1024]{1,0:T(8,128)(2,1)S(1)} %collective-permute-done.8.refs_3_), channel_id=1, source_target_pairs={{0,1},{4,5},{1,2},{5,6},{2,3},{6,7},{3,11},{7,15},{11,10},{15,14},... | collective-permute-start | bytes 835592 | tf_op jit(solution)/shard_map/ppermute | solution.py:285
  14.9 3.5 %collective-permute-done.3.refs_1_ = bf16[128,1024]{1,0:T(8,128)(2,1)S(1)} collective-permute-done((bf16[128,1024]{1,0:T(8,128)(2,1)S(1)}, bf16[128,1024]{1,0:T(8,128)(2,1)S(1)}, u32[]{:S(2)}, u32[]{:S(2)}) %collective-permute-start.3) | collective-permute-done | bytes 262176 | tf_op jit(solution)/shard_map/ppermute | solution.py:285
  18.4 2.0 %collective-permute-start.4 = (bf16[128,1024]{1,0:T(8,128)(2,1)S(1)}, bf16[128,1024]{1,0:T(8,128)(2,1)S(1)}, u32[]{:S(2)}, u32[]{:S(2)}) collective-permute-start(bf16[128,1024]{1,0:T(8,128)(2,1)S(1)} %collective-permute-done.3.refs_1_), channel_id=1, source_target_pairs={{0,1},{4,5},{1,2},{5,6},{2,3},{6,7},{3,11},{7,15},{11,10},{15,14},... | collective-permute-start | bytes 786440 | tf_op jit(solution)/shard_map/ppermute | solution.py:285
  20.6 3.3 %shard_map.87 = (bf16[1024,512]{1,0:T(8,128)(2,1)S(1)}, bf16[1024,512]{1,0:T(8,128)(2,1)S(1)}, bf16[512,1024]{1,0:T(8,128)(2,1)S(1)}, bf16[1024,512]{1,0:T(8,128...) custom-call(bf16[1024,512]{1,0:T(8,128)(2,1)} %bitcast.14, bf16[1024,512]{1,0:T(8,128)(2,1)} %bitcast.16, ...), custom_call_target="tpu_custom_call" | custom-call | tf_op jit(solution)/shard_map/pallas_call | solution.py:167
  23.9 2.9 %shard_map.88 = (f32[144,512]{1,0:T(8,128)S(1)}, f32[128,512]{1,0:T(8,128)S(1)}) custom-call(s32[1,2]{1,0:T(1,128)S(1)} %add_bitcast_fusion.refs_0_, bf16[128,1024]{1,0:T(8,128)(2,1)S(1)} %copy-done, bf16[136,1024]{1,0:T(8,128)(2,1)S(1)} %shard_map.86.refs_2_, bf16[1024,512]{1,0:T(8,128)(2,1)S(1)} %get-tuple-element.44.refs_3_.refs_5_, ...), custom_call_target="tpu_custom_call" | custom-call | tf_op jit(solution)/shard_map/pallas_call | solution.py:218
  26.8 2.1 %collective-permute-start.14 = (bf16[136,1024]{1,0:T(8,128)(2,1)S(1)}, bf16[136,1024]{1,0:T(8,128)(2,1)S(1)}, u32[]{:S(2)}, u32[]{:S(2)}) collective-permute-start(bf16[136,1024]{1,0:T(8,128)(2,1)S(1)} %collective-permute-done.9.refs_3_), channel_id=1, source_target_pairs={{0,1},{4,5},{1,2},{5,6},{2,3},{6,7},{3,11},{7,15},{11,10},{15,14},... | collective-permute-start | bytes 835592 | tf_op jit(solution)/shard_map/ppermute | solution.py:285
  30.0 2.0 %collective-permute-start.5 = (bf16[128,1024]{1,0:T(8,128)(2,1)S(1)}, bf16[128,1024]{1,0:T(8,128)(2,1)S(1)}, u32[]{:S(2)}, u32[]{:S(2)}) collective-permute-start(bf16[128,1024]{1,0:T(8,128)(2,1)S(1)} %collective-permute-done.4.refs_1_), channel_id=1, source_target_pairs={{0,1},{4,5},{1,2},{5,6},{2,3},{6,7},{3,11},{7,15},{11,10},{15,14},... | collective-permute-start | bytes 786440 | tf_op jit(solution)/shard_map/ppermute | solution.py:285
  32.1 3.4 %shard_map.91 = (f32[144,512]{1,0:T(8,128)S(1)}, f32[128,512]{1,0:T(8,128)S(1)}, f32[144,512]{1,0:T(8,128)S(1)}, f32[128,512]{1,0:T(8,128)S(1)}) custom-call(s32[1,2]{1,0:T(1,128)S(1)} %add_bitcast_fusion.refs_0_, bf16[128,1024]{1,0:T(8,128)(2,1)S(1)} %collective-permute-done.3.refs_1_, bf16[128,1024]{1,0:T(8,128)(2,1)S(1)} %collective-permute-done.6.refs_2_, ...), custom_call_target="tpu_custom_call" | custom-call | tf_op jit(solution)/shard_map/pallas_call | solution.py:218
  36.5 2.0 %collective-permute-done.15.refs_4_ = bf16[136,1024]{1,0:T(8,128)(2,1)S(1)} collective-permute-done((bf16[136,1024]{1,0:T(8,128)(2,1)S(1)}, bf16[136,1024]{1,0:T(8,128)(2,1)S(1)}, u32[]{:S(2)}, u32[]{:S(2)}) %collective-permute-start.15) | collective-permute-done | bytes 278560 | tf_op jit(solution)/shard_map/ppermute | solution.py:285
  38.5 3.4 %shard_map.89 = (f32[144,512]{1,0:T(8,128)S(1)}, f32[128,512]{1,0:T(8,128)S(1)}, f32[144,512]{1,0:T(8,128)S(1)}, f32[128,512]{1,0:T(8,128)S(1)}) custom-call(s32[1,2]{1,0:T(1,128)S(1)} %add_bitcast_fusion.refs_0_, bf16[128,1024]{1,0:T(8,128)(2,1)S(1)} %collective-permute-done.4.refs_1_, bf16[128,1024]{1,0:T(8,128)(2,1)S(1)} %collective-permute-done.7.refs_2_, ...), custom_call_target="tpu_custom_call" | custom-call | tf_op jit(solution)/shard_map/pallas_call | solution.py:218
  41.9 2.3 %collective-permute-start.12 = (bf16[128,1024]{1,0:T(8,128)(2,1)S(1)}, bf16[128,1024]{1,0:T(8,128)(2,1)S(1)}, u32[]{:S(2)}, u32[]{:S(2)}) collective-permute-start(bf16[128,1024]{1,0:T(8,128)(2,1)S(1)} %collective-permute-done.5.refs_1_), channel_id=1, source_target_pairs={{0,1},{4,5},{1,2},{5,6},{2,3},{6,7},{3,11},{7,15},{11,10},{15,14},... | collective-permute-start | bytes 786440 | tf_op jit(solution)/shard_map/ppermute | solution.py:285
  44.2 3.4 %shard_map.90 = (bf16[144,512]{1,0:T(8,128)(2,1)S(1)}, f32[128,512]{1,0:T(8,128)S(1)}, f32[144,512]{1,0:T(8,128)S(1)}, bf16[128,512]{1,0:T(8,128)(2,1)S(1)}) custom-call(s32[1,2]{1,0:T(1,128)S(1)} %add_bitcast_fusion.refs_0_, bf16[128,1024]{1,0:T(8,128)(2,1)S(1)} %collective-permute-done.5.refs_1_, bf16[128,1024]{1,0:T(8,128)(2,1)S(1)} %collective-permute-done.13.refs_2_, ...), custom_call_target="tpu_custom_call" | custom-call | tf_op jit(solution)/shard_map/pallas_call | solution.py:218
  47.7 2.0 %collective-permute-start.17 = (bf16[128,512]{1,0:T(8,128)(2,1)S(1)}, bf16[128,512]{1,0:T(8,128)(2,1)S(1)}, u32[]{:S(2)}, u32[]{:S(2)}) collective-permute-start(bf16[128,512]{1,0:T(8,128)(2,1)S(1)} %get-tuple-element.63), channel_id=1, source_target_pairs={{0,1},{4,5},{1,2},{5,6},{2,3},{6,7},{3,11},{7,15},{11,10},{15,14},... | collective-permute-start | bytes 393224 | tf_op jit(solution)/shard_map/ppermute | solution.py:285
  49.7 2.9 %shard_map.92 = (bf16[144,512]{1,0:T(8,128)(2,1)S(1)}, bf16[128,512]{1,0:T(8,128)(2,1)S(1)}) custom-call(s32[1,2]{1,0:T(1,128)S(1)} %add_bitcast_fusion.refs_0_, bf16[128,1024]{1,0:T(8,128)(2,1)S(1)} %collective-permute-done.12.refs_1_, bf16[136,1024]{1,0:T(8,128)(2,1)S(1)} %collective-permute-done.16.refs_2_, ...), custom_call_target="tpu_custom_call" | custom-call | tf_op jit(solution)/shard_map/pallas_call | solution.py:218
  52.8 1.9 %collective-permute-start.19 = (bf16[144,512]{1,0:T(8,128)(2,1)S(1)}, bf16[144,512]{1,0:T(8,128)(2,1)S(1)}, u32[]{:S(2)}, u32[]{:S(2)}) collective-permute-start(bf16[144,512]{1,0:T(8,128)(2,1)S(1)} %get-tuple-element.64), channel_id=1, source_target_pairs={{0,1},{4,5},{1,2},{5,6},{2,3},{6,7},{3,11},{7,15},{11,10},{15,14},... | collective-permute-start | bytes 442376 | tf_op jit(solution)/shard_map/ppermute | solution.py:285
  54.8 4.8 %collective-permute-done.20.refs_2_ = bf16[128,512]{1,0:T(8,128)(2,1)S(1)} collective-permute-done((bf16[128,512]{1,0:T(8,128)(2,1)S(1)}, bf16[128,512]{1,0:T(8,128)(2,1)S(1)}, u32[]{:S(2)}, u32[]{:S(2)}) %collective-permute-start.20) | collective-permute-done | bytes 131104 | tf_op jit(solution)/shard_map/ppermute | solution.py:285
  63.9 3.6 %collective-permute-done.22.refs_2_ = bf16[128,512]{1,0:T(8,128)(2,1)S(1)} collective-permute-done((bf16[128,512]{1,0:T(8,128)(2,1)S(1)}, bf16[128,512]{1,0:T(8,128)(2,1)S(1)}, u32[]{:S(2)}, u32[]{:S(2)}) %collective-permute-start.22) | collective-permute-done | bytes 131104 | tf_op jit(solution)/shard_map/ppermute | solution.py:285
  67.6 2.3 %collective-permute-start.23 = (bf16[144,512]{1,0:T(8,128)(2,1)S(1)}, bf16[144,512]{1,0:T(8,128)(2,1)S(1)}, u32[]{:S(2)}, u32[]{:S(2)}) collective-permute-start(bf16[144,512]{1,0:T(8,128)(2,1)S(1)} %get-tuple-element.72), channel_id=1, source_target_pairs={{0,1},{4,5},{1,2},{5,6},{2,3},{6,7},{3,11},{7,15},{11,10},{15,14},... | collective-permute-start | bytes 442376 | tf_op jit(solution)/shard_map/ppermute | solution.py:285
  71.2 3.8 %collective-permute-done.24.refs_2_ = bf16[128,512]{1,0:T(8,128)(2,1)S(1)} collective-permute-done((bf16[128,512]{1,0:T(8,128)(2,1)S(1)}, bf16[128,512]{1,0:T(8,128)(2,1)S(1)}, u32[]{:S(2)}, u32[]{:S(2)}) %collective-permute-start.24) | collective-permute-done | bytes 131104 | tf_op jit(solution)/shard_map/ppermute | solution.py:285
  75.0 2.1 %collective-permute-start.25 = (bf16[144,512]{1,0:T(8,128)(2,1)S(1)}, bf16[144,512]{1,0:T(8,128)(2,1)S(1)}, u32[]{:S(2)}, u32[]{:S(2)}) collective-permute-start(bf16[144,512]{1,0:T(8,128)(2,1)S(1)} %get-tuple-element.76), channel_id=1, source_target_pairs={{0,1},{4,5},{1,2},{5,6},{2,3},{6,7},{3,11},{7,15},{11,10},{15,14},... | collective-permute-start | bytes 442376 | tf_op jit(solution)/shard_map/ppermute | solution.py:285
  79.1 2.9 %collective-permute-done.29.right_a = bf16[128,512]{1,0:T(8,128)(2,1)S(1)} collective-permute-done((bf16[128,512]{1,0:T(8,128)(2,1)S(1)}, bf16[128,512]{1,0:T(8,128)(2,1)S(1)}, u32[]{:S(2)}, u32[]{:S(2)}) %collective-permute-start.29) | collective-permute-done | bytes 131104 | tf_op jit(solution)/shard_map/ppermute | solution.py:285
  (64 shorter events, 14.9 us)
Async XLA Ops:
  1.2 5.5 %collective-permute-start.1 = (bf16[1024,512]{1,0:T(8,128)(2,1)}, bf16[1024,512]{1,0:T(8,128)(2,1)S(1)}, u32[]{:S(2)}, u32[]{:S(2)}) collective-permute-start(bf16[1024,512]{1,0:T(8,128)(2,1)} %bitcast.15), channel_id=1, source_target_pairs={{0,4},{4,0},{1,5},{5,1},{2,6},{6,2},{3,7},{7,3},{11,15},{15,11},{1... | collective-permute-start | bytes 3145736 | tf_op jit(solution)/shard_map/ppermute | solution.py:285
  1.2 19.3 %collective-permute-start.2 = (bf16[512,1024]{1,0:T(8,128)(2,1)}, bf16[512,1024]{1,0:T(8,128)(2,1)}, u32[]{:S(2)}, u32[]{:S(2)}) collective-permute-start(bf16[512,1024]{1,0:T(8,128)(2,1)} %bitcast.17), channel_id=1, source_target_pairs={{0,4},{4,0},{1,5},{5,1},{2,6},{6,2},{3,7},{7,3},{11,15},{15,11},{1... | collective-permute-start | bytes 3145736 | tf_op jit(solution)/shard_map/ppermute | solution.py:285
  2.7 10.1 %collective-permute-start.8 = (bf16[136,1024]{1,0:T(8,128)(2,1)S(1)}, bf16[136,1024]{1,0:T(8,128)(2,1)S(1)}, u32[]{:S(2)}, u32[]{:S(2)}) collective-permute-start(bf16[136,1024]{1,0:T(8,128)(2,1)S(1)} %shard_map.86.refs_2_), channel_id=1, source_target_pairs={{0,1},{4,5},{1,2},{5,6},{2,3},{6,7},{3,11},{7,15},{11,10},{15,14},... | collective-permute-start | bytes 835592 | tf_op jit(solution)/shard_map/ppermute | solution.py:285
  5.4 9.5 %collective-permute-start.10 = (bf16[136,1024]{1,0:T(8,128)(2,1)S(1)}, bf16[136,1024]{1,0:T(8,128)(2,1)S(1)}, u32[]{:S(2)}, u32[]{:S(2)}) collective-permute-start(bf16[136,1024]{1,0:T(8,128)(2,1)S(1)} %shard_map.86.refs_2_), channel_id=1, source_target_pairs={{0,8},{4,12},{1,0},{5,4},{2,1},{6,5},{3,2},{7,6},{11,3},{15,7},{10... | collective-permute-start | bytes 835592 | tf_op jit(solution)/shard_map/ppermute | solution.py:285
  6.7 11.8 %collective-permute-start.3 = (bf16[128,1024]{1,0:T(8,128)(2,1)S(1)}, bf16[128,1024]{1,0:T(8,128)(2,1)S(1)}, u32[]{:S(2)}, u32[]{:S(2)}) collective-permute-start(bf16[128,1024]{1,0:T(8,128)(2,1)S(1)} %copy-done), channel_id=1, source_target_pairs={{0,1},{4,5},{1,2},{5,6},{2,3},{6,7},{3,11},{7,15},{11,10},{15,14},... | collective-permute-start | bytes 786440 | tf_op jit(solution)/shard_map/ppermute | solution.py:285
  9.6 10.9 %collective-permute-start.6 = (bf16[128,1024]{1,0:T(8,128)(2,1)S(1)}, bf16[128,1024]{1,0:T(8,128)(2,1)S(1)}, u32[]{:S(2)}, u32[]{:S(2)}) collective-permute-start(bf16[128,1024]{1,0:T(8,128)(2,1)S(1)} %copy-done), channel_id=1, source_target_pairs={{0,8},{4,12},{1,0},{5,4},{2,1},{6,5},{3,2},{7,6},{11,3},{15,7},{10... | collective-permute-start | bytes 786440 | tf_op jit(solution)/shard_map/ppermute | solution.py:285
  12.8 14.0 %collective-permute-start.9 = (bf16[136,1024]{1,0:T(8,128)(2,1)S(1)}, bf16[136,1024]{1,0:T(8,128)(2,1)S(1)}, u32[]{:S(2)}, u32[]{:S(2)}) collective-permute-start(bf16[136,1024]{1,0:T(8,128)(2,1)S(1)} %collective-permute-done.8.refs_3_), channel_id=1, source_target_pairs={{0,1},{4,5},{1,2},{5,6},{2,3},{6,7},{3,11},{7,15},{11,10},{15,14},... | collective-permute-start | bytes 835592 | tf_op jit(solution)/shard_map/ppermute | solution.py:285
  14.9 11.9 %collective-permute-start.11 = (bf16[136,1024]{1,0:T(8,128)(2,1)S(1)}, bf16[136,1024]{1,0:T(8,128)(2,1)S(1)}, u32[]{:S(2)}, u32[]{:S(2)}) collective-permute-start(bf16[136,1024]{1,0:T(8,128)(2,1)S(1)} %collective-permute-done.10.refs_4_), channel_id=1, source_target_pairs={{0,8},{4,12},{1,0},{5,4},{2,1},{6,5},{3,2},{7,6},{11,3},{15,7},{10... | collective-permute-start | bytes 835592 | tf_op jit(solution)/shard_map/ppermute | solution.py:285
  18.4 11.6 %collective-permute-start.4 = (bf16[128,1024]{1,0:T(8,128)(2,1)S(1)}, bf16[128,1024]{1,0:T(8,128)(2,1)S(1)}, u32[]{:S(2)}, u32[]{:S(2)}) collective-permute-start(bf16[128,1024]{1,0:T(8,128)(2,1)S(1)} %collective-permute-done.3.refs_1_), channel_id=1, source_target_pairs={{0,1},{4,5},{1,2},{5,6},{2,3},{6,7},{3,11},{7,15},{11,10},{15,14},... | collective-permute-start | bytes 786440 | tf_op jit(solution)/shard_map/ppermute | solution.py:285
  20.5 11.6 %collective-permute-start.7 = (bf16[128,1024]{1,0:T(8,128)(2,1)S(1)}, bf16[128,1024]{1,0:T(8,128)(2,1)S(1)}, u32[]{:S(2)}, u32[]{:S(2)}) collective-permute-start(bf16[128,1024]{1,0:T(8,128)(2,1)S(1)} %collective-permute-done.6.refs_2_), channel_id=1, source_target_pairs={{0,8},{4,12},{1,0},{5,4},{2,1},{6,5},{3,2},{7,6},{11,3},{15,7},{10... | collective-permute-start | bytes 786440 | tf_op jit(solution)/shard_map/ppermute | solution.py:285
  26.8 9.6 %collective-permute-start.14 = (bf16[136,1024]{1,0:T(8,128)(2,1)S(1)}, bf16[136,1024]{1,0:T(8,128)(2,1)S(1)}, u32[]{:S(2)}, u32[]{:S(2)}) collective-permute-start(bf16[136,1024]{1,0:T(8,128)(2,1)S(1)} %collective-permute-done.9.refs_3_), channel_id=1, source_target_pairs={{0,1},{4,5},{1,2},{5,6},{2,3},{6,7},{3,11},{7,15},{11,10},{15,14},... | collective-permute-start | bytes 835592 | tf_op jit(solution)/shard_map/ppermute | solution.py:285
  28.9 9.6 %collective-permute-start.15 = (bf16[136,1024]{1,0:T(8,128)(2,1)S(1)}, bf16[136,1024]{1,0:T(8,128)(2,1)S(1)}, u32[]{:S(2)}, u32[]{:S(2)}) collective-permute-start(bf16[136,1024]{1,0:T(8,128)(2,1)S(1)} %collective-permute-done.11.refs_4_), channel_id=1, source_target_pairs={{0,8},{4,12},{1,0},{5,4},{2,1},{6,5},{3,2},{7,6},{11,3},{15,7},{10... | collective-permute-start | bytes 835592 | tf_op jit(solution)/shard_map/ppermute | solution.py:285
  30.0 11.9 %collective-permute-start.5 = (bf16[128,1024]{1,0:T(8,128)(2,1)S(1)}, bf16[128,1024]{1,0:T(8,128)(2,1)S(1)}, u32[]{:S(2)}, u32[]{:S(2)}) collective-permute-start(bf16[128,1024]{1,0:T(8,128)(2,1)S(1)} %collective-permute-done.4.refs_1_), channel_id=1, source_target_pairs={{0,1},{4,5},{1,2},{5,6},{2,3},{6,7},{3,11},{7,15},{11,10},{15,14},... | collective-permute-start | bytes 786440 | tf_op jit(solution)/shard_map/ppermute | solution.py:285
  32.1 12.1 %collective-permute-start.13 = (bf16[128,1024]{1,0:T(8,128)(2,1)S(1)}, bf16[128,1024]{1,0:T(8,128)(2,1)S(1)}, u32[]{:S(2)}, u32[]{:S(2)}) collective-permute-start(bf16[128,1024]{1,0:T(8,128)(2,1)S(1)} %collective-permute-done.7.refs_2_), channel_id=1, source_target_pairs={{0,8},{4,12},{1,0},{5,4},{2,1},{6,5},{3,2},{7,6},{11,3},{15,7},{10... | collective-permute-start | bytes 786440 | tf_op jit(solution)/shard_map/ppermute | solution.py:285
  38.5 11.2 %collective-permute-start.16 = (bf16[136,1024]{1,0:T(8,128)(2,1)S(1)}, bf16[136,1024]{1,0:T(8,128)(2,1)S(1)}, u32[]{:S(2)}, u32[]{:S(2)}) collective-permute-start(bf16[136,1024]{1,0:T(8,128)(2,1)S(1)} %collective-permute-done.15.refs_4_), channel_id=1, source_target_pairs={{0,8},{4,12},{1,0},{5,4},{2,1},{6,5},{3,2},{7,6},{11,3},{15,7},{10... | collective-permute-start | bytes 835592 | tf_op jit(solution)/shard_map/ppermute | solution.py:285
  41.9 7.7 %collective-permute-start.12 = (bf16[128,1024]{1,0:T(8,128)(2,1)S(1)}, bf16[128,1024]{1,0:T(8,128)(2,1)S(1)}, u32[]{:S(2)}, u32[]{:S(2)}) collective-permute-start(bf16[128,1024]{1,0:T(8,128)(2,1)S(1)} %collective-permute-done.5.refs_1_), channel_id=1, source_target_pairs={{0,1},{4,5},{1,2},{5,6},{2,3},{6,7},{3,11},{7,15},{11,10},{15,14},... | collective-permute-start | bytes 786440 | tf_op jit(solution)/shard_map/ppermute | solution.py:285
  52.8 6.8 %collective-permute-start.19 = (bf16[144,512]{1,0:T(8,128)(2,1)S(1)}, bf16[144,512]{1,0:T(8,128)(2,1)S(1)}, u32[]{:S(2)}, u32[]{:S(2)}) collective-permute-start(bf16[144,512]{1,0:T(8,128)(2,1)S(1)} %get-tuple-element.64), channel_id=1, source_target_pairs={{0,1},{4,5},{1,2},{5,6},{2,3},{6,7},{3,11},{7,15},{11,10},{15,14},... | collective-permute-start | bytes 442376 | tf_op jit(solution)/shard_map/ppermute | solution.py:285
  59.7 7.9 %collective-permute-start.21 = (bf16[144,512]{1,0:T(8,128)(2,1)S(1)}, bf16[144,512]{1,0:T(8,128)(2,1)S(1)}, u32[]{:S(2)}, u32[]{:S(2)}) collective-permute-start(bf16[144,512]{1,0:T(8,128)(2,1)S(1)} %get-tuple-element.68), channel_id=1, source_target_pairs={{0,1},{4,5},{1,2},{5,6},{2,3},{6,7},{3,11},{7,15},{11,10},{15,14},... | collective-permute-start | bytes 442376 | tf_op jit(solution)/shard_map/ppermute | solution.py:285
  61.3 6.2 %collective-permute-start.22 = (bf16[128,512]{1,0:T(8,128)(2,1)S(1)}, bf16[128,512]{1,0:T(8,128)(2,1)S(1)}, u32[]{:S(2)}, u32[]{:S(2)}) collective-permute-start(bf16[128,512]{1,0:T(8,128)(2,1)S(1)} %get-tuple-element.70), channel_id=1, source_target_pairs={{0,8},{4,12},{1,0},{5,4},{2,1},{6,5},{3,2},{7,6},{11,3},{15,7},{10... | collective-permute-start | bytes 393224 | tf_op jit(solution)/shard_map/ppermute | solution.py:285
  61.8 8.1 %collective-permute-start.26 = (bf16[128,512]{1,0:T(8,128)(2,1)S(1)}, bf16[128,512]{1,0:T(8,128)(2,1)S(1)}, u32[]{:S(2)}, u32[]{:S(2)}) collective-permute-start(bf16[128,512]{1,0:T(8,128)(2,1)S(1)} %get-tuple-element.78), channel_id=1, source_target_pairs={{0,1},{4,5},{1,2},{5,6},{2,3},{6,7},{3,11},{7,15},{11,10},{15,14},... | collective-permute-start | bytes 393224 | tf_op jit(solution)/shard_map/ppermute | solution.py:285
  63.5 7.3 %collective-permute-start.27 = (bf16[144,512]{1,0:T(8,128)(2,1)S(1)}, bf16[144,512]{1,0:T(8,128)(2,1)S(1)}, u32[]{:S(2)}, u32[]{:S(2)}) collective-permute-start(bf16[144,512]{1,0:T(8,128)(2,1)S(1)} %get-tuple-element.80), channel_id=1, source_target_pairs={{0,8},{4,12},{1,0},{5,4},{2,1},{6,5},{3,2},{7,6},{11,3},{15,7},{10... | collective-permute-start | bytes 442376 | tf_op jit(solution)/shard_map/ppermute | solution.py:285
  67.6 7.3 %collective-permute-start.23 = (bf16[144,512]{1,0:T(8,128)(2,1)S(1)}, bf16[144,512]{1,0:T(8,128)(2,1)S(1)}, u32[]{:S(2)}, u32[]{:S(2)}) collective-permute-start(bf16[144,512]{1,0:T(8,128)(2,1)S(1)} %get-tuple-element.72), channel_id=1, source_target_pairs={{0,1},{4,5},{1,2},{5,6},{2,3},{6,7},{3,11},{7,15},{11,10},{15,14},... | collective-permute-start | bytes 442376 | tf_op jit(solution)/shard_map/ppermute | solution.py:285
  70.8 11.3 %collective-permute-start.28 = (bf16[144,512]{1,0:T(8,128)(2,1)S(1)}, bf16[144,512]{1,0:T(8,128)(2,1)S(1)}, u32[]{:S(2)}, u32[]{:S(2)}) collective-permute-start(bf16[144,512]{1,0:T(8,128)(2,1)S(1)} %get-tuple-element.81), channel_id=1, source_target_pairs={{0,8},{4,12},{1,0},{5,4},{2,1},{6,5},{3,2},{7,6},{11,3},{15,7},{10... | collective-permute-start | bytes 442376 | tf_op jit(solution)/shard_map/ppermute | solution.py:285
  75.0 7.5 %collective-permute-start.25 = (bf16[144,512]{1,0:T(8,128)(2,1)S(1)}, bf16[144,512]{1,0:T(8,128)(2,1)S(1)}, u32[]{:S(2)}, u32[]{:S(2)}) collective-permute-start(bf16[144,512]{1,0:T(8,128)(2,1)S(1)} %get-tuple-element.76), channel_id=1, source_target_pairs={{0,1},{4,5},{1,2},{5,6},{2,3},{6,7},{3,11},{7,15},{11,10},{15,14},... | collective-permute-start | bytes 442376 | tf_op jit(solution)/shard_map/ppermute | solution.py:285
  (13 other events, 56.8 us)
